TPU v7x, 32 devices: a whole 2x2x4 slice. The times are simulated.
32 devices in a mesh: rep: 2 (over y), tract: 4 (over x, core), head: 4 (over z).
Axes of the slice: x: 2, y: 2, z: 4, core: 2. Of those that a mesh axis runs over, the one named last changes fastest.
Arguments:
- frames: bfloat16 [8, 256, 6144], P(('rep', 'tract'), 'head'), parts along dimension 0, may hold values from -7 to 7
- levels: int32 [8], P(('rep', 'tract')), parts along dimension 0, may hold values from 0 to 7
- visible: int32 [8, 4], P(('rep', 'tract')), parts along dimension 0, may hold values from 0 to 1, as said below
- w_qkv: bfloat16 [6144, 3, 1024], P(None, None, 'head'), may hold values from -0.2 to 0.2
- w_out: bfloat16 [1024, 6144], P('head'), may hold values from -1.5 to 1.5
- modulation: float32 [8, 3, 6144], replicated, may hold values from -3 to 3
Outputs:
- mixed: bfloat16 [8, 256, 6144], P(('rep', 'tract'), 'head'), parts along dimension 0
There are 2 independent parts, one for each index of `rep`. A program takes and returns all parts, laid end to end along the dimension named above; an argument that names none is the same for every part. Nothing has to cross between parts.
Inputs may be any that keep to these rules, and one draw needn't show every extreme that they name: visible[c, c] is 1 and visible[c, j] is 0 for every j > c.
All inputs are finite; a program needn't handle non-finite values.
Results may differ from a plain program's by a relative error of at most 0.019.
Values may be sent and summed in bfloat16 or wider, within the bound.
No kernel may reach another device: no remote copies, remote signals or barrier semaphores. Data moves between devices by JAX's collectives and lax.ppermute only.
A program may use at most 64 MiB of HBM per device.

v0:
```python
import jax
import jax.numpy as jnp
from jax import lax
from jax.sharding import PartitionSpec as P

HD = 128


def from_behind(value, axis, by):
    count = lax.axis_size(axis)
    pairs = [(i, i + by) for i in range(count) if 0 <= i + by < count]
    return lax.ppermute(value, axis, pairs)


def body(frames, levels, visible, w_qkv, w_out, modulation):
    col_width = w_qkv.shape[2]
    heads_here = col_width // HD
    n_levels = modulation.shape[0]
    chosen = (lax.iota(jnp.int32, n_levels) == levels[0]).astype(jnp.float32)
    styles = jnp.tensordot(chosen, modulation, axes=1, precision=lax.Precision.HIGHEST)
    floats = lax.all_gather(frames, "head", axis=1, tiled=True).astype(jnp.float32)
    normed = floats * lax.rsqrt(jnp.mean(floats * floats, axis=-1, keepdims=True) + 1e-06)
    shaped = (normed * (1.0 + styles[1]) + styles[0]).astype(jnp.bfloat16)
    qkv = jnp.einsum("crd,dke->crke", shaped, w_qkv, preferred_element_type=jnp.float32).astype(
        jnp.bfloat16
    )
    total_rows = qkv.shape[1]
    queries = qkv[0, :, 0].reshape(total_rows, heads_here, HD)
    kv_block = qkv[:, :, 1:]
    visible_row = visible[0]
    score_scale = HD ** (-0.5)

    def absorb(state, incoming, offset):
        row_peak, denominator, running = state
        blocks = incoming.shape[0]
        allowed = (lax.dynamic_slice_in_dim(visible_row, offset, blocks) > 0) & (offset >= 0)
        key_rows = incoming[:, :, 0].reshape(blocks, total_rows, heads_here, HD)
        values = incoming[:, :, 1].reshape(blocks, total_rows, heads_here, HD)
        scores = (
            jnp.einsum("qhd,nkhd->qhnk", queries, key_rows, preferred_element_type=jnp.float32)
            * score_scale
        )
        allowed = allowed[None, None, :, None]
        scores = jnp.where(allowed, scores, -1e30)
        new_peak = jnp.maximum(row_peak, jnp.max(scores, axis=(2, 3)))
        probs = jnp.where(allowed, jnp.exp(scores - new_peak[:, :, None, None]), 0.0)
        rescale = jnp.exp(row_peak - new_peak)
        denominator = denominator * rescale + jnp.sum(probs, axis=(2, 3))
        weighted = jnp.einsum(
            "qhnk,nkhd->qhd", probs.astype(jnp.bfloat16), values, preferred_element_type=jnp.float32
        )
        running = running * rescale[:, :, None] + weighted
        return (new_peak, denominator, running)

    initial = (
        jnp.full((total_rows, heads_here), -1e30, jnp.float32),
        jnp.zeros((total_rows, heads_here), jnp.float32),
        jnp.zeros((total_rows, heads_here, HD), jnp.float32),
    )
    own_index = lax.axis_index("tract")
    state = absorb(initial, kv_block, own_index)
    for distance in range(1, lax.axis_size("tract")):
        moved = from_behind(kv_block, "tract", distance)
        state = absorb(state, moved, own_index - distance)
    row_peak, denominator, running = state
    attended = (
        (running / denominator[:, :, None]).astype(jnp.bfloat16).reshape(total_rows, col_width)
    )
    summed = lax.psum_scatter(
        jnp.dot(attended, w_out, preferred_element_type=jnp.float32).astype(jnp.bfloat16),
        "head",
        scatter_dimension=0,
        tiled=True,
    ).astype(jnp.float32)
    mixed = (summed * styles[2]).astype(jnp.bfloat16)
    return mixed[None]


def solution(mesh):
    placed = (
        P(("rep", "tract"), "head", None),
        P(("rep", "tract")),
        P(("rep", "tract"), None),
        P(None, None, "head"),
        P("head", None),
        P(),
    )
    return jax.shard_map(
        body,
        mesh=mesh,
        in_specs=placed,
        out_specs=P(("rep", "tract"), "head", None),
        check_vma=False,
    )
```

profile of v0, /device:TPU:3, one launch (start us, length us, event | category | flops | bytes accessed | tf_op | source)
XLA Modules:
  0.0 173.5 jit_solution(12812611216690335462)
XLA Ops:
  6.5 0.7 all-gather.2.cloned.1.call-update
  8.1 1.5 constant_dynamic-slice_fusion.2
  12.1 1.5 fusion.62
  13.7 60.0 %all-gather.2.cloned.1.call-done = bf16[1,256,6144]{2,1,0:T(8,128)(2,1)} async-done(((bf16[1,64,6144]{2,1,0:T(8,128)(2,1)}), bf16[1,256,6144]{2,1,0:T(8,128)(2,1)}) %all-gather.2.cloned.1.call-update) | async-done | bytes 3145744 | tf_op jit(solution)/shard_map/all_gather | solution.py:21
  73.7 2.7 %fusion = f32[256]{0:T(256)S(1)} fusion(bf16[1,256,6144]{2,1,0:T(8,128)(2,1)} %all-gather.2.cloned.1.call-done), kind=kLoop, calls=%fused_computation.3 | loop fusion | flops 4718336 | bytes 3146752 | tf_op jit(solution)/shard_map/reduce_sum | solution.py:22
  76.4 0.1 copy-done.1
  76.5 7.8 %fusion.21 = bf16[1,256,3,256]{1,3,2,0:T(8,128)(2,1)S(1)} fusion(bf16[6144,3,256]{2,0,1:T(8,128)(2,1)} %param.9, bf16[1,256,6144]{2,1,0:T(8,128)(2,1)S(1)} %copy-done.1, f32[6144]{0:T(1024)S(1)} %bitcast.130, f32[6144]{0:T(1024)S(1)} %bitcast.131, f32[256]{0:T(256)S(1)} %add_rsqrt_fusion), kind=kOutput, calls=%fused_computation.26 | convolution fusion | flops 2423980032 | bytes 13026304 | tf_op jit(solution)/shard_map/crd,dke->crke/dot_general | solution.py:24
  84.3 1.3 collective-permute-start.2
  85.6 1.3 collective-permute-start.1
  86.9 1.3 collective-permute-start
  88.3 0.3 fusion.82
  88.6 7.3 %collective-permute-done.1 = bf16[1,256,2,256]{1,3,2,0:T(8,128)(2,1)S(1)} collective-permute-done((bf16[1,256,2,256]{1,3,2,0:T(8,128)(2,1)S(1)}, bf16[1,256,2,256]{1,3,2,0:T(8,128)(2,1)S(1)}, u32[]{:S(2)}, u32[]{:S(2)}) %collective-permute-start.1) | collective-permute-done | bytes 262176 | tf_op jit(solution)/shard_map/ppermute | solution.py:12
  95.9 0.3 fusion.81
  96.2 0.3 fusion.80
  96.5 0.3 fusion.79
  96.8 0.2 fusion.34
  97.0 0.2 fusion.38
  97.2 0.2 fusion.31
  97.5 0.2 fusion.29
  97.7 0.2 fusion.27
  98.0 0.2 fusion.32
  98.2 2.7 %convolution_convert_fusion = bf16[256,6144]{1,0:T(8,128)(2,1)} fusion(bf16[256,256]{0,1:T(8,128)(2,1)S(1)} %bitcast.127, bf16[256,6144]{1,0:T(8,128)(2,1)S(1)} %copy-done), kind=kOutput, calls=%fused_computation.2 | convolution fusion | flops 806879232 | bytes 6422528 | tf_op jit(solution)/shard_map/dot_general | solution.py:70
  100.9 63.6 %reduce-scatter.2.cloned.1.call-done = bf16[64,6144]{1,0:T(8,128)(2,1)} async-done(((bf16[256,6144]{1,0:T(8,128)(2,1)}), bf16[64,6144]{1,0:T(8,128)(2,1)}) %reduce-scatter.2.cloned.1.call-update) | async-done | bytes 786448 | tf_op jit(solution)/shard_map/reduce_scatter | solution.py:69
  164.6 2.2 %fusion.33 = bf16[1,64,6144]{2,1,0:T(8,128)(2,1)} fusion(bf16[64,6144]{1,0:T(8,128)(2,1)} %reduce-scatter.2.cloned.1.call-done, f32[6144]{0:T(1024)S(1)} %bitcast.129), kind=kLoop, calls=%fused_computation.40 | loop fusion | flops 1179648 | bytes 1597440 | tf_op jit(solution)/shard_map/broadcast_in_dim | solution.py:76
  (18 shorter events, 0.3 us)
Async XLA Ops:
  6.5 91.7 %copy-start = (bf16[256,6144]{1,0:T(8,128)(2,1)S(1)}, bf16[256,6144]{1,0:T(8,128)(2,1)}, u32[]{:S(2)}) copy-start(bf16[256,6144]{1,0:T(8,128)(2,1)} %param.10) | copy-start | bytes 9437188
  6.5 67.1 %all-gather.2.cloned.1.call-start = ((), (), s32[]{:S(2)}) async-start(), calls=%async_computation.1 | async-start | bytes 3932160 | tf_op jit(solution)/shard_map/all_gather | solution.py:21
  7.3 157.3 %reduce-scatter.2.cloned.1.call-start = ((), (), s32[]{:S(2)}) async-start(), calls=%async_computation.2 | async-start | bytes 3932160 | tf_op jit(solution)/shard_map/reduce_scatter | solution.py:69
  73.7 2.8 %copy-start.1 = (bf16[1,256,6144]{2,1,0:T(8,128)(2,1)S(1)}, bf16[1,256,6144]{2,1,0:T(8,128)(2,1)}, u32[]{:S(2)}) copy-start(bf16[1,256,6144]{2,1,0:T(8,128)(2,1)} %all-gather.2.cloned.1.call-done) | copy-start | bytes 9437188
  84.3 12.1 %collective-permute-start.2 = (bf16[1,256,2,256]{1,3,2,0:T(8,128)(2,1)S(1)}, bf16[1,256,2,256]{1,3,2,0:T(8,128)(2,1)S(1)}, u32[]{:S(2)}, u32[]{:S(2)}) collective-permute-start(bf16[1,256,2,256]{1,3,2,0:T(8,128)(2,1)S(1)} %slice.59), channel_id=1, source_target_pairs={{0,12},{1,13},{2,14},{3,15},{16,28},{17,29},{18,30},{19,31}} | collective-permute-start | bytes 786440 | tf_op jit(solution)/shard_map/ppermute | solution.py:12
  85.6 10.2 %collective-permute-start.1 = (bf16[1,256,2,256]{1,3,2,0:T(8,128)(2,1)S(1)}, bf16[1,256,2,256]{1,3,2,0:T(8,128)(2,1)S(1)}, u32[]{:S(2)}, u32[]{:S(2)}) collective-permute-start(bf16[1,256,2,256]{1,3,2,0:T(8,128)(2,1)S(1)} %slice.59), channel_id=1, source_target_pairs={{0,8},{4,12},{1,9},{5,13},{2,10},{6,14},{3,11},{7,15},{16,24},{20,... | collective-permute-start | bytes 786440 | tf_op jit(solution)/shard_map/ppermute | solution.py:12
  86.9 8.9 %collective-permute-start = (bf16[1,256,2,256]{1,3,2,0:T(8,128)(2,1)S(1)}, bf16[1,256,2,256]{1,3,2,0:T(8,128)(2,1)S(1)}, u32[]{:S(2)}, u32[]{:S(2)}) collective-permute-start(bf16[1,256,2,256]{1,3,2,0:T(8,128)(2,1)S(1)} %slice.59), channel_id=1, source_target_pairs={{0,4},{4,8},{8,12},{1,5},{5,9},{9,13},{2,6},{6,10},{10,14},{3,7},{... | collective-permute-start | bytes 786440 | tf_op jit(solution)/shard_map/ppermute | solution.py:12
Sparse Core Ops, SparseCore 0:
  8.9 64.6 all-gather.1
  101.0 63.4 reduce-scatter.1
where the time goes:
time: 176 us; the launch traced here: 174 us
  waiting for transfers between devices  132 us (75%)
  between operations  16.9 us (10%)
  matrix products  14 us (8%)
  other arithmetic  5.39 us (3%)
  starting transfers between devices  3.92 us (2%)
    reduce_scatter x1, waiting for transfers between devices, body(): lax.psum_scatter(jnp.dot(attended, w_out, preferred_element_type=jnp.floa...  63.6 us
    all_gather x1, waiting for transfers between devices, body(): lax.all_gather(frames, 'head', axis=1, tiled=True).astype(jnp.float32)  60 us
    dot_general x1, matrix products, body(): jnp.einsum('crd,dke->crke', shaped, w_qkv, preferred_element_type=jnp.flo...  7.82 us
    ppermute x3, waiting for transfers between devices, from_behind(): return lax.ppermute(value, axis, pairs)  7.28 us
    ppermute x3, starting transfers between devices, from_behind(): return lax.ppermute(value, axis, pairs)  3.88 us
  transfers between devices with their start and end apart: 5, of which 3 were waited for; matrix products, arithmetic and copies ran while one was open for 2% of the time, Pallas kernels for 0%

commit v1 on v0

--- a/solution.py
+++ b/solution.py
@@ -1,9 +1,14 @@
+import functools
+
 import jax
 import jax.numpy as jnp
 from jax import lax
+from jax.experimental import pallas as pl
+from jax.experimental.pallas import tpu as pltpu
 from jax.sharding import PartitionSpec as P
 
 HD = 128
+PLANE = ("rep", "tract")
 
 
 def from_behind(value, axis, by):
@@ -12,12 +17,262 @@
     return lax.ppermute(value, axis, pairs)
 
 
-def body(frames, levels, visible, w_qkv, w_out, modulation):
+def pick_styles(levels, modulation):
+    n_levels = modulation.shape[0]
+    chosen = (lax.iota(jnp.int32, n_levels) == levels[0]).astype(jnp.float32)
+    return jnp.tensordot(chosen, modulation, axes=1, precision=lax.Precision.HIGHEST)
+
+
+def attention_kernel(heads_here, q_ref, *refs):
+    kv_refs, seen_ref, out_ref = refs[:-2], refs[-2], refs[-1]
+    cols = heads_here * HD
+    score_scale = HD ** (-0.5)
+    for h in range(heads_here):
+        q = q_ref[:, h * HD : (h + 1) * HD]
+        scores = []
+        for d, kv in enumerate(kv_refs):
+            raw = lax.dot_general(
+                q,
+                kv[:, h * HD : (h + 1) * HD],
+                (((1,), (1,)), ((), ())),
+                preferred_element_type=jnp.float32,
+            )
+            scores.append(jnp.where(seen_ref[d // 2] > 0, raw * score_scale, -1e30))
+        peak = jnp.max(scores[0], axis=1, keepdims=True)
+        for part in scores[1:]:
+            peak = jnp.maximum(peak, jnp.max(part, axis=1, keepdims=True))
+        denominator = jnp.zeros_like(peak)
+        total = jnp.zeros((q.shape[0], HD), jnp.float32)
+        for part, kv in zip(scores, kv_refs):
+            probs = jnp.exp(part - peak)
+            denominator += jnp.sum(probs, axis=1, keepdims=True)
+            total += jnp.dot(
+                probs.astype(jnp.bfloat16),
+                kv[:, cols + h * HD : cols + (h + 1) * HD],
+                preferred_element_type=jnp.float32,
+            )
+        out_ref[:, h * HD : (h + 1) * HD] = (total / denominator).astype(jnp.bfloat16)
+
+
+def attend(queries, kv, seen):
+    rows, cols = queries.shape
+    vmem = pl.BlockSpec(memory_space=pltpu.VMEM)
+    return pl.pallas_call(
+        functools.partial(attention_kernel, cols // HD),
+        out_shape=jax.ShapeDtypeStruct((rows, cols), jnp.bfloat16),
+        in_specs=[vmem] * (1 + len(kv)) + [pl.BlockSpec(memory_space=pltpu.SMEM)],
+        out_specs=vmem,
+        compiler_params=pltpu.CompilerParams(vmem_limit_bytes=32 << 20),
+        cost_estimate=pl.CostEstimate(
+            flops=2 * rows * rows * len(kv) * cols,
+            bytes_accessed=2 * rows * cols * (2 + len(kv)),
+            transcendentals=rows * rows * len(kv) * cols // (2 * HD),
+        ),
+        name="attend",
+    )(queries, *kv, seen)
+
+
+def qkv_kernel(groups, outer_ref, *refs):
+    count = sum(groups)
+    tokens, w_ref, out_ref, rows_ref, acc_ref = refs[:count], *refs[count:]
+    rows = tokens[0].shape[0]
+    cols = w_ref.shape[2]
+    step = pl.program_id(0)
+    at = 0
+    for i, size in enumerate(groups):
+        block = tokens[at][...]
+        if size == 2:
+            block = jnp.where(outer_ref[0] > 0, block, tokens[at + 1][...])
+        rows_ref[i * rows : (i + 1) * rows] = block
+        at += size
+
+    @pl.when(step == 0)
+    def _():
+        acc_ref[...] = jnp.zeros_like(acc_ref)
+
+    for j in range(3):
+        acc_ref[:, j * cols : (j + 1) * cols] += jnp.dot(
+            rows_ref[...], w_ref[j], preferred_element_type=jnp.float32
+        )
+
+    @pl.when(step == pl.num_programs(0) - 1)
+    def _():
+        out_ref[...] = acc_ref[...].astype(out_ref.dtype)
+
+
+def project_qkv(outer, groups, weights, chunk):
+    tokens = [block for group in groups for block in group]
+    rows, width = tokens[0].shape
+    cols = weights.shape[2]
+    total = rows * len(groups)
+    return pl.pallas_call(
+        functools.partial(qkv_kernel, [len(group) for group in groups]),
+        grid=(width // chunk,),
+        out_shape=jax.ShapeDtypeStruct((total, 3 * cols), jnp.bfloat16),
+        in_specs=[pl.BlockSpec(memory_space=pltpu.SMEM)]
+        + [pl.BlockSpec((rows, chunk), lambda k: (0, k))] * len(tokens)
+        + [pl.BlockSpec((3, chunk, cols), lambda k: (0, k, 0))],
+        out_specs=pl.BlockSpec((total, 3 * cols), lambda k: (0, 0)),
+        scratch_shapes=[
+            pltpu.VMEM((total, chunk), jnp.bfloat16),
+            pltpu.VMEM((total, 3 * cols), jnp.float32),
+        ],
+        compiler_params=pltpu.CompilerParams(
+            dimension_semantics=("arbitrary",), vmem_limit_bytes=32 << 20
+        ),
+        cost_estimate=pl.CostEstimate(
+            flops=6 * total * width * cols,
+            bytes_accessed=6 * width * cols + 2 * total * width,
+            transcendentals=0,
+        ),
+        name="project_qkv",
+    )(outer, *tokens, weights)
+
+
+def output_kernel(place_ref, att_ref, gate_ref, own_ref, *refs):
+    pieces, out_ref = refs[:-1], refs[-1]
+    count = len(pieces) // 3
+    span = out_ref.shape[1] // count
+    width = own_ref.shape[0]
+    rows = out_ref.shape[0] // 2
+    core, chip = place_ref[0] % 2, place_ref[0] // 2
+    for delta in range(count):
+        chunk = chip ^ delta
+        start = pl.multiple_of((core * count + chunk) * span, 128)
+        there = pl.ds(start, span)
+        total = jnp.dot(att_ref[:, :width], own_ref[:, there], preferred_element_type=jnp.float32)
+        for s in range(3):
+            total += jnp.dot(
+                att_ref[:, (s + 1) * width : (s + 2) * width],
+                pieces[count * s + delta][...],
+                preferred_element_type=jnp.float32,
+            )
+        target = pl.ds(pl.multiple_of(chunk * span, 128), span)
+        for half in range(2):
+            part = total[half * rows : (half + 1) * rows] * gate_ref[half : half + 1, there]
+            out_ref[half * rows : (half + 1) * rows, target] = part.astype(jnp.bfloat16)
+
+
+def project_out(place, att, gate, own, pieces):
+    rows, width = att.shape[0], own.shape[1] // 2
+    vmem = pl.BlockSpec(memory_space=pltpu.VMEM)
+    return pl.pallas_call(
+        output_kernel,
+        out_shape=jax.ShapeDtypeStruct((rows, width), jnp.bfloat16),
+        in_specs=[pl.BlockSpec(memory_space=pltpu.SMEM)] + [vmem] * (3 + len(pieces)),
+        out_specs=vmem,
+        compiler_params=pltpu.CompilerParams(vmem_limit_bytes=40 << 20),
+        cost_estimate=pl.CostEstimate(
+            flops=2 * rows * att.shape[1] * width,
+            bytes_accessed=2 * att.shape[1] * width,
+            transcendentals=0,
+        ),
+        name="project_out",
+    )(place, att, gate, own, *pieces)
+
+
+def after(value, *earlier):
+    return lax.optimization_barrier((value, *earlier))[0]
+
+
+def gather_body(frames, levels, visible, w_qkv, w_out, modulation):
+    here = lax.axis_index("head")
+    n_tract = lax.axis_size("tract")
+    tract = lax.axis_index("tract")
+    plane = lax.axis_size("rep") * n_tract
+    place = lax.axis_index("rep") * n_tract + tract
+    core = lax.rem(place, 2)
+    rows, width = frames.shape[1], frames.shape[2]
+    cols = w_qkv.shape[2]
+    span = width // plane
+    outer = (here == 0) | (here == 3)
+    outer_flag = outer.astype(jnp.int32)[None]
+    w3 = jnp.moveaxis(w_qkv, 1, 0)
+
+    def pair(value):
+        return lax.ppermute(value, "head", [(0, 1), (1, 0), (2, 3), (3, 2)])
+
+    def middle(value):
+        return lax.ppermute(value, "head", [(1, 2), (2, 1)])
+
+    def outward(value):
+        return lax.ppermute(value, "head", [(1, 0), (2, 3)])
+
+    def swap(value):
+        return lax.ppermute(value, PLANE, [(i, i ^ 1) for i in range(plane)])
+
+    def across_plane(piece):
+        return [piece] + [
+            lax.ppermute(piece, PLANE, [(i, i ^ delta) for i in range(plane)])
+            for delta in range(2, plane, 2)
+        ]
+
+    chunk = core * (plane // 2) + place // 2
+    piece = lax.dynamic_slice_in_dim(w_out, chunk * span, span, 1)
+    w_first = pair(piece)
+    w_mid = middle(piece)
+
+    styles = lax.dynamic_index_in_dim(modulation, levels[0], 0, keepdims=False)
+    floats = frames[0].astype(jnp.float32)
+    normed = floats * lax.rsqrt(jnp.mean(floats * floats, axis=-1, keepdims=True) + 1e-06)
+    own = (normed * (1.0 + styles[1]) + styles[0]).astype(jnp.bfloat16)
+
+    ready = after(own, w_first, w_mid)
+    first = pair(ready)
+    mid = middle(ready)
+    w_far_mid = middle(w_first)
+    w_out_mid = outward(w_mid)
+    w_far_out = outward(w_far_mid)
+    w_first_pieces = across_plane(w_first)
+    w_second = jnp.where(outer, w_out_mid, w_mid)
+    w_second_pieces = across_plane(w_second)
+    w_third = jnp.where(outer, w_far_out, w_far_mid)
+    w_third_pieces = across_plane(w_third)
+    far_mid = middle(after(first, w_out_mid, *w_first_pieces))
+    out = outward(mid)
+    far_out = outward(after(far_mid, *w_second_pieces))
+    pieces = w_first_pieces + w_second_pieces + w_third_pieces
+    gates = jnp.stack([styles[2], swap(styles[2])])
+
+    def exchange(value):
+        return [value] + [from_behind(value, "tract", d) for d in range(1, n_tract)]
+
+    early = project_qkv(outer_flag, [[own], [first], [out, mid]], w3, 768)
+    early_kv = exchange(early[:, cols:])
+    late = project_qkv(outer_flag, [[after(far_out, *w_third_pieces), far_mid]], w3, 768)
+    late_kv = exchange(late[:, cols:])
+    kv = [block for both in zip(early_kv, late_kv) for block in both]
+    offsets = tract - lax.iota(jnp.int32, n_tract)
+    seen = jnp.sum(
+        jnp.where(offsets[:, None] == lax.iota(jnp.int32, n_tract)[None, :], visible, 0), axis=1
+    )
+    queries = jnp.concatenate([early[:, :cols], late[:, :cols]], axis=0)
+    attended = attend(queries, kv, seen)
+
+    blocks = [attended[i * rows : (i + 1) * rows] for i in range(4)]
+    leaving = [blocks[1], jnp.where(outer, blocks[2], blocks[3]), jnp.where(outer, blocks[3], blocks[2])]
+    came = [
+        lax.ppermute(value, "head", [(i, i ^ (s + 1)) for i in range(4)])
+        for s, value in enumerate(leaving)
+    ]
+    att = jnp.concatenate(
+        [blocks[0], came[0], jnp.where(outer, came[1], came[2]), jnp.where(outer, came[2], came[1])],
+        axis=1,
+    )
+    both = project_out(place[None], jnp.concatenate([att, swap(att)], axis=0), gates, w_out, pieces)
+    mine, theirs = both[:rows], swap(both[rows:])
+    mixed = jnp.where(
+        core == 0,
+        jnp.concatenate([mine, theirs], axis=1),
+        jnp.concatenate([theirs, mine], axis=1),
+    )
+    return mixed[None]
+
+
+def scatter_body(frames, levels, visible, w_qkv, w_out, modulation):
     col_width = w_qkv.shape[2]
     heads_here = col_width // HD
-    n_levels = modulation.shape[0]
-    chosen = (lax.iota(jnp.int32, n_levels) == levels[0]).astype(jnp.float32)
-    styles = jnp.tensordot(chosen, modulation, axes=1, precision=lax.Precision.HIGHEST)
+    styles = pick_styles(levels, modulation)
     floats = lax.all_gather(frames, "head", axis=1, tiled=True).astype(jnp.float32)
     normed = floats * lax.rsqrt(jnp.mean(floats * floats, axis=-1, keepdims=True) + 1e-06)
     shaped = (normed * (1.0 + styles[1]) + styles[0]).astype(jnp.bfloat16)
@@ -85,10 +340,20 @@
         P("head", None),
         P(),
     )
-    return jax.shard_map(
-        body,
-        mesh=mesh,
-        in_specs=placed,
-        out_specs=P(("rep", "tract"), "head", None),
-        check_vma=False,
-    )
+
+    def run(frames, levels, visible, w_qkv, w_out, modulation):
+        n_head, n_tract, n_rep = mesh.shape["head"], mesh.shape["tract"], mesh.shape["rep"]
+        tokens_here = frames.shape[1] // n_head
+        weight_rows_here = w_out.shape[0] // n_head
+        plane = n_tract * n_rep
+        fits = (n_head, n_tract, n_rep) == (4, 4, 2) and frames.shape[2] % (2 * plane * 128) == 0
+        gather = fits and weight_rows_here < tokens_here * plane
+        return jax.shard_map(
+            gather_body if gather else scatter_body,
+            mesh=mesh,
+            in_specs=placed,
+            out_specs=P(("rep", "tract"), "head", None),
+            check_vma=False,
+        )(frames, levels, visible, w_qkv, w_out, modulation)
+
+    return run

time: 176 us -> 139 us (0.79)
  waiting for transfers between devices: 132 us -> 67.9 us
  starting transfers between devices: 3.92 us -> 36.6 us
  Pallas kernels: 0 us -> 16.8 us
  between operations: 16.9 us -> 1.12 us
  matrix products: 14 us -> 0 us
  local copies, waits for them, and re-layouts: 1.7 us -> 8.68 us
    reduce_scatter x1 -> x0, waiting for transfers between devices: 63.6 us -> none  [body(): lax.psum_scatter(jnp.dot(attended, w_out, preferred_element_type=jnp.floa...]
    all_gather x1 -> x0, waiting for transfers between devices: 60 us -> none  [body(): lax.all_gather(frames, 'head', axis=1, tiled=True).astype(jnp.float32)]
    ppermute x0 -> x25, waiting for transfers between devices: none -> 58.1 us  [the longest x4 37.9 us: outward(): return lax.ppermute(value, 'head', [(1, 0), (2, 3)])]
    ppermute x0 -> x25, starting transfers between devices: none -> 28.7 us  [the longest x9 8.21 us: across_plane(): lax.ppermute(piece, PLANE, [(i, i ^ delta) for i in range(plane)])]
    pallas_call x0 -> x4, Pallas kernels: none -> 16.8 us  [the longest x2 12.4 us: project_qkv(): pl.pallas_call(functools.partial(qkv_kernel, [len(group) for group in gro...]
    dot_general x11 -> x0, matrix products: 14 us -> none  [the longest x1 7.82 us: body(): jnp.einsum('crd,dke->crke', shaped, w_qkv, preferred_element_type=jnp.flo...]
    unnamed x4 -> x36, local copies, waits for them, and re-layouts: 0.09 us -> 7.5 us
    ppermute x3 -> x6, starting transfers between devices: 3.88 us -> 7.88 us  [from_behind(): return lax.ppermute(value, axis, pairs)]
  transfers between devices with their start and end apart: 5 -> 31, of which waited for: 3 -> 16; matrix products, arithmetic and copies ran while one was open for 2% -> 4% of each run, Pallas kernels for 0% -> 9%
where the time goes in v1:
time: 139 us; the launch traced here: 137 us
  waiting for transfers between devices  67.9 us (49%)
  starting transfers between devices  36.6 us (26%)
  Pallas kernels  16.8 us (12%)
  local copies, waits for them, and re-layouts  8.68 us (6%)
  other arithmetic  5.92 us (4%)
    ppermute x4, waiting for transfers between devices, outward(): return lax.ppermute(value, 'head', [(1, 0), (2, 3)])  37.9 us
    pallas_call x2, Pallas kernels, project_qkv(): pl.pallas_call(functools.partial(qkv_kernel, [len(group) for group in gro...  12.4 us
    ppermute x9, waiting for transfers between devices, across_plane(): lax.ppermute(piece, PLANE, [(i, i ^ delta) for i in range(plane)])  11.1 us
    ppermute x6, waiting for transfers between devices, from_behind(): return lax.ppermute(value, axis, pairs)  9.8 us
    ppermute x9, starting transfers between devices, across_plane(): lax.ppermute(piece, PLANE, [(i, i ^ delta) for i in range(plane)])  8.21 us
    ppermute x6, starting transfers between devices, from_behind(): return lax.ppermute(value, axis, pairs)  7.88 us
    unnamed x36, local copies, waits for them, and re-layouts  7.5 us
    ppermute x2, starting transfers between devices, pair(): return lax.ppermute(value, 'head', [(0, 1), (1, 0), (2, 3), (3, 2)])  5.78 us
  transfers between devices with their start and end apart: 31, of which 16 were waited for; matrix products, arithmetic and copies ran while one was open for 4% of the time, Pallas kernels for 9%

profile of v1, /device:TPU:3, one launch (start us, length us, event | category | flops | bytes accessed | tf_op | source)
XLA Modules:
  0.0 137.0 jit_solution(8613804188704703985)
XLA Ops:
  1.1 1.4 collective-permute-start
  2.5 1.4 %collective-permute-start.1 = (bf16[256,768]{1,0:T(8,128)(2,1)S(1)}, bf16[256,768]{1,0:T(8,128)(2,1)}, u32[]{:S(2)}, u32[]{:S(2)}) collective-permute-start(bf16[256,768]{1,0:T(8,128)(2,1)S(1)} %constant_dynamic-slice_fusion.1), channel_id=1, source_target_pairs={{1,2},{2,1},{5,6},{6,5},{9,10},{10,9},{13,14},{14,13},{17,18},{18,... | collective-permute-start | bytes 1179656 | tf_op jit(solution)/shard_map/ppermute | solution.py:196
  4.5 1.4 %fusion = f32[64]{0:T(128)S(1)} fusion(bf16[1,64,6144]{2,1,0:T(8,128)(2,1)} %param.6), kind=kLoop, calls=%fused_computation.2 | loop fusion | flops 1179584 | bytes 786688 | tf_op jit(solution)/shard_map/reduce_sum | solution.py:217
  5.9 1.8 %constant_dynamic-slice_fusion.2 = (f32[1,1,6144]{2,0,1:T(1,128)}, f32[1,1,6144]{2,0,1:T(1,128)S(1)}, f32[1,1,6144]{2,0,1:T(1,128)S(1)}) fusion(f32[8,3,6144]{2,0,1:T(8,128)} %param.11, s32[]{:T(128)S(6)} %select_n.64, s32[]{:T(128)S(6)} %add.61, s32[]{:T(128)S(6)} %add.60), kind=kLoop, calls=%fused_computation.23 | loop fusion | flops 6144 | bytes 147468 | tf_op jit(solution)/shard_map/slice | solution.py:235
  8.0 3.1 %collective-permute-done.refs_0_ = bf16[256,768]{1,0:T(8,128)(2,1)S(1)} collective-permute-done((bf16[256,768]{1,0:T(8,128)(2,1)S(1)}, bf16[256,768]{1,0:T(8,128)(2,1)S(1)}, u32[]{:S(2)}, u32[]{:S(2)}) %collective-permute-start) | collective-permute-done | bytes 393248 | tf_op jit(solution)/shard_map/ppermute | solution.py:193
  11.2 4.4 %collective-permute-start.2 = (bf16[64,6144]{1,0:T(8,128)(2,1)S(1)}, bf16[64,6144]{1,0:T(8,128)(2,1)S(1)}, u32[]{:S(2)}, u32[]{:S(2)}) collective-permute-start(bf16[64,6144]{1,0:T(8,128)(2,1)S(1)} %fusion.3.refs_0_), channel_id=1, source_target_pairs={{0,1},{1,0},{2,3},{3,2},{4,5},{5,4},{6,7},{7,6},{8,9},{9,8},{10,11... | collective-permute-start | bytes 2359304 | tf_op jit(solution)/shard_map/ppermute | solution.py:193
  19.6 20.8 %collective-permute-done.5 = bf16[256,768]{1,0:T(8,128)(2,1)} collective-permute-done((bf16[256,768]{1,0:T(8,128)(2,1)}, bf16[256,768]{1,0:T(8,128)(2,1)}, u32[]{:S(2)}, u32[]{:S(2)}) %collective-permute-start.5) | collective-permute-done | bytes 393248 | tf_op jit(solution)/shard_map/ppermute | solution.py:199
  40.4 1.6 %collective-permute-start.3 = (bf16[64,6144]{1,0:T(8,128)(2,1)S(1)}, bf16[64,6144]{1,0:T(8,128)(2,1)}, u32[]{:S(2)}, u32[]{:S(2)}) collective-permute-start(bf16[64,6144]{1,0:T(8,128)(2,1)S(1)} %fusion.3.refs_0_), channel_id=1, source_target_pairs={{1,2},{2,1},{5,6},{6,5},{9,10},{10,9},{13,14},{14,13},{17,18},{18,... | collective-permute-start | bytes 2359304 | tf_op jit(solution)/shard_map/ppermute | solution.py:196
  50.1 4.4 %collective-permute-done.10.refs_5_ = bf16[256,768]{1,0:T(8,128)(2,1)S(1)} collective-permute-done((bf16[256,768]{1,0:T(8,128)(2,1)S(1)}, bf16[256,768]{1,0:T(8,128)(2,1)S(1)}, u32[]{:S(2)}, u32[]{:S(2)}) %collective-permute-start.10) | collective-permute-done | bytes 393248 | tf_op jit(solution)/shard_map/ppermute | solution.py:206
  57.3 6.6 %collective-permute-done.12.refs_7_ = bf16[256,768]{1,0:T(8,128)(2,1)S(1)} collective-permute-done((bf16[256,768]{1,0:T(8,128)(2,1)S(1)}, bf16[256,768]{1,0:T(8,128)(2,1)S(1)}, u32[]{:S(2)}, u32[]{:S(2)}) %collective-permute-start.12) | collective-permute-done | bytes 393248 | tf_op jit(solution)/shard_map/ppermute | solution.py:206
  66.0 14.6 %collective-permute-done.15 = bf16[256,768]{1,0:T(8,128)(2,1)S(1)} collective-permute-done((bf16[256,768]{1,0:T(8,128)(2,1)S(1)}, bf16[256,768]{1,0:T(8,128)(2,1)S(1)}, u32[]{:S(2)}, u32[]{:S(2)}) %collective-permute-start.15) | collective-permute-done | bytes 393248 | tf_op jit(solution)/shard_map/ppermute | solution.py:199
  83.3 3.7 %copy-done = bf16[6144,3,256]{2,0,1:T(8,128)(2,1)S(1)} copy-done((bf16[6144,3,256]{2,0,1:T(8,128)(2,1)S(1)}, bf16[6144,3,256]{2,0,1:T(8,128)(2,1)}, u32[]{:S(2)}) %copy-start) | copy-done | bytes 9437208
  87.0 6.8 %project_qkv.2 = bf16[192,768]{1,0:T(8,128)(2,1)S(1)} custom-call(s32[1]{0:T(128)} %bitcast.1.outer_ref, bf16[64,6144]{1,0:T(8,128)(2,1)S(1)} %fusion.3.refs_0_, bf16[64,6144]{1,0:T(8,128)(2,1)S(1)} %collective-permute-done.2.refs_1_, bf16[64,6144]{1,0:T(8,128)(2,1)} %collective-permute-done.4.refs_2_, bf16[64,6144]{1,0:T(8,128)(2,1)} %collective-permute-done.3.refs_3_, ...), custom_call_target="tpu_custom_call" | custom-call | flops 1811939328 | bytes 11796480 | tf_op jit(solution)/shard_map/project_qkv/pallas_call | solution.py:108
  98.0 2.5 %collective-permute-done.13.refs_0_ = bf16[64,6144]{1,0:T(8,128)(2,1)} collective-permute-done((bf16[64,6144]{1,0:T(8,128)(2,1)S(1)}, bf16[64,6144]{1,0:T(8,128)(2,1)}, u32[]{:S(2)}, u32[]{:S(2)}) %collective-permute-start.13) | collective-permute-done | bytes 786464 | tf_op jit(solution)/shard_map/ppermute | solution.py:199
  100.4 5.7 %project_qkv.3 = bf16[64,768]{1,0:T(8,128)(2,1)S(1)} custom-call(s32[1]{0:T(128)} %bitcast.1.outer_ref, bf16[64,6144]{1,0:T(8,128)(2,1)} %collective-permute-done.13.refs_0_, bf16[64,6144]{1,0:T(8,128)(2,1)S(1)} %collective-permute-done.9.refs_1_, bf16[3,6144,256]{2,1,0:T(8,128)(2,1)S(1)} %bitcast.21), custom_call_target="tpu_custom_call" | custom-call | flops 603979776 | bytes 10223616 | tf_op jit(solution)/shard_map/project_qkv/pallas_call | solution.py:108
  106.2 1.4 %collective-permute-start.20 = (bf16[64,512]{1,0:T(8,128)(2,1)S(1)}, bf16[64,512]{1,0:T(8,128)(2,1)S(1)}, u32[]{:S(2)}, u32[]{:S(2)}) collective-permute-start(bf16[64,512]{1,0:T(8,128)(2,1)S(1)} %slice.62.refs_1_), channel_id=1, source_target_pairs={{0,4},{4,8},{8,12},{1,5},{5,9},{9,13},{2,6},{6,10},{10,14},{3,7},{... | collective-permute-start | bytes 196616 | tf_op jit(solution)/shard_map/ppermute | solution.py:17
  111.6 2.3 %collective-permute-done.23.refs_6_ = bf16[192,512]{1,0:T(8,128)(2,1)S(1)} collective-permute-done((bf16[192,512]{1,0:T(8,128)(2,1)S(1)}, bf16[192,512]{1,0:T(8,128)(2,1)S(1)}, u32[]{:S(2)}, u32[]{:S(2)}) %collective-permute-start.23) | collective-permute-done | bytes 196640 | tf_op jit(solution)/shard_map/ppermute | solution.py:17
  114.0 3.6 %collective-permute-done.22.refs_5_ = bf16[64,512]{1,0:T(8,128)(2,1)S(1)} collective-permute-done((bf16[64,512]{1,0:T(8,128)(2,1)S(1)}, bf16[64,512]{1,0:T(8,128)(2,1)S(1)}, u32[]{:S(2)}, u32[]{:S(2)}) %collective-permute-start.22) | collective-permute-done | bytes 65568 | tf_op jit(solution)/shard_map/ppermute | solution.py:17
  117.5 2.5 %collective-permute-done.24.refs_7_ = bf16[64,512]{1,0:T(8,128)(2,1)S(1)} collective-permute-done((bf16[64,512]{1,0:T(8,128)(2,1)S(1)}, bf16[64,512]{1,0:T(8,128)(2,1)S(1)}, u32[]{:S(2)}, u32[]{:S(2)}) %collective-permute-start.24) | collective-permute-done | bytes 65568 | tf_op jit(solution)/shard_map/ppermute | solution.py:17
  120.0 2.2 %attend.1 = bf16[256,256]{1,0:T(8,128)(2,1)S(1)} custom-call(bf16[256,256]{1,0:T(8,128)(2,1)S(1)} %pad_maximum_fusion.1.q_ref, bf16[192,512]{1,0:T(8,128)(2,1)S(1)} %slice.61.refs_0_, bf16[64,512]{1,0:T(8,128)(2,1)S(1)} %slice.62.refs_1_, bf16[192,512]{1,0:T(8,128)(2,1)S(1)} %collective-permute-done.19.refs_2_, ...), custom_call_target="tpu_custom_call" | custom-call | flops 268435456 | bytes 1310720 | tf_op jit(solution)/shard_map/attend/pallas_call | solution.py:60
  122.2 2.4 %collective-permute-start.26 = (bf16[64,256]{1,0:T(8,128)(2,1)S(1)}, bf16[64,256]{1,0:T(8,128)(2,1)S(1)}, u32[]{:S(2)}, u32[]{:S(2)}) collective-permute-start(bf16[64,256]{1,0:T(8,128)(2,1)S(1)} %get-tuple-element.19), channel_id=1, source_target_pairs={{0,2},{1,3},{2,0},{3,1},{4,6},{5,7},{6,4},{7,5},{8,10},{9,11},{10,... | collective-permute-start | bytes 98312 | tf_op jit(solution)/shard_map/ppermute | solution.py:255
  124.7 1.5 %collective-permute-start.27 = (bf16[64,256]{1,0:T(8,128)(2,1)S(1)}, bf16[64,256]{1,0:T(8,128)(2,1)S(1)}, u32[]{:S(2)}, u32[]{:S(2)}) collective-permute-start(bf16[64,256]{1,0:T(8,128)(2,1)S(1)} %get-tuple-element.20), channel_id=1, source_target_pairs={{0,3},{1,2},{2,1},{3,0},{4,7},{5,6},{6,5},{7,4},{8,11},{9,10},{10,... | collective-permute-start | bytes 98312 | tf_op jit(solution)/shard_map/ppermute | solution.py:255
  126.3 3.5 %collective-permute-done.27 = bf16[64,256]{1,0:T(8,128)(2,1)S(1)} collective-permute-done((bf16[64,256]{1,0:T(8,128)(2,1)S(1)}, bf16[64,256]{1,0:T(8,128)(2,1)S(1)}, u32[]{:S(2)}, u32[]{:S(2)}) %collective-permute-start.27) | collective-permute-done | bytes 32800 | tf_op jit(solution)/shard_map/ppermute | solution.py:255
  131.9 2.2 %project_out.1 = bf16[128,3072]{1,0:T(8,128)(2,1)S(1)} custom-call(s32[1]{0:T(128)} %bitcast.place_ref, bf16[128,1024]{1,0:T(8,128)(2,1)S(1)} %pad_maximum_fusion.att_ref, f32[2,6144]{1,0:T(2,128)S(1)} %pad_maximum_fusion.3.gate_ref, bf16[256,6144]{1,0:T(8,128)(2,1)S(1)} %copy-done.2, bf16[256,768]{1,0:T(8,128)(2,1)S(1)} %collective-permute-done.refs_0_, ...), custom_call_target="tpu_custom_call" | custom-call | flops 805306368 | bytes 6291456 | tf_op jit(solution)/shard_map/project_out/pallas_call | solution.py:159
  (99 shorter events, 34.2 us)
Async XLA Ops:
  1.1 10.0 %collective-permute-start = (bf16[256,768]{1,0:T(8,128)(2,1)S(1)}, bf16[256,768]{1,0:T(8,128)(2,1)S(1)}, u32[]{:S(2)}, u32[]{:S(2)}) collective-permute-start(bf16[256,768]{1,0:T(8,128)(2,1)S(1)} %constant_dynamic-slice_fusion.1), channel_id=1, source_target_pairs={{0,1},{1,0},{2,3},{3,2},{4,5},{5,4},{6,7},{7,6},{8,9},{9,8},{10,11... | collective-permute-start | bytes 1179656 | tf_op jit(solution)/shard_map/ppermute | solution.py:193
  2.5 8.7 %collective-permute-start.1 = (bf16[256,768]{1,0:T(8,128)(2,1)S(1)}, bf16[256,768]{1,0:T(8,128)(2,1)}, u32[]{:S(2)}, u32[]{:S(2)}) collective-permute-start(bf16[256,768]{1,0:T(8,128)(2,1)S(1)} %constant_dynamic-slice_fusion.1), channel_id=1, source_target_pairs={{1,2},{2,1},{5,6},{6,5},{9,10},{10,9},{13,14},{14,13},{17,18},{18,... | collective-permute-start | bytes 1179656 | tf_op jit(solution)/shard_map/ppermute | solution.py:196
  11.2 33.1 %collective-permute-start.2 = (bf16[64,6144]{1,0:T(8,128)(2,1)S(1)}, bf16[64,6144]{1,0:T(8,128)(2,1)S(1)}, u32[]{:S(2)}, u32[]{:S(2)}) collective-permute-start(bf16[64,6144]{1,0:T(8,128)(2,1)S(1)} %fusion.3.refs_0_), channel_id=1, source_target_pairs={{0,1},{1,0},{2,3},{3,2},{4,5},{5,4},{6,7},{7,6},{8,9},{9,8},{10,11... | collective-permute-start | bytes 2359304 | tf_op jit(solution)/shard_map/ppermute | solution.py:193
  15.6 24.8 %collective-permute-start.5 = (bf16[256,768]{1,0:T(8,128)(2,1)}, bf16[256,768]{1,0:T(8,128)(2,1)}, u32[]{:S(2)}, u32[]{:S(2)}) collective-permute-start(bf16[256,768]{1,0:T(8,128)(2,1)} %collective-permute-done.1), channel_id=1, source_target_pairs={{1,0},{2,3},{5,4},{6,7},{9,8},{10,11},{13,12},{14,15},{17,16},{18,... | collective-permute-start | bytes 1179656 | tf_op jit(solution)/shard_map/ppermute | solution.py:199
  16.9 25.1 %collective-permute-start.6 = (bf16[256,768]{1,0:T(8,128)(2,1)S(1)}, bf16[256,768]{1,0:T(8,128)(2,1)S(1)}, u32[]{:S(2)}, u32[]{:S(2)}) collective-permute-start(bf16[256,768]{1,0:T(8,128)(2,1)S(1)} %collective-permute-done.refs_0_), channel_id=1, source_target_pairs={{0,8},{4,12},{8,0},{12,4},{16,24},{20,28},{24,16},{28,20},{1,9},{5... | collective-permute-start | bytes 1179656 | tf_op jit(solution)/shard_map/ppermute | solution.py:206
  17.2 26.2 %collective-permute-start.7 = (bf16[256,768]{1,0:T(8,128)(2,1)S(1)}, bf16[256,768]{1,0:T(8,128)(2,1)S(1)}, u32[]{:S(2)}, u32[]{:S(2)}) collective-permute-start(bf16[256,768]{1,0:T(8,128)(2,1)S(1)} %collective-permute-done.refs_0_), channel_id=1, source_target_pairs={{0,16},{4,20},{8,24},{12,28},{16,0},{20,4},{24,8},{28,12},{1,17},{... | collective-permute-start | bytes 1179656 | tf_op jit(solution)/shard_map/ppermute | solution.py:206
  18.4 25.0 %collective-permute-start.8 = (bf16[256,768]{1,0:T(8,128)(2,1)S(1)}, bf16[256,768]{1,0:T(8,128)(2,1)S(1)}, u32[]{:S(2)}, u32[]{:S(2)}) collective-permute-start(bf16[256,768]{1,0:T(8,128)(2,1)S(1)} %collective-permute-done.refs_0_), channel_id=1, source_target_pairs={{0,24},{4,28},{8,16},{12,20},{16,8},{20,12},{24,0},{28,4},{1,25},{... | collective-permute-start | bytes 1179656 | tf_op jit(solution)/shard_map/ppermute | solution.py:206
  42.7 6.2 %collective-permute-start.14 = (bf16[256,768]{1,0:T(8,128)(2,1)S(1)}, bf16[256,768]{1,0:T(8,128)(2,1)S(1)}, u32[]{:S(2)}, u32[]{:S(2)}) collective-permute-start(bf16[256,768]{1,0:T(8,128)(2,1)S(1)} %collective-permute-done.refs_0_), channel_id=1, source_target_pairs={{1,2},{2,1},{5,6},{6,5},{9,10},{10,9},{13,14},{14,13},{17,18},{18,... | collective-permute-start | bytes 1179656 | tf_op jit(solution)/shard_map/ppermute | solution.py:196
  44.2 20.4 %collective-permute-start.9 = (bf16[64,6144]{1,0:T(8,128)(2,1)S(1)}, bf16[64,6144]{1,0:T(8,128)(2,1)S(1)}, u32[]{:S(2)}, u32[]{:S(2)}) collective-permute-start(bf16[64,6144]{1,0:T(8,128)(2,1)S(1)} %collective-permute-done.2.refs_1_), channel_id=1, source_target_pairs={{1,2},{2,1},{5,6},{6,5},{9,10},{10,9},{13,14},{14,13},{17,18},{18,... | collective-permute-start | bytes 2359304 | tf_op jit(solution)/shard_map/ppermute | solution.py:196
  46.0 8.5 %collective-permute-start.10 = (bf16[256,768]{1,0:T(8,128)(2,1)S(1)}, bf16[256,768]{1,0:T(8,128)(2,1)S(1)}, u32[]{:S(2)}, u32[]{:S(2)}) collective-permute-start(bf16[256,768]{1,0:T(8,128)(2,1)S(1)} %broadcast_select_fusion.1.refs_4_), channel_id=1, source_target_pairs={{0,8},{4,12},{8,0},{12,4},{16,24},{20,28},{24,16},{28,20},{1,9},{5... | collective-permute-start | bytes 1179656 | tf_op jit(solution)/shard_map/ppermute | solution.py:206
  46.3 37.0 %collective-permute-start.4 = (bf16[64,6144]{1,0:T(8,128)(2,1)}, bf16[64,6144]{1,0:T(8,128)(2,1)}, u32[]{:S(2)}, u32[]{:S(2)}) collective-permute-start(bf16[64,6144]{1,0:T(8,128)(2,1)} %collective-permute-done.3.refs_3_), channel_id=1, source_target_pairs={{1,0},{2,3},{5,4},{6,7},{9,8},{10,11},{13,12},{14,15},{17,16},{18,... | collective-permute-start | bytes 2359304 | tf_op jit(solution)/shard_map/ppermute | solution.py:199
  47.6 8.9 %collective-permute-start.11 = (bf16[256,768]{1,0:T(8,128)(2,1)S(1)}, bf16[256,768]{1,0:T(8,128)(2,1)S(1)}, u32[]{:S(2)}, u32[]{:S(2)}) collective-permute-start(bf16[256,768]{1,0:T(8,128)(2,1)S(1)} %broadcast_select_fusion.1.refs_4_), channel_id=1, source_target_pairs={{0,16},{4,20},{8,24},{12,28},{16,0},{20,4},{24,8},{28,12},{1,17},{... | collective-permute-start | bytes 1179656 | tf_op jit(solution)/shard_map/ppermute | solution.py:206
  48.9 15.0 %collective-permute-start.12 = (bf16[256,768]{1,0:T(8,128)(2,1)S(1)}, bf16[256,768]{1,0:T(8,128)(2,1)S(1)}, u32[]{:S(2)}, u32[]{:S(2)}) collective-permute-start(bf16[256,768]{1,0:T(8,128)(2,1)S(1)} %broadcast_select_fusion.1.refs_4_), channel_id=1, source_target_pairs={{0,24},{4,28},{8,16},{12,20},{16,8},{20,12},{24,0},{28,4},{1,25},{... | collective-permute-start | bytes 1179656 | tf_op jit(solution)/shard_map/ppermute | solution.py:206
  55.2 25.3 %collective-permute-start.15 = (bf16[256,768]{1,0:T(8,128)(2,1)S(1)}, bf16[256,768]{1,0:T(8,128)(2,1)S(1)}, u32[]{:S(2)}, u32[]{:S(2)}) collective-permute-start(bf16[256,768]{1,0:T(8,128)(2,1)S(1)} %collective-permute-done.14), channel_id=1, source_target_pairs={{1,0},{2,3},{5,4},{6,7},{9,8},{10,11},{13,12},{14,15},{17,16},{18,... | collective-permute-start | bytes 1179656 | tf_op jit(solution)/shard_map/ppermute | solution.py:199
  64.7 35.8 %collective-permute-start.13 = (bf16[64,6144]{1,0:T(8,128)(2,1)S(1)}, bf16[64,6144]{1,0:T(8,128)(2,1)}, u32[]{:S(2)}, u32[]{:S(2)}) collective-permute-start(bf16[64,6144]{1,0:T(8,128)(2,1)S(1)} %collective-permute-done.9.refs_1_), channel_id=1, source_target_pairs={{1,0},{2,3},{5,4},{6,7},{9,8},{10,11},{13,12},{14,15},{17,16},{18,... | collective-permute-start | bytes 2359304 | tf_op jit(solution)/shard_map/ppermute | solution.py:199
  80.6 14.5 %collective-permute-start.16 = (bf16[256,768]{1,0:T(8,128)(2,1)S(1)}, bf16[256,768]{1,0:T(8,128)(2,1)}, u32[]{:S(2)}, u32[]{:S(2)}) collective-permute-start(bf16[256,768]{1,0:T(8,128)(2,1)S(1)} %broadcast_select_fusion.refs_8_), channel_id=1, source_target_pairs={{0,8},{4,12},{8,0},{12,4},{16,24},{20,28},{24,16},{28,20},{1,9},{5... | collective-permute-start | bytes 1179656 | tf_op jit(solution)/shard_map/ppermute | solution.py:206
  81.2 15.2 %collective-permute-start.17 = (bf16[256,768]{1,0:T(8,128)(2,1)S(1)}, bf16[256,768]{1,0:T(8,128)(2,1)}, u32[]{:S(2)}, u32[]{:S(2)}) collective-permute-start(bf16[256,768]{1,0:T(8,128)(2,1)S(1)} %broadcast_select_fusion.refs_8_), channel_id=1, source_target_pairs={{0,16},{4,20},{8,24},{12,28},{16,0},{20,4},{24,8},{28,12},{1,17},{... | collective-permute-start | bytes 1179656 | tf_op jit(solution)/shard_map/ppermute | solution.py:206
  82.2 15.8 %collective-permute-start.18 = (bf16[256,768]{1,0:T(8,128)(2,1)S(1)}, bf16[256,768]{1,0:T(8,128)(2,1)S(1)}, u32[]{:S(2)}, u32[]{:S(2)}) collective-permute-start(bf16[256,768]{1,0:T(8,128)(2,1)S(1)} %broadcast_select_fusion.refs_8_), channel_id=1, source_target_pairs={{0,24},{4,28},{8,16},{12,20},{16,8},{20,12},{24,0},{28,4},{1,25},{... | collective-permute-start | bytes 1179656 | tf_op jit(solution)/shard_map/ppermute | solution.py:206
  93.8 15.1 %collective-permute-start.19 = (bf16[192,512]{1,0:T(8,128)(2,1)S(1)}, bf16[192,512]{1,0:T(8,128)(2,1)S(1)}, u32[]{:S(2)}, u32[]{:S(2)}) collective-permute-start(bf16[192,512]{1,0:T(8,128)(2,1)S(1)} %slice.61.refs_0_), channel_id=1, source_target_pairs={{0,4},{4,8},{8,12},{1,5},{5,9},{9,13},{2,6},{6,10},{10,14},{3,7},{... | collective-permute-start | bytes 589832 | tf_op jit(solution)/shard_map/ppermute | solution.py:17
  95.1 16.4 %collective-permute-start.21 = (bf16[192,512]{1,0:T(8,128)(2,1)S(1)}, bf16[192,512]{1,0:T(8,128)(2,1)S(1)}, u32[]{:S(2)}, u32[]{:S(2)}) collective-permute-start(bf16[192,512]{1,0:T(8,128)(2,1)S(1)} %slice.61.refs_0_), channel_id=1, source_target_pairs={{0,8},{4,12},{1,9},{5,13},{2,10},{6,14},{3,11},{7,15},{16,24},{20,... | collective-permute-start | bytes 589832 | tf_op jit(solution)/shard_map/ppermute | solution.py:17
  96.5 17.4 %collective-permute-start.23 = (bf16[192,512]{1,0:T(8,128)(2,1)S(1)}, bf16[192,512]{1,0:T(8,128)(2,1)S(1)}, u32[]{:S(2)}, u32[]{:S(2)}) collective-permute-start(bf16[192,512]{1,0:T(8,128)(2,1)S(1)} %slice.61.refs_0_), channel_id=1, source_target_pairs={{0,12},{1,13},{2,14},{3,15},{16,28},{17,29},{18,30},{19,31}} | collective-permute-start | bytes 589832 | tf_op jit(solution)/shard_map/ppermute | solution.py:17
  106.2 7.8 %collective-permute-start.20 = (bf16[64,512]{1,0:T(8,128)(2,1)S(1)}, bf16[64,512]{1,0:T(8,128)(2,1)S(1)}, u32[]{:S(2)}, u32[]{:S(2)}) collective-permute-start(bf16[64,512]{1,0:T(8,128)(2,1)S(1)} %slice.62.refs_1_), channel_id=1, source_target_pairs={{0,4},{4,8},{8,12},{1,5},{5,9},{9,13},{2,6},{6,10},{10,14},{3,7},{... | collective-permute-start | bytes 196616 | tf_op jit(solution)/shard_map/ppermute | solution.py:17
  107.6 9.9 %collective-permute-start.22 = (bf16[64,512]{1,0:T(8,128)(2,1)S(1)}, bf16[64,512]{1,0:T(8,128)(2,1)S(1)}, u32[]{:S(2)}, u32[]{:S(2)}) collective-permute-start(bf16[64,512]{1,0:T(8,128)(2,1)S(1)} %slice.62.refs_1_), channel_id=1, source_target_pairs={{0,8},{4,12},{1,9},{5,13},{2,10},{6,14},{3,11},{7,15},{16,24},{20,... | collective-permute-start | bytes 196616 | tf_op jit(solution)/shard_map/ppermute | solution.py:17
  108.9 11.1 %collective-permute-start.24 = (bf16[64,512]{1,0:T(8,128)(2,1)S(1)}, bf16[64,512]{1,0:T(8,128)(2,1)S(1)}, u32[]{:S(2)}, u32[]{:S(2)}) collective-permute-start(bf16[64,512]{1,0:T(8,128)(2,1)S(1)} %slice.62.refs_1_), channel_id=1, source_target_pairs={{0,12},{1,13},{2,14},{3,15},{16,28},{17,29},{18,30},{19,31}} | collective-permute-start | bytes 196616 | tf_op jit(solution)/shard_map/ppermute | solution.py:17
  (25 other events, 300.5 us)

commit v2 on v1

--- a/solution.py
+++ b/solution.py
@@ -37,7 +37,7 @@
                 (((1,), (1,)), ((), ())),
                 preferred_element_type=jnp.float32,
             )
-            scores.append(jnp.where(seen_ref[d // 2] > 0, raw * score_scale, -1e30))
+            scores.append(jnp.where(seen_ref[d] > 0, raw * score_scale, -1e30))
         peak = jnp.max(scores[0], axis=1, keepdims=True)
         for part in scores[1:]:
             peak = jnp.maximum(peak, jnp.max(part, axis=1, keepdims=True))
@@ -72,54 +72,87 @@
     )(queries, *kv, seen)
 
 
+def shape_kernel(level_ref, frames_ref, style_ref, out_ref, gate_ref):
+    count, _, span = out_ref.shape
+    floats = frames_ref[...].astype(jnp.float32)
+    scale = lax.rsqrt(jnp.mean(floats * floats, axis=-1, keepdims=True) + 1e-06)
+    for c in range(count):
+        part = slice(c * span, (c + 1) * span)
+        normed = frames_ref[:, part].astype(jnp.float32) * scale
+        shaped = normed * (1.0 + style_ref[0, 1:2, part]) + style_ref[0, 0:1, part]
+        out_ref[c] = shaped.astype(jnp.bfloat16)
+    gate_ref[...] = style_ref[0, 2:3]
+
+
+def shape_tokens(levels, frames, modulation, count):
+    rows, width = frames.shape
+    span = width // count
+    blocks, gate = pl.pallas_call(
+        shape_kernel,
+        grid_spec=pltpu.PrefetchScalarGridSpec(
+            num_scalar_prefetch=1,
+            grid=(1,),
+            in_specs=[
+                pl.BlockSpec((rows, width), lambda i, level: (0, 0)),
+                pl.BlockSpec((1,) + modulation.shape[1:], lambda i, level: (level[0], 0, 0)),
+            ],
+            out_specs=[
+                pl.BlockSpec((count, rows, span), lambda i, level: (0, 0, 0)),
+                pl.BlockSpec((1, width), lambda i, level: (0, 0)),
+            ],
+        ),
+        out_shape=[
+            jax.ShapeDtypeStruct((count, rows, span), jnp.bfloat16),
+            jax.ShapeDtypeStruct((1, width), jnp.float32),
+        ],
+        compiler_params=pltpu.CompilerParams(vmem_limit_bytes=32 << 20),
+        cost_estimate=pl.CostEstimate(
+            flops=6 * rows * width, bytes_accessed=4 * rows * width, transcendentals=rows
+        ),
+        name="shape_tokens",
+    )(levels, frames, modulation)
+    return blocks.reshape(count * rows, span), gate
+
+
 def qkv_kernel(groups, outer_ref, *refs):
     count = sum(groups)
-    tokens, w_ref, out_ref, rows_ref, acc_ref = refs[:count], *refs[count:]
-    rows = tokens[0].shape[0]
+    tokens, w_ref, out_ref, rows_ref = refs[:count], *refs[count:]
     cols = w_ref.shape[2]
-    step = pl.program_id(0)
-    at = 0
-    for i, size in enumerate(groups):
-        block = tokens[at][...]
-        if size == 2:
-            block = jnp.where(outer_ref[0] > 0, block, tokens[at + 1][...])
-        rows_ref[i * rows : (i + 1) * rows] = block
-        at += size
-
-    @pl.when(step == 0)
-    def _():
-        acc_ref[...] = jnp.zeros_like(acc_ref)
-
+    chunk = rows_ref.shape[1]
+    rows = rows_ref.shape[0] // len(groups)
+    total = [jnp.zeros((rows_ref.shape[0], cols), jnp.float32) for _ in range(3)]
+    for k in range(w_ref.shape[1] // chunk):
+        at = 0
+        source = slice(k * rows, (k + 1) * rows)
+        for i, size in enumerate(groups):
+            block = tokens[at][source]
+            if size == 2:
+                block = jnp.where(outer_ref[0] > 0, block, tokens[at + 1][source])
+            rows_ref[i * rows : (i + 1) * rows] = block
+            at += size
+        for j in range(3):
+            total[j] += jnp.dot(
+                rows_ref[...],
+                w_ref[j, k * chunk : (k + 1) * chunk],
+                preferred_element_type=jnp.float32,
+            )
     for j in range(3):
-        acc_ref[:, j * cols : (j + 1) * cols] += jnp.dot(
-            rows_ref[...], w_ref[j], preferred_element_type=jnp.float32
-        )
-
-    @pl.when(step == pl.num_programs(0) - 1)
-    def _():
-        out_ref[...] = acc_ref[...].astype(out_ref.dtype)
-
-
-def project_qkv(outer, groups, weights, chunk):
+        out_ref[:, j * cols : (j + 1) * cols] = total[j].astype(out_ref.dtype)
+
+
+def project_qkv(outer, groups, weights, rows):
     tokens = [block for group in groups for block in group]
-    rows, width = tokens[0].shape
-    cols = weights.shape[2]
+    chunk = tokens[0].shape[1]
+    width, cols = weights.shape[1], weights.shape[2]
     total = rows * len(groups)
+    vmem = pl.BlockSpec(memory_space=pltpu.VMEM)
     return pl.pallas_call(
         functools.partial(qkv_kernel, [len(group) for group in groups]),
-        grid=(width // chunk,),
         out_shape=jax.ShapeDtypeStruct((total, 3 * cols), jnp.bfloat16),
-        in_specs=[pl.BlockSpec(memory_space=pltpu.SMEM)]
-        + [pl.BlockSpec((rows, chunk), lambda k: (0, k))] * len(tokens)
-        + [pl.BlockSpec((3, chunk, cols), lambda k: (0, k, 0))],
-        out_specs=pl.BlockSpec((total, 3 * cols), lambda k: (0, 0)),
-        scratch_shapes=[
-            pltpu.VMEM((total, chunk), jnp.bfloat16),
-            pltpu.VMEM((total, 3 * cols), jnp.float32),
-        ],
-        compiler_params=pltpu.CompilerParams(
-            dimension_semantics=("arbitrary",), vmem_limit_bytes=32 << 20
-        ),
+        in_specs=[pl.BlockSpec(memory_space=pltpu.SMEM)] + [vmem] * (len(tokens) + 1),
+        out_specs=vmem,
+        scratch_shapes=[pltpu.VMEM((total, chunk), jnp.bfloat16)],
+        compiler_params=pltpu.CompilerParams(vmem_limit_bytes=40 << 20),
         cost_estimate=pl.CostEstimate(
             flops=6 * total * width * cols,
             bytes_accessed=6 * width * cols + 2 * total * width,
@@ -211,43 +244,30 @@
     piece = lax.dynamic_slice_in_dim(w_out, chunk * span, span, 1)
     w_first = pair(piece)
     w_mid = middle(piece)
-
-    styles = lax.dynamic_index_in_dim(modulation, levels[0], 0, keepdims=False)
-    floats = frames[0].astype(jnp.float32)
-    normed = floats * lax.rsqrt(jnp.mean(floats * floats, axis=-1, keepdims=True) + 1e-06)
-    own = (normed * (1.0 + styles[1]) + styles[0]).astype(jnp.bfloat16)
-
-    ready = after(own, w_first, w_mid)
-    first = pair(ready)
-    mid = middle(ready)
-    w_far_mid = middle(w_first)
-    w_out_mid = outward(w_mid)
-    w_far_out = outward(w_far_mid)
+    own, gate = shape_tokens(levels, frames[0], modulation, plane)
+    gates = jnp.concatenate([gate, swap(gate)], axis=0)
+    high = own.shape[0]
+
+    first = pair(after(jnp.concatenate([own, w_mid], axis=0), gates))
+    mid = middle(jnp.concatenate([own, w_first], axis=0))
     w_first_pieces = across_plane(w_first)
-    w_second = jnp.where(outer, w_out_mid, w_mid)
-    w_second_pieces = across_plane(w_second)
-    w_third = jnp.where(outer, w_far_out, w_far_mid)
-    w_third_pieces = across_plane(w_third)
-    far_mid = middle(after(first, w_out_mid, *w_first_pieces))
+    far_mid = middle(after(first[:high], *w_first_pieces))
     out = outward(mid)
-    far_out = outward(after(far_mid, *w_second_pieces))
+    w_second_pieces = across_plane(jnp.where(outer, first[high:], w_mid))
+    far_out = outward(after(far_mid, out, *w_second_pieces))
+    w_third_pieces = across_plane(jnp.where(outer, out[high:], mid[high:]))
     pieces = w_first_pieces + w_second_pieces + w_third_pieces
-    gates = jnp.stack([styles[2], swap(styles[2])])
-
-    def exchange(value):
-        return [value] + [from_behind(value, "tract", d) for d in range(1, n_tract)]
-
-    early = project_qkv(outer_flag, [[own], [first], [out, mid]], w3, 768)
-    early_kv = exchange(early[:, cols:])
-    late = project_qkv(outer_flag, [[after(far_out, *w_third_pieces), far_mid]], w3, 768)
-    late_kv = exchange(late[:, cols:])
-    kv = [block for both in zip(early_kv, late_kv) for block in both]
+
+    early = project_qkv(outer_flag, [[own], [first], [out, mid]], w3, rows)
+    late = project_qkv(outer_flag, [[far_out, far_mid]], w3, rows)
+    qkv = jnp.concatenate([early, late], axis=0)
+    kv_own = qkv[:, cols:]
+    kv = [kv_own] + [from_behind(kv_own, "tract", d) for d in range(1, n_tract)]
     offsets = tract - lax.iota(jnp.int32, n_tract)
     seen = jnp.sum(
         jnp.where(offsets[:, None] == lax.iota(jnp.int32, n_tract)[None, :], visible, 0), axis=1
     )
-    queries = jnp.concatenate([early[:, :cols], late[:, :cols]], axis=0)
-    attended = attend(queries, kv, seen)
+    attended = attend(after(qkv[:, :cols], *w_third_pieces), kv, seen)
 
     blocks = [attended[i * rows : (i + 1) * rows] for i in range(4)]
     leaving = [blocks[1], jnp.where(outer, blocks[2], blocks[3]), jnp.where(outer, blocks[3], blocks[2])]

time: 139 us -> 127 us (0.914)
  starting transfers between devices: 36.6 us -> 29.6 us
  Pallas kernels: 16.8 us -> 11 us
  local copies, waits for them, and re-layouts: 8.68 us -> 13.5 us
  waiting for transfers between devices: 67.9 us -> 65.3 us
  other arithmetic: 5.92 us -> 3.97 us
    ppermute x4 -> x2, waiting for transfers between devices: 37.9 us -> 4.68 us  [outward(): return lax.ppermute(value, 'head', [(1, 0), (2, 3)])]
    ppermute x2, waiting for transfers between devices: 3.14 us -> 25.1 us  [pair(): return lax.ppermute(value, 'head', [(0, 1), (1, 0), (2, 3), (3, 2)])]
    ppermute x6 -> x3, waiting for transfers between devices: 9.8 us -> 15.6 us  [from_behind(): return lax.ppermute(value, axis, pairs)]
    pallas_call x2, Pallas kernels: 12.4 us -> 6.74 us  [project_qkv(): pl.pallas_call(functools.partial(qkv_kernel, [len(group) for group in gro...]
    unnamed x36 -> x51, local copies, waits for them, and re-layouts: 7.5 us -> 11.4 us
    ppermute x6 -> x3, starting transfers between devices: 7.88 us -> 4.14 us  [from_behind(): return lax.ppermute(value, axis, pairs)]
    ppermute x9, waiting for transfers between devices: 11.1 us -> 14.1 us  [across_plane(): lax.ppermute(piece, PLANE, [(i, i ^ delta) for i in range(plane)])]
    ppermute x4 -> x2, starting transfers between devices: 5.12 us -> 2.56 us  [outward(): return lax.ppermute(value, 'head', [(1, 0), (2, 3)])]
  transfers between devices with their start and end apart: 31 -> 25, of which waited for: 16 -> 14; matrix products, arithmetic and copies ran while one was open for 4% -> 4% of each run, Pallas kernels for 9% -> 6%
where the time goes in v2:
time: 127 us; the launch traced here: 124 us
  waiting for transfers between devices  65.3 us (51%)
  starting transfers between devices  29.6 us (23%)
  local copies, waits for them, and re-layouts  13.5 us (11%)
  Pallas kernels  11 us (9%)
  other arithmetic  3.97 us (3%)
    ppermute x2, waiting for transfers between devices, pair(): return lax.ppermute(value, 'head', [(0, 1), (1, 0), (2, 3), (3, 2)])  25.1 us
    ppermute x3, waiting for transfers between devices, from_behind(): return lax.ppermute(value, axis, pairs)  15.6 us
    ppermute x9, waiting for transfers between devices, across_plane(): lax.ppermute(piece, PLANE, [(i, i ^ delta) for i in range(plane)])  14.1 us
    unnamed x51, local copies, waits for them, and re-layouts  11.4 us
    ppermute x9, starting transfers between devices, across_plane(): lax.ppermute(piece, PLANE, [(i, i ^ delta) for i in range(plane)])  8.01 us
    ppermute x2, starting transfers between devices, pair(): return lax.ppermute(value, 'head', [(0, 1), (1, 0), (2, 3), (3, 2)])  7.01 us
    pallas_call x2, Pallas kernels, project_qkv(): pl.pallas_call(functools.partial(qkv_kernel, [len(group) for group in gro...  6.74 us
    ppermute x2, waiting for transfers between devices, outward(): return lax.ppermute(value, 'head', [(1, 0), (2, 3)])  4.68 us
  transfers between devices with their start and end apart: 25, of which 14 were waited for; matrix products, arithmetic and copies ran while one was open for 4% of the time, Pallas kernels for 6%

profile of v2, /device:TPU:3, one launch (start us, length us, event | category | flops | bytes accessed | tf_op | source)
XLA Modules:
  0.0 124.5 jit_solution(10653511139938282439)
XLA Ops:
  1.8 3.9 %collective-permute-start.3 = (bf16[256,768]{1,0:T(8,128)(2,1)S(1)}, bf16[256,768]{1,0:T(8,128)(2,1)S(1)}, u32[]{:S(2)}, u32[]{:S(2)}) collective-permute-start(bf16[256,768]{1,0:T(8,128)(2,1)S(1)} %constant_dynamic-slice_fusion), channel_id=1, source_target_pairs={{0,1},{1,0},{2,3},{3,2},{4,5},{5,4},{6,7},{7,6},{8,9},{9,8},{10,11... | collective-permute-start | bytes 1179656 | tf_op jit(solution)/shard_map/ppermute | solution.py:226
  5.7 1.5 %copy.8.style_ref = f32[8,3,6144]{2,1,0:T(4,128)S(1)} copy(f32[8,3,6144]{2,0,1:T(8,128)} %param.11) | data formatting | bytes 1179648 | tf_op args[5]
  9.6 4.6 %collective-permute-done.3.refs_0_ = bf16[256,768]{1,0:T(8,128)(2,1)S(1)} collective-permute-done((bf16[256,768]{1,0:T(8,128)(2,1)S(1)}, bf16[256,768]{1,0:T(8,128)(2,1)S(1)}, u32[]{:S(2)}, u32[]{:S(2)}) %collective-permute-start.3) | collective-permute-done | bytes 393248 | tf_op jit(solution)/shard_map/ppermute | solution.py:226
  15.8 3.1 %collective-permute-start.2 = (bf16[768,768]{1,0:T(8,128)(2,1)S(1)}, bf16[768,768]{1,0:T(8,128)(2,1)S(1)}, u32[]{:S(2)}, u32[]{:S(2)}) collective-permute-start(bf16[768,768]{1,0:T(8,128)(2,1)S(1)} %get-tuple-element.13), channel_id=1, source_target_pairs={{0,1},{1,0},{2,3},{3,2},{4,5},{5,4},{6,7},{7,6},{8,9},{9,8},{10,11... | collective-permute-start | bytes 3538952 | tf_op jit(solution)/shard_map/ppermute | solution.py:226
  22.9 20.5 %collective-permute-done.2.refs_1_ = bf16[768,768]{1,0:T(8,128)(2,1)S(1)} collective-permute-done((bf16[768,768]{1,0:T(8,128)(2,1)S(1)}, bf16[768,768]{1,0:T(8,128)(2,1)S(1)}, u32[]{:S(2)}, u32[]{:S(2)}) %collective-permute-start.2) | collective-permute-done | bytes 1179680 | tf_op jit(solution)/shard_map/ppermute | solution.py:226
  46.6 1.6 %collective-permute-start.9 = (bf16[512,768]{1,0:T(8,128)(2,1)}, bf16[512,768]{1,0:T(8,128)(2,1)}, u32[]{:S(2)}, u32[]{:S(2)}) collective-permute-start(bf16[512,768]{1,0:T(8,128)(2,1)} %slice.48), channel_id=1, source_target_pairs={{1,2},{2,1},{5,6},{6,5},{9,10},{10,9},{13,14},{14,13},{17,18},{18,... | collective-permute-start | bytes 2359304 | tf_op jit(solution)/shard_map/ppermute | solution.py:229
  50.9 5.6 %collective-permute-done.10.refs_5_ = bf16[256,768]{1,0:T(8,128)(2,1)S(1)} collective-permute-done((bf16[256,768]{1,0:T(8,128)(2,1)S(1)}, bf16[256,768]{1,0:T(8,128)(2,1)S(1)}, u32[]{:S(2)}, u32[]{:S(2)}) %collective-permute-start.10) | collective-permute-done | bytes 393248 | tf_op jit(solution)/shard_map/ppermute | solution.py:239
  57.3 8.5 %collective-permute-done.12.refs_7_ = bf16[256,768]{1,0:T(8,128)(2,1)S(1)} collective-permute-done((bf16[256,768]{1,0:T(8,128)(2,1)S(1)}, bf16[256,768]{1,0:T(8,128)(2,1)S(1)}, u32[]{:S(2)}, u32[]{:S(2)}) %collective-permute-start.12) | collective-permute-done | bytes 393248 | tf_op jit(solution)/shard_map/ppermute | solution.py:239
  66.5 1.3 %collective-permute-done.5.refs_2_ = bf16[768,768]{1,0:T(8,128)(2,1)} collective-permute-done((bf16[768,768]{1,0:T(8,128)(2,1)S(1)}, bf16[768,768]{1,0:T(8,128)(2,1)}, u32[]{:S(2)}, u32[]{:S(2)}) %collective-permute-start.5) | collective-permute-done | bytes 1179680 | tf_op jit(solution)/shard_map/ppermute | solution.py:232
  69.2 1.8 %slice_select_fusion.refs_8_ = bf16[256,768]{1,0:T(8,128)(2,1)} fusion(bf16[768,768]{1,0:T(8,128)(2,1)S(1)} %collective-permute-done.4.refs_3_, bf16[768,768]{1,0:T(8,128)(2,1)} %collective-permute-done.5.refs_2_, pred[]{:T(512)S(6)} %or.3), kind=kLoop, calls=%fused_computation.4 | loop fusion | flops 196608 | bytes 1179649 | tf_op jit(solution)/shard_map/jit(_where)/select_n | solution.py:258
  73.6 3.7 %copy-done = bf16[6144,3,256]{2,0,1:T(8,128)(2,1)S(1)} copy-done((bf16[6144,3,256]{2,0,1:T(8,128)(2,1)S(1)}, bf16[6144,3,256]{2,0,1:T(8,128)(2,1)}, u32[]{:S(2)}) %copy-start) | copy-done | bytes 9437208
  79.7 3.5 %project_qkv.2 = bf16[192,768]{1,0:T(8,128)(2,1)S(1)} custom-call(s32[1]{0:T(128)} %bitcast.1.outer_ref, bf16[512,768]{1,0:T(8,128)(2,1)S(1)} %bitcast.12, bf16[768,768]{1,0:T(8,128)(2,1)S(1)} %collective-permute-done.2.refs_1_, bf16[768,768]{1,0:T(8,128)(2,1)} %collective-permute-done.5.refs_2_, bf16[768,768]{1,0:T(8,128)(2,1)S(1)} %copy-done.6, ...), custom_call_target="tpu_custom_call" | custom-call | flops 1811939328 | bytes 11796480 | tf_op jit(solution)/shard_map/project_qkv/pallas_call | solution.py:149
  83.2 3.3 %collective-permute-done.13.refs_0_ = bf16[512,768]{1,0:T(8,128)(2,1)} collective-permute-done((bf16[512,768]{1,0:T(8,128)(2,1)}, bf16[512,768]{1,0:T(8,128)(2,1)}, u32[]{:S(2)}, u32[]{:S(2)}) %collective-permute-start.13) | collective-permute-done | bytes 786464 | tf_op jit(solution)/shard_map/ppermute | solution.py:232
  86.6 3.3 %project_qkv.3 = bf16[64,768]{1,0:T(8,128)(2,1)S(1)} custom-call(s32[1]{0:T(128)} %bitcast.1.outer_ref, bf16[512,768]{1,0:T(8,128)(2,1)} %collective-permute-done.13.refs_0_, bf16[512,768]{1,0:T(8,128)(2,1)} %collective-permute-done.9.refs_1_, bf16[3,6144,256]{2,1,0:T(8,128)(2,1)S(1)} %bitcast.10), custom_call_target="tpu_custom_call" | custom-call | flops 603979776 | bytes 10223616 | tf_op jit(solution)/shard_map/project_qkv/pallas_call | solution.py:149
  89.9 1.6 %collective-permute-start.17 = (bf16[256,512]{1,0:T(8,128)(2,1)S(1)}, bf16[256,512]{1,0:T(8,128)(2,1)S(1)}, u32[]{:S(2)}, u32[]{:S(2)}) collective-permute-start(bf16[256,512]{1,0:T(8,128)(2,1)S(1)} %pad_maximum_fusion.2.refs_0_), channel_id=1, source_target_pairs={{0,4},{4,8},{8,12},{1,5},{5,9},{9,13},{2,6},{6,10},{10,14},{3,7},{... | collective-permute-start | bytes 786440 | tf_op jit(solution)/shard_map/ppermute | solution.py:17
  94.3 3.1 %collective-permute-done.17.refs_1_ = bf16[256,512]{1,0:T(8,128)(2,1)S(1)} collective-permute-done((bf16[256,512]{1,0:T(8,128)(2,1)S(1)}, bf16[256,512]{1,0:T(8,128)(2,1)S(1)}, u32[]{:S(2)}, u32[]{:S(2)}) %collective-permute-start.17) | collective-permute-done | bytes 262176 | tf_op jit(solution)/shard_map/ppermute | solution.py:17
  97.4 9.9 %collective-permute-done.18.refs_2_ = bf16[256,512]{1,0:T(8,128)(2,1)S(1)} collective-permute-done((bf16[256,512]{1,0:T(8,128)(2,1)S(1)}, bf16[256,512]{1,0:T(8,128)(2,1)S(1)}, u32[]{:S(2)}, u32[]{:S(2)}) %collective-permute-start.18) | collective-permute-done | bytes 262176 | tf_op jit(solution)/shard_map/ppermute | solution.py:17
  107.3 2.6 %collective-permute-done.19.refs_3_ = bf16[256,512]{1,0:T(8,128)(2,1)S(1)} collective-permute-done((bf16[256,512]{1,0:T(8,128)(2,1)S(1)}, bf16[256,512]{1,0:T(8,128)(2,1)S(1)}, u32[]{:S(2)}, u32[]{:S(2)}) %collective-permute-start.19) | collective-permute-done | bytes 262176 | tf_op jit(solution)/shard_map/ppermute | solution.py:17
  109.9 1.7 %attend.1 = bf16[256,256]{1,0:T(8,128)(2,1)S(1)} custom-call(bf16[256,256]{1,0:T(8,128)(2,1)S(1)} %pad_maximum_fusion.4.q_ref, bf16[256,512]{1,0:T(8,128)(2,1)S(1)} %pad_maximum_fusion.2.refs_0_, bf16[256,512]{1,0:T(8,128)(2,1)S(1)} %collective-permute-done.17.refs_1_, bf16[256,512]{1,0:T(8,128)(2,1)S(1)} %collective-permute-done.18.refs_2_, ...), custom_call_target="tpu_custom_call" | custom-call | flops 134217728 | bytes 786432 | tf_op jit(solution)/shard_map/attend/pallas_call | solution.py:60
  111.6 1.3 %collective-permute-start.21 = (bf16[64,256]{1,0:T(8,128)(2,1)S(1)}, bf16[64,256]{1,0:T(8,128)(2,1)S(1)}, u32[]{:S(2)}, u32[]{:S(2)}) collective-permute-start(bf16[64,256]{1,0:T(8,128)(2,1)S(1)} %get-tuple-element.22), channel_id=1, source_target_pairs={{0,2},{1,3},{2,0},{3,1},{4,6},{5,7},{6,4},{7,5},{8,10},{9,11},{10,... | collective-permute-start | bytes 98312 | tf_op jit(solution)/shard_map/ppermute | solution.py:275
  112.9 2.0 %collective-permute-start.22 = (bf16[64,256]{1,0:T(8,128)(2,1)S(1)}, bf16[64,256]{1,0:T(8,128)(2,1)S(1)}, u32[]{:S(2)}, u32[]{:S(2)}) collective-permute-start(bf16[64,256]{1,0:T(8,128)(2,1)S(1)} %get-tuple-element.23), channel_id=1, source_target_pairs={{0,3},{1,2},{2,1},{3,0},{4,7},{5,6},{6,5},{7,4},{8,11},{9,10},{10,... | collective-permute-start | bytes 98312 | tf_op jit(solution)/shard_map/ppermute | solution.py:275
  115.3 2.2 %collective-permute-done.22 = bf16[64,256]{1,0:T(8,128)(2,1)S(1)} collective-permute-done((bf16[64,256]{1,0:T(8,128)(2,1)S(1)}, bf16[64,256]{1,0:T(8,128)(2,1)S(1)}, u32[]{:S(2)}, u32[]{:S(2)}) %collective-permute-start.22) | collective-permute-done | bytes 32800 | tf_op jit(solution)/shard_map/ppermute | solution.py:275
  119.4 2.2 %project_out.1 = bf16[128,3072]{1,0:T(8,128)(2,1)S(1)} custom-call(s32[1]{0:T(128)} %bitcast.place_ref, bf16[128,1024]{1,0:T(8,128)(2,1)S(1)} %pad_maximum_fusion.3.att_ref, f32[2,6144]{1,0:T(2,128)S(1)} %copy-done.22, bf16[256,6144]{1,0:T(8,128)(2,1)S(1)} %copy-done.2, bf16[256,768]{1,0:T(8,128)(2,1)S(1)} %copy-done.8, bf16[256,768]{1,0:T(8,128)(2,1)S(1)} %copy-done.11, ...), custom_call_target="tpu_custom_call" | custom-call | flops 805306368 | bytes 6291456 | tf_op jit(solution)/shard_map/project_out/pallas_call | solution.py:192
  121.8 1.6 %collective-permute-done.24 = bf16[64,3072]{1,0:T(8,128)(2,1)S(1)} collective-permute-done((bf16[64,3072]{1,0:T(8,128)(2,1)S(1)}, bf16[64,3072]{1,0:T(8,128)(2,1)S(1)}, u32[]{:S(2)}, u32[]{:S(2)}) %collective-permute-start.24) | collective-permute-done | bytes 393248 | tf_op jit(solution)/shard_map/ppermute | solution.py:235
  (98 shorter events, 29.2 us)
Async XLA Ops:
  1.1 8.5 %collective-permute-start = (bf16[256,768]{1,0:T(8,128)(2,1)S(1)}, bf16[256,768]{1,0:T(8,128)(2,1)S(1)}, u32[]{:S(2)}, u32[]{:S(2)}) collective-permute-start(bf16[256,768]{1,0:T(8,128)(2,1)S(1)} %constant_dynamic-slice_fusion), channel_id=1, source_target_pairs={{1,2},{2,1},{5,6},{6,5},{9,10},{10,9},{13,14},{14,13},{17,18},{18,... | collective-permute-start | bytes 1179656 | tf_op jit(solution)/shard_map/ppermute | solution.py:229
  1.8 12.4 %collective-permute-start.3 = (bf16[256,768]{1,0:T(8,128)(2,1)S(1)}, bf16[256,768]{1,0:T(8,128)(2,1)S(1)}, u32[]{:S(2)}, u32[]{:S(2)}) collective-permute-start(bf16[256,768]{1,0:T(8,128)(2,1)S(1)} %constant_dynamic-slice_fusion), channel_id=1, source_target_pairs={{0,1},{1,0},{2,3},{3,2},{4,5},{5,4},{6,7},{7,6},{8,9},{9,8},{10,11... | collective-permute-start | bytes 1179656 | tf_op jit(solution)/shard_map/ppermute | solution.py:226
  8.3 6.9 %collective-permute-start.1 = (f32[1,6144]{1,0:T(1,128)S(1)}, f32[1,6144]{1,0:T(1,128)S(1)}, u32[]{:S(2)}, u32[]{:S(2)}) collective-permute-start(f32[1,6144]{1,0:T(1,128)S(1)} %get-tuple-element.12), channel_id=1, source_target_pairs={{0,4},{4,0},{8,12},{12,8},{16,20},{20,16},{24,28},{28,24},{1,5},{5... | collective-permute-start | bytes 73736 | tf_op jit(solution)/shard_map/ppermute | solution.py:235
  14.4 7.2 %collective-permute-start.4 = (bf16[768,768]{1,0:T(8,128)(2,1)S(1)}, bf16[768,768]{1,0:T(8,128)(2,1)S(1)}, u32[]{:S(2)}, u32[]{:S(2)}) collective-permute-start(bf16[768,768]{1,0:T(8,128)(2,1)S(1)} %get-tuple-element.19), channel_id=1, source_target_pairs={{1,2},{2,1},{5,6},{6,5},{9,10},{10,9},{13,14},{14,13},{17,18},{18,... | collective-permute-start | bytes 3538952 | tf_op jit(solution)/shard_map/ppermute | solution.py:229
  15.8 27.6 %collective-permute-start.2 = (bf16[768,768]{1,0:T(8,128)(2,1)S(1)}, bf16[768,768]{1,0:T(8,128)(2,1)S(1)}, u32[]{:S(2)}, u32[]{:S(2)}) collective-permute-start(bf16[768,768]{1,0:T(8,128)(2,1)S(1)} %get-tuple-element.13), channel_id=1, source_target_pairs={{0,1},{1,0},{2,3},{3,2},{4,5},{5,4},{6,7},{7,6},{8,9},{9,8},{10,11... | collective-permute-start | bytes 3538952 | tf_op jit(solution)/shard_map/ppermute | solution.py:226
  18.9 25.4 %collective-permute-start.6 = (bf16[256,768]{1,0:T(8,128)(2,1)S(1)}, bf16[256,768]{1,0:T(8,128)(2,1)S(1)}, u32[]{:S(2)}, u32[]{:S(2)}) collective-permute-start(bf16[256,768]{1,0:T(8,128)(2,1)S(1)} %collective-permute-done.3.refs_0_), channel_id=1, source_target_pairs={{0,8},{4,12},{8,0},{12,4},{16,24},{20,28},{24,16},{28,20},{1,9},{5... | collective-permute-start | bytes 1179656 | tf_op jit(solution)/shard_map/ppermute | solution.py:239
  19.2 25.9 %collective-permute-start.7 = (bf16[256,768]{1,0:T(8,128)(2,1)S(1)}, bf16[256,768]{1,0:T(8,128)(2,1)S(1)}, u32[]{:S(2)}, u32[]{:S(2)}) collective-permute-start(bf16[256,768]{1,0:T(8,128)(2,1)S(1)} %collective-permute-done.3.refs_0_), channel_id=1, source_target_pairs={{0,16},{4,20},{8,24},{12,28},{16,0},{20,4},{24,8},{28,12},{1,17},{... | collective-permute-start | bytes 1179656 | tf_op jit(solution)/shard_map/ppermute | solution.py:239
  20.4 25.4 %collective-permute-start.8 = (bf16[256,768]{1,0:T(8,128)(2,1)S(1)}, bf16[256,768]{1,0:T(8,128)(2,1)S(1)}, u32[]{:S(2)}, u32[]{:S(2)}) collective-permute-start(bf16[256,768]{1,0:T(8,128)(2,1)S(1)} %collective-permute-done.3.refs_0_), channel_id=1, source_target_pairs={{0,24},{4,28},{8,16},{12,20},{16,8},{20,12},{24,0},{28,4},{1,25},{... | collective-permute-start | bytes 1179656 | tf_op jit(solution)/shard_map/ppermute | solution.py:239
  21.6 46.3 %collective-permute-start.5 = (bf16[768,768]{1,0:T(8,128)(2,1)S(1)}, bf16[768,768]{1,0:T(8,128)(2,1)}, u32[]{:S(2)}, u32[]{:S(2)}) collective-permute-start(bf16[768,768]{1,0:T(8,128)(2,1)S(1)} %collective-permute-done.4.refs_3_), channel_id=1, source_target_pairs={{1,0},{2,3},{5,4},{6,7},{9,8},{10,11},{13,12},{14,15},{17,16},{18,... | collective-permute-start | bytes 3538952 | tf_op jit(solution)/shard_map/ppermute | solution.py:232
  46.6 20.0 %collective-permute-start.9 = (bf16[512,768]{1,0:T(8,128)(2,1)}, bf16[512,768]{1,0:T(8,128)(2,1)}, u32[]{:S(2)}, u32[]{:S(2)}) collective-permute-start(bf16[512,768]{1,0:T(8,128)(2,1)} %slice.48), channel_id=1, source_target_pairs={{1,2},{2,1},{5,6},{6,5},{9,10},{10,9},{13,14},{14,13},{17,18},{18,... | collective-permute-start | bytes 2359304 | tf_op jit(solution)/shard_map/ppermute | solution.py:229
  48.2 8.3 %collective-permute-start.10 = (bf16[256,768]{1,0:T(8,128)(2,1)S(1)}, bf16[256,768]{1,0:T(8,128)(2,1)S(1)}, u32[]{:S(2)}, u32[]{:S(2)}) collective-permute-start(bf16[256,768]{1,0:T(8,128)(2,1)S(1)} %slice_select_fusion.1.refs_4_), channel_id=1, source_target_pairs={{0,8},{4,12},{8,0},{12,4},{16,24},{20,28},{24,16},{28,20},{1,9},{5... | collective-permute-start | bytes 1179656 | tf_op jit(solution)/shard_map/ppermute | solution.py:239
  48.5 8.0 %collective-permute-start.11 = (bf16[256,768]{1,0:T(8,128)(2,1)S(1)}, bf16[256,768]{1,0:T(8,128)(2,1)S(1)}, u32[]{:S(2)}, u32[]{:S(2)}) collective-permute-start(bf16[256,768]{1,0:T(8,128)(2,1)S(1)} %slice_select_fusion.1.refs_4_), channel_id=1, source_target_pairs={{0,16},{4,20},{8,24},{12,28},{16,0},{20,4},{24,8},{28,12},{1,17},{... | collective-permute-start | bytes 1179656 | tf_op jit(solution)/shard_map/ppermute | solution.py:239
  49.7 16.0 %collective-permute-start.12 = (bf16[256,768]{1,0:T(8,128)(2,1)S(1)}, bf16[256,768]{1,0:T(8,128)(2,1)S(1)}, u32[]{:S(2)}, u32[]{:S(2)}) collective-permute-start(bf16[256,768]{1,0:T(8,128)(2,1)S(1)} %slice_select_fusion.1.refs_4_), channel_id=1, source_target_pairs={{0,24},{4,28},{8,16},{12,20},{16,8},{20,12},{24,0},{28,4},{1,25},{... | collective-permute-start | bytes 1179656 | tf_op jit(solution)/shard_map/ppermute | solution.py:239
  67.9 18.6 %collective-permute-start.13 = (bf16[512,768]{1,0:T(8,128)(2,1)}, bf16[512,768]{1,0:T(8,128)(2,1)}, u32[]{:S(2)}, u32[]{:S(2)}) collective-permute-start(bf16[512,768]{1,0:T(8,128)(2,1)} %collective-permute-done.9.refs_1_), channel_id=1, source_target_pairs={{1,0},{2,3},{5,4},{6,7},{9,8},{10,11},{13,12},{14,15},{17,16},{18,... | collective-permute-start | bytes 2359304 | tf_op jit(solution)/shard_map/ppermute | solution.py:232
  71.0 21.8 %collective-permute-start.14 = (bf16[256,768]{1,0:T(8,128)(2,1)}, bf16[256,768]{1,0:T(8,128)(2,1)}, u32[]{:S(2)}, u32[]{:S(2)}) collective-permute-start(bf16[256,768]{1,0:T(8,128)(2,1)} %slice_select_fusion.refs_8_), channel_id=1, source_target_pairs={{0,8},{4,12},{8,0},{12,4},{16,24},{20,28},{24,16},{28,20},{1,9},{5... | collective-permute-start | bytes 1179656 | tf_op jit(solution)/shard_map/ppermute | solution.py:239
  71.2 23.1 %collective-permute-start.15 = (bf16[256,768]{1,0:T(8,128)(2,1)}, bf16[256,768]{1,0:T(8,128)(2,1)S(1)}, u32[]{:S(2)}, u32[]{:S(2)}) collective-permute-start(bf16[256,768]{1,0:T(8,128)(2,1)} %slice_select_fusion.refs_8_), channel_id=1, source_target_pairs={{0,16},{4,20},{8,24},{12,28},{16,0},{20,4},{24,8},{28,12},{1,17},{... | collective-permute-start | bytes 1179656 | tf_op jit(solution)/shard_map/ppermute | solution.py:239
  72.4 21.9 %collective-permute-start.16 = (bf16[256,768]{1,0:T(8,128)(2,1)}, bf16[256,768]{1,0:T(8,128)(2,1)S(1)}, u32[]{:S(2)}, u32[]{:S(2)}) collective-permute-start(bf16[256,768]{1,0:T(8,128)(2,1)} %slice_select_fusion.refs_8_), channel_id=1, source_target_pairs={{0,24},{4,28},{8,16},{12,20},{16,8},{20,12},{24,0},{28,4},{1,25},{... | collective-permute-start | bytes 1179656 | tf_op jit(solution)/shard_map/ppermute | solution.py:239
  89.9 7.5 %collective-permute-start.17 = (bf16[256,512]{1,0:T(8,128)(2,1)S(1)}, bf16[256,512]{1,0:T(8,128)(2,1)S(1)}, u32[]{:S(2)}, u32[]{:S(2)}) collective-permute-start(bf16[256,512]{1,0:T(8,128)(2,1)S(1)} %pad_maximum_fusion.2.refs_0_), channel_id=1, source_target_pairs={{0,4},{4,8},{8,12},{1,5},{5,9},{9,13},{2,6},{6,10},{10,14},{3,7},{... | collective-permute-start | bytes 786440 | tf_op jit(solution)/shard_map/ppermute | solution.py:17
  91.5 15.9 %collective-permute-start.18 = (bf16[256,512]{1,0:T(8,128)(2,1)S(1)}, bf16[256,512]{1,0:T(8,128)(2,1)S(1)}, u32[]{:S(2)}, u32[]{:S(2)}) collective-permute-start(bf16[256,512]{1,0:T(8,128)(2,1)S(1)} %pad_maximum_fusion.2.refs_0_), channel_id=1, source_target_pairs={{0,8},{4,12},{1,9},{5,13},{2,10},{6,14},{3,11},{7,15},{16,24},{20,... | collective-permute-start | bytes 786440 | tf_op jit(solution)/shard_map/ppermute | solution.py:17
  92.8 17.1 %collective-permute-start.19 = (bf16[256,512]{1,0:T(8,128)(2,1)S(1)}, bf16[256,512]{1,0:T(8,128)(2,1)S(1)}, u32[]{:S(2)}, u32[]{:S(2)}) collective-permute-start(bf16[256,512]{1,0:T(8,128)(2,1)S(1)} %pad_maximum_fusion.2.refs_0_), channel_id=1, source_target_pairs={{0,12},{1,13},{2,14},{3,15},{16,28},{17,29},{18,30},{19,31}} | collective-permute-start | bytes 786440 | tf_op jit(solution)/shard_map/ppermute | solution.py:17
  111.6 3.7 %collective-permute-start.21 = (bf16[64,256]{1,0:T(8,128)(2,1)S(1)}, bf16[64,256]{1,0:T(8,128)(2,1)S(1)}, u32[]{:S(2)}, u32[]{:S(2)}) collective-permute-start(bf16[64,256]{1,0:T(8,128)(2,1)S(1)} %get-tuple-element.22), channel_id=1, source_target_pairs={{0,2},{1,3},{2,0},{3,1},{4,6},{5,7},{6,4},{7,5},{8,10},{9,11},{10,... | collective-permute-start | bytes 98312 | tf_op jit(solution)/shard_map/ppermute | solution.py:275
  112.9 4.6 %collective-permute-start.22 = (bf16[64,256]{1,0:T(8,128)(2,1)S(1)}, bf16[64,256]{1,0:T(8,128)(2,1)S(1)}, u32[]{:S(2)}, u32[]{:S(2)}) collective-permute-start(bf16[64,256]{1,0:T(8,128)(2,1)S(1)} %get-tuple-element.23), channel_id=1, source_target_pairs={{0,3},{1,2},{2,1},{3,0},{4,7},{5,6},{6,5},{7,4},{8,11},{9,10},{10,... | collective-permute-start | bytes 98312 | tf_op jit(solution)/shard_map/ppermute | solution.py:275
  114.9 2.9 %collective-permute-start.20 = (bf16[64,256]{1,0:T(8,128)(2,1)S(1)}, bf16[64,256]{1,0:T(8,128)(2,1)S(1)}, u32[]{:S(2)}, u32[]{:S(2)}) collective-permute-start(bf16[64,256]{1,0:T(8,128)(2,1)S(1)} %get-tuple-element.24), channel_id=1, source_target_pairs={{0,1},{1,0},{2,3},{3,2},{4,5},{5,4},{6,7},{7,6},{8,9},{9,8},{10,11... | collective-permute-start | bytes 98312 | tf_op jit(solution)/shard_map/ppermute | solution.py:275
  121.6 1.8 %collective-permute-start.24 = (bf16[64,3072]{1,0:T(8,128)(2,1)S(1)}, bf16[64,3072]{1,0:T(8,128)(2,1)S(1)}, u32[]{:S(2)}, u32[]{:S(2)}) collective-permute-start(bf16[64,3072]{1,0:T(8,128)(2,1)S(1)} %get-tuple-element.18), channel_id=1, source_target_pairs={{0,4},{4,0},{8,12},{12,8},{16,20},{20,16},{24,28},{28,24},{1,5},{5... | collective-permute-start | bytes 1179656 | tf_op jit(solution)/shard_map/ppermute | solution.py:235
  (26 other events, 405.9 us)

commit v3 on v2

--- a/solution.py
+++ b/solution.py
@@ -196,8 +196,8 @@
         out_specs=vmem,
         compiler_params=pltpu.CompilerParams(vmem_limit_bytes=40 << 20),
         cost_estimate=pl.CostEstimate(
-            flops=2 * rows * att.shape[1] * width,
-            bytes_accessed=2 * att.shape[1] * width,
+            flops=16 * rows * att.shape[1] * width,
+            bytes_accessed=2 * rows * width,
             transcendentals=0,
         ),
         name="project_out",
@@ -261,13 +261,24 @@
     early = project_qkv(outer_flag, [[own], [first], [out, mid]], w3, rows)
     late = project_qkv(outer_flag, [[far_out, far_mid]], w3, rows)
     qkv = jnp.concatenate([early, late], axis=0)
-    kv_own = qkv[:, cols:]
-    kv = [kv_own] + [from_behind(kv_own, "tract", d) for d in range(1, n_tract)]
-    offsets = tract - lax.iota(jnp.int32, n_tract)
+    kv_own = after(qkv[:, cols:], *w_third_pieces)
+    kv_chip = from_behind(kv_own, "tract", 2)
+    kv_core = lax.ppermute(kv_own, "tract", [(0, 1), (2, 3)])
+    kv_both = lax.ppermute(kv_chip, "tract", [(2, 3), (3, 2)])
+    sources = jnp.stack(
+        [
+            tract,
+            jnp.where(tract % 2 == 1, tract - 1, -1),
+            tract - 2,
+            jnp.where(tract > 1, 3 - tract, -1),
+        ]
+    )
     seen = jnp.sum(
-        jnp.where(offsets[:, None] == lax.iota(jnp.int32, n_tract)[None, :], visible, 0), axis=1
-    )
-    attended = attend(after(qkv[:, :cols], *w_third_pieces), kv, seen)
+        jnp.where(sources[:, None] == lax.iota(jnp.int32, n_tract)[None, :], visible, 0), axis=1
+    )
+    attended = attend(
+        qkv[:, :cols], [kv_own, kv_core, kv_chip, kv_both], seen
+    )
 
     blocks = [attended[i * rows : (i + 1) * rows] for i in range(4)]
     leaving = [blocks[1], jnp.where(outer, blocks[2], blocks[3]), jnp.where(outer, blocks[3], blocks[2])]

time: 127 us -> 126 us (level); the launches traced: 124 us -> 125 us
  waiting for transfers between devices: 65.3 us -> 54.7 us
  starting transfers between devices: 29.6 us -> 38.6 us
  local copies, waits for them, and re-layouts: 13.5 us -> 16.4 us
    ppermute x3 -> x1, waiting for transfers between devices: 15.6 us -> 4.36 us  [from_behind(): return lax.ppermute(value, axis, pairs)]
    ppermute x0 -> x2, starting transfers between devices: none -> 8.82 us  [the longest x1 7.4 us: gather_body(): kv_both = lax.ppermute(kv_chip, 'tract', [(2, 3), (3, 2)])]
    unnamed x51 -> x55, local copies, waits for them, and re-layouts: 11.4 us -> 14.3 us
    ppermute x3 -> x1, starting transfers between devices: 4.14 us -> 1.42 us  [from_behind(): return lax.ppermute(value, axis, pairs)]
    ppermute x3, starting transfers between devices: 1.59 us -> 3.6 us  [swap(): return lax.ppermute(value, PLANE, [(i, i ^ 1) for i in range(plane)])]
  transfers between devices with their start and end apart: 25 -> 25, of which waited for: 14 -> 12; matrix products, arithmetic and copies ran while one was open for 4% -> 4% of each run, Pallas kernels for 6% -> 6%
where the time goes in v3:
time: 126 us; the launch traced here: 125 us
  waiting for transfers between devices  54.7 us (43%)
  starting transfers between devices  38.6 us (31%)
  local copies, waits for them, and re-layouts  16.4 us (13%)
  Pallas kernels  11 us (9%)
  other arithmetic  3.43 us (3%)
    ppermute x2, waiting for transfers between devices, pair(): return lax.ppermute(value, 'head', [(0, 1), (1, 0), (2, 3), (3, 2)])  25.1 us
    unnamed x55, local copies, waits for them, and re-layouts  14.3 us
    ppermute x9, waiting for transfers between devices, across_plane(): lax.ppermute(piece, PLANE, [(i, i ^ delta) for i in range(plane)])  14.1 us
    ppermute x9, starting transfers between devices, across_plane(): lax.ppermute(piece, PLANE, [(i, i ^ delta) for i in range(plane)])  8.01 us
    ppermute x1, starting transfers between devices, gather_body(): kv_both = lax.ppermute(kv_chip, 'tract', [(2, 3), (3, 2)])  7.4 us
    ppermute x2, starting transfers between devices, pair(): return lax.ppermute(value, 'head', [(0, 1), (1, 0), (2, 3), (3, 2)])  7.08 us
    pallas_call x2, Pallas kernels, project_qkv(): pl.pallas_call(functools.partial(qkv_kernel, [len(group) for group in gro...  6.53 us
    ppermute x2, waiting for transfers between devices, outward(): return lax.ppermute(value, 'head', [(1, 0), (2, 3)])  4.42 us
  transfers between devices with their start and end apart: 25, of which 12 were waited for; matrix products, arithmetic and copies ran while one was open for 4% of the time, Pallas kernels for 6%

profile of v3, /device:TPU:3, one launch (start us, length us, event | category | flops | bytes accessed | tf_op | source)
XLA Modules:
  0.0 125.3 jit_solution(9882174832841928070)
XLA Ops:
  1.8 3.9 %collective-permute-start.3 = (bf16[256,768]{1,0:T(8,128)(2,1)S(1)}, bf16[256,768]{1,0:T(8,128)(2,1)S(1)}, u32[]{:S(2)}, u32[]{:S(2)}) collective-permute-start(bf16[256,768]{1,0:T(8,128)(2,1)S(1)} %constant_dynamic-slice_fusion), channel_id=1, source_target_pairs={{0,1},{1,0},{2,3},{3,2},{4,5},{5,4},{6,7},{7,6},{8,9},{9,8},{10,11... | collective-permute-start | bytes 1179656 | tf_op jit(solution)/shard_map/ppermute | solution.py:226
  5.7 1.5 %copy.8.style_ref = f32[8,3,6144]{2,1,0:T(4,128)S(1)} copy(f32[8,3,6144]{2,0,1:T(8,128)} %param.11) | data formatting | bytes 1179648 | tf_op args[5]
  9.6 4.6 %collective-permute-done.3.refs_0_ = bf16[256,768]{1,0:T(8,128)(2,1)S(1)} collective-permute-done((bf16[256,768]{1,0:T(8,128)(2,1)S(1)}, bf16[256,768]{1,0:T(8,128)(2,1)S(1)}, u32[]{:S(2)}, u32[]{:S(2)}) %collective-permute-start.3) | collective-permute-done | bytes 393248 | tf_op jit(solution)/shard_map/ppermute | solution.py:226
  15.3 3.2 %collective-permute-start.2 = (bf16[768,768]{1,0:T(8,128)(2,1)S(1)}, bf16[768,768]{1,0:T(8,128)(2,1)S(1)}, u32[]{:S(2)}, u32[]{:S(2)}) collective-permute-start(bf16[768,768]{1,0:T(8,128)(2,1)S(1)} %get-tuple-element.13), channel_id=1, source_target_pairs={{0,1},{1,0},{2,3},{3,2},{4,5},{5,4},{6,7},{7,6},{8,9},{9,8},{10,11... | collective-permute-start | bytes 3538952 | tf_op jit(solution)/shard_map/ppermute | solution.py:226
  22.5 20.5 %collective-permute-done.2.refs_1_ = bf16[768,768]{1,0:T(8,128)(2,1)S(1)} collective-permute-done((bf16[768,768]{1,0:T(8,128)(2,1)S(1)}, bf16[768,768]{1,0:T(8,128)(2,1)S(1)}, u32[]{:S(2)}, u32[]{:S(2)}) %collective-permute-start.2) | collective-permute-done | bytes 1179680 | tf_op jit(solution)/shard_map/ppermute | solution.py:226
  46.2 1.5 %collective-permute-start.9 = (bf16[512,768]{1,0:T(8,128)(2,1)}, bf16[512,768]{1,0:T(8,128)(2,1)}, u32[]{:S(2)}, u32[]{:S(2)}) collective-permute-start(bf16[512,768]{1,0:T(8,128)(2,1)} %slice.48), channel_id=1, source_target_pairs={{1,2},{2,1},{5,6},{6,5},{9,10},{10,9},{13,14},{14,13},{17,18},{18,... | collective-permute-start | bytes 2359304 | tf_op jit(solution)/shard_map/ppermute | solution.py:229
  50.5 5.6 %collective-permute-done.10.refs_5_ = bf16[256,768]{1,0:T(8,128)(2,1)S(1)} collective-permute-done((bf16[256,768]{1,0:T(8,128)(2,1)S(1)}, bf16[256,768]{1,0:T(8,128)(2,1)S(1)}, u32[]{:S(2)}, u32[]{:S(2)}) %collective-permute-start.10) | collective-permute-done | bytes 393248 | tf_op jit(solution)/shard_map/ppermute | solution.py:239
  56.9 8.5 %collective-permute-done.12.refs_7_ = bf16[256,768]{1,0:T(8,128)(2,1)S(1)} collective-permute-done((bf16[256,768]{1,0:T(8,128)(2,1)S(1)}, bf16[256,768]{1,0:T(8,128)(2,1)S(1)}, u32[]{:S(2)}, u32[]{:S(2)}) %collective-permute-start.12) | collective-permute-done | bytes 393248 | tf_op jit(solution)/shard_map/ppermute | solution.py:239
  66.1 1.9 %collective-permute-done.5.refs_2_ = bf16[768,768]{1,0:T(8,128)(2,1)} collective-permute-done((bf16[768,768]{1,0:T(8,128)(2,1)S(1)}, bf16[768,768]{1,0:T(8,128)(2,1)}, u32[]{:S(2)}, u32[]{:S(2)}) %collective-permute-start.5) | collective-permute-done | bytes 1179680 | tf_op jit(solution)/shard_map/ppermute | solution.py:232
  69.3 1.8 %slice_select_fusion.refs_8_ = bf16[256,768]{1,0:T(8,128)(2,1)} fusion(bf16[768,768]{1,0:T(8,128)(2,1)S(1)} %collective-permute-done.4.refs_3_, bf16[768,768]{1,0:T(8,128)(2,1)} %collective-permute-done.5.refs_2_, pred[]{:T(512)S(6)} %or.3), kind=kLoop, calls=%fused_computation.4 | loop fusion | flops 196608 | bytes 1179649 | tf_op jit(solution)/shard_map/jit(_where)/select_n | solution.py:258
  73.8 3.7 %copy-done = bf16[6144,3,256]{2,0,1:T(8,128)(2,1)S(1)} copy-done((bf16[6144,3,256]{2,0,1:T(8,128)(2,1)S(1)}, bf16[6144,3,256]{2,0,1:T(8,128)(2,1)}, u32[]{:S(2)}) %copy-start) | copy-done | bytes 9437208
  79.8 3.4 %project_qkv.2 = bf16[192,768]{1,0:T(8,128)(2,1)S(1)} custom-call(s32[1]{0:T(128)} %bitcast.1.outer_ref, bf16[512,768]{1,0:T(8,128)(2,1)S(1)} %bitcast.16, bf16[768,768]{1,0:T(8,128)(2,1)S(1)} %collective-permute-done.2.refs_1_, bf16[768,768]{1,0:T(8,128)(2,1)} %collective-permute-done.5.refs_2_, bf16[768,768]{1,0:T(8,128)(2,1)S(1)} %copy-done.5, ...), custom_call_target="tpu_custom_call" | custom-call | flops 1811939328 | bytes 11796480 | tf_op jit(solution)/shard_map/project_qkv/pallas_call | solution.py:149
  83.3 2.5 %collective-permute-done.13.refs_0_ = bf16[512,768]{1,0:T(8,128)(2,1)} collective-permute-done((bf16[512,768]{1,0:T(8,128)(2,1)}, bf16[512,768]{1,0:T(8,128)(2,1)}, u32[]{:S(2)}, u32[]{:S(2)}) %collective-permute-start.13) | collective-permute-done | bytes 786464 | tf_op jit(solution)/shard_map/ppermute | solution.py:232
  85.8 3.1 %project_qkv.3 = bf16[64,768]{1,0:T(8,128)(2,1)S(1)} custom-call(s32[1]{0:T(128)} %bitcast.1.outer_ref, bf16[512,768]{1,0:T(8,128)(2,1)} %collective-permute-done.13.refs_0_, bf16[512,768]{1,0:T(8,128)(2,1)} %collective-permute-done.9.refs_1_, bf16[3,6144,256]{2,1,0:T(8,128)(2,1)S(1)} %bitcast.14), custom_call_target="tpu_custom_call" | custom-call | flops 603979776 | bytes 10223616 | tf_op jit(solution)/shard_map/project_qkv/pallas_call | solution.py:149
  89.1 1.4 %collective-permute-start.18 = (bf16[256,512]{1,0:T(8,128)(2,1)S(1)}, bf16[256,512]{1,0:T(8,128)(2,1)S(1)}, u32[]{:S(2)}, u32[]{:S(2)}) collective-permute-start(bf16[256,512]{1,0:T(8,128)(2,1)S(1)} %pad_maximum_fusion.2.refs_0_), channel_id=1, source_target_pairs={{0,8},{4,12},{1,9},{5,13},{2,10},{6,14},{3,11},{7,15},{16,24},{20,... | collective-permute-start | bytes 786440 | tf_op jit(solution)/shard_map/ppermute | solution.py:17
  90.5 1.4 %collective-permute-start.17 = (bf16[256,512]{1,0:T(8,128)(2,1)S(1)}, bf16[256,512]{1,0:T(8,128)(2,1)S(1)}, u32[]{:S(2)}, u32[]{:S(2)}) collective-permute-start(bf16[256,512]{1,0:T(8,128)(2,1)S(1)} %pad_maximum_fusion.2.refs_0_), channel_id=1, source_target_pairs={{0,4},{8,12},{1,5},{9,13},{2,6},{10,14},{3,7},{11,15},{16,20},{24,... | collective-permute-start | bytes 786440 | tf_op jit(solution)/shard_map/ppermute | solution.py:266
  92.0 4.4 %collective-permute-done.18.refs_2_ = bf16[256,512]{1,0:T(8,128)(2,1)S(1)} collective-permute-done((bf16[256,512]{1,0:T(8,128)(2,1)S(1)}, bf16[256,512]{1,0:T(8,128)(2,1)S(1)}, u32[]{:S(2)}, u32[]{:S(2)}) %collective-permute-start.18) | collective-permute-done | bytes 262176 | tf_op jit(solution)/shard_map/ppermute | solution.py:17
  96.3 7.4 %collective-permute-start.19 = (bf16[256,512]{1,0:T(8,128)(2,1)S(1)}, bf16[256,512]{1,0:T(8,128)(2,1)S(1)}, u32[]{:S(2)}, u32[]{:S(2)}) collective-permute-start(bf16[256,512]{1,0:T(8,128)(2,1)S(1)} %collective-permute-done.18.refs_2_), channel_id=1, source_target_pairs={{8,12},{12,8},{9,13},{13,9},{10,14},{14,10},{11,15},{15,11},{24,28... | collective-permute-start | bytes 786440 | tf_op jit(solution)/shard_map/ppermute | solution.py:267
  104.9 1.6 %attend.1 = bf16[256,256]{1,0:T(8,128)(2,1)S(1)} custom-call(bf16[256,256]{1,0:T(8,128)(2,1)S(1)} %pad_maximum_fusion.4.q_ref, bf16[256,512]{1,0:T(8,128)(2,1)S(1)} %pad_maximum_fusion.2.refs_0_, bf16[256,512]{1,0:T(8,128)(2,1)S(1)} %collective-permute-done.17.refs_1_, bf16[256,512]{1,0:T(8,128)(2,1)S(1)} %collective-permute-done.18.refs_2_, ...), custom_call_target="tpu_custom_call" | custom-call | flops 134217728 | bytes 786432 | tf_op jit(solution)/shard_map/attend/pallas_call | solution.py:60
  106.5 3.0 %collective-permute-start.21 = (bf16[64,256]{1,0:T(8,128)(2,1)S(1)}, bf16[64,256]{1,0:T(8,128)(2,1)S(1)}, u32[]{:S(2)}, u32[]{:S(2)}) collective-permute-start(bf16[64,256]{1,0:T(8,128)(2,1)S(1)} %get-tuple-element.22), channel_id=1, source_target_pairs={{0,2},{1,3},{2,0},{3,1},{4,6},{5,7},{6,4},{7,5},{8,10},{9,11},{10,... | collective-permute-start | bytes 98312 | tf_op jit(solution)/shard_map/ppermute | solution.py:286
  110.8 3.3 %collective-permute-done.22 = bf16[64,256]{1,0:T(8,128)(2,1)S(1)} collective-permute-done((bf16[64,256]{1,0:T(8,128)(2,1)S(1)}, bf16[64,256]{1,0:T(8,128)(2,1)S(1)}, u32[]{:S(2)}, u32[]{:S(2)}) %collective-permute-start.22) | collective-permute-done | bytes 32800 | tf_op jit(solution)/shard_map/ppermute | solution.py:286
  114.1 1.9 %collective-permute-start.23 = (bf16[64,1024]{1,0:T(8,128)(2,1)S(1)}, bf16[64,1024]{1,0:T(8,128)(2,1)S(1)}, u32[]{:S(2)}, u32[]{:S(2)}) collective-permute-start(bf16[64,1024]{1,0:T(8,128)(2,1)S(1)} %pad_maximum_fusion.5), channel_id=1, source_target_pairs={{0,4},{4,0},{8,12},{12,8},{16,20},{20,16},{24,28},{28,24},{1,5},{5... | collective-permute-start | bytes 393224 | tf_op jit(solution)/shard_map/ppermute | solution.py:235
  117.1 1.9 %copy-done.11 = bf16[256,6144]{1,0:T(8,128)(2,1)S(1)} copy-done((bf16[256,6144]{1,0:T(8,128)(2,1)S(1)}, bf16[256,6144]{1,0:T(8,128)(2,1)}, u32[]{:S(2)}) %copy-start.11) | copy-done | bytes 3145752
  120.0 2.4 %project_out.1 = bf16[128,3072]{1,0:T(8,128)(2,1)S(1)} custom-call(s32[1]{0:T(128)} %bitcast.place_ref, bf16[128,1024]{1,0:T(8,128)(2,1)S(1)} %pad_maximum_fusion.3.att_ref, f32[2,6144]{1,0:T(2,128)S(1)} %pad_maximum_fusion.6.gate_ref, bf16[256,6144]{1,0:T(8,128)(2,1)S(1)} %copy-done.11, bf16[256,768]{1,0:T(8,128)(2,1)S(1)} %copy-done.10, ...), custom_call_target="tpu_custom_call" | custom-call | flops 6442450944 | bytes 786432 | tf_op jit(solution)/shard_map/project_out/pallas_call | solution.py:192
  (102 shorter events, 29.8 us)
Async XLA Ops:
  1.1 8.5 %collective-permute-start = (bf16[256,768]{1,0:T(8,128)(2,1)S(1)}, bf16[256,768]{1,0:T(8,128)(2,1)S(1)}, u32[]{:S(2)}, u32[]{:S(2)}) collective-permute-start(bf16[256,768]{1,0:T(8,128)(2,1)S(1)} %constant_dynamic-slice_fusion), channel_id=1, source_target_pairs={{1,2},{2,1},{5,6},{6,5},{9,10},{10,9},{13,14},{14,13},{17,18},{18,... | collective-permute-start | bytes 1179656 | tf_op jit(solution)/shard_map/ppermute | solution.py:229
  1.8 12.4 %collective-permute-start.3 = (bf16[256,768]{1,0:T(8,128)(2,1)S(1)}, bf16[256,768]{1,0:T(8,128)(2,1)S(1)}, u32[]{:S(2)}, u32[]{:S(2)}) collective-permute-start(bf16[256,768]{1,0:T(8,128)(2,1)S(1)} %constant_dynamic-slice_fusion), channel_id=1, source_target_pairs={{0,1},{1,0},{2,3},{3,2},{4,5},{5,4},{6,7},{7,6},{8,9},{9,8},{10,11... | collective-permute-start | bytes 1179656 | tf_op jit(solution)/shard_map/ppermute | solution.py:226
  8.3 7.0 %collective-permute-start.1 = (f32[1,6144]{1,0:T(1,128)S(1)}, f32[1,6144]{1,0:T(1,128)S(1)}, u32[]{:S(2)}, u32[]{:S(2)}) collective-permute-start(f32[1,6144]{1,0:T(1,128)S(1)} %get-tuple-element.12), channel_id=1, source_target_pairs={{0,4},{4,0},{8,12},{12,8},{16,20},{20,16},{24,28},{28,24},{1,5},{5... | collective-permute-start | bytes 73736 | tf_op jit(solution)/shard_map/ppermute | solution.py:235
  14.4 6.8 %collective-permute-start.4 = (bf16[768,768]{1,0:T(8,128)(2,1)S(1)}, bf16[768,768]{1,0:T(8,128)(2,1)S(1)}, u32[]{:S(2)}, u32[]{:S(2)}) collective-permute-start(bf16[768,768]{1,0:T(8,128)(2,1)S(1)} %get-tuple-element.19), channel_id=1, source_target_pairs={{1,2},{2,1},{5,6},{6,5},{9,10},{10,9},{13,14},{14,13},{17,18},{18,... | collective-permute-start | bytes 3538952 | tf_op jit(solution)/shard_map/ppermute | solution.py:229
  15.3 27.6 %collective-permute-start.2 = (bf16[768,768]{1,0:T(8,128)(2,1)S(1)}, bf16[768,768]{1,0:T(8,128)(2,1)S(1)}, u32[]{:S(2)}, u32[]{:S(2)}) collective-permute-start(bf16[768,768]{1,0:T(8,128)(2,1)S(1)} %get-tuple-element.13), channel_id=1, source_target_pairs={{0,1},{1,0},{2,3},{3,2},{4,5},{5,4},{6,7},{7,6},{8,9},{9,8},{10,11... | collective-permute-start | bytes 3538952 | tf_op jit(solution)/shard_map/ppermute | solution.py:226
  18.5 25.4 %collective-permute-start.6 = (bf16[256,768]{1,0:T(8,128)(2,1)S(1)}, bf16[256,768]{1,0:T(8,128)(2,1)S(1)}, u32[]{:S(2)}, u32[]{:S(2)}) collective-permute-start(bf16[256,768]{1,0:T(8,128)(2,1)S(1)} %collective-permute-done.3.refs_0_), channel_id=1, source_target_pairs={{0,8},{4,12},{8,0},{12,4},{16,24},{20,28},{24,16},{28,20},{1,9},{5... | collective-permute-start | bytes 1179656 | tf_op jit(solution)/shard_map/ppermute | solution.py:239
  18.8 25.9 %collective-permute-start.7 = (bf16[256,768]{1,0:T(8,128)(2,1)S(1)}, bf16[256,768]{1,0:T(8,128)(2,1)S(1)}, u32[]{:S(2)}, u32[]{:S(2)}) collective-permute-start(bf16[256,768]{1,0:T(8,128)(2,1)S(1)} %collective-permute-done.3.refs_0_), channel_id=1, source_target_pairs={{0,16},{4,20},{8,24},{12,28},{16,0},{20,4},{24,8},{28,12},{1,17},{... | collective-permute-start | bytes 1179656 | tf_op jit(solution)/shard_map/ppermute | solution.py:239
  20.0 25.4 %collective-permute-start.8 = (bf16[256,768]{1,0:T(8,128)(2,1)S(1)}, bf16[256,768]{1,0:T(8,128)(2,1)S(1)}, u32[]{:S(2)}, u32[]{:S(2)}) collective-permute-start(bf16[256,768]{1,0:T(8,128)(2,1)S(1)} %collective-permute-done.3.refs_0_), channel_id=1, source_target_pairs={{0,24},{4,28},{8,16},{12,20},{16,8},{20,12},{24,0},{28,4},{1,25},{... | collective-permute-start | bytes 1179656 | tf_op jit(solution)/shard_map/ppermute | solution.py:239
  21.2 46.8 %collective-permute-start.5 = (bf16[768,768]{1,0:T(8,128)(2,1)S(1)}, bf16[768,768]{1,0:T(8,128)(2,1)}, u32[]{:S(2)}, u32[]{:S(2)}) collective-permute-start(bf16[768,768]{1,0:T(8,128)(2,1)S(1)} %collective-permute-done.4.refs_3_), channel_id=1, source_target_pairs={{1,0},{2,3},{5,4},{6,7},{9,8},{10,11},{13,12},{14,15},{17,16},{18,... | collective-permute-start | bytes 3538952 | tf_op jit(solution)/shard_map/ppermute | solution.py:232
  46.2 20.0 %collective-permute-start.9 = (bf16[512,768]{1,0:T(8,128)(2,1)}, bf16[512,768]{1,0:T(8,128)(2,1)}, u32[]{:S(2)}, u32[]{:S(2)}) collective-permute-start(bf16[512,768]{1,0:T(8,128)(2,1)} %slice.48), channel_id=1, source_target_pairs={{1,2},{2,1},{5,6},{6,5},{9,10},{10,9},{13,14},{14,13},{17,18},{18,... | collective-permute-start | bytes 2359304 | tf_op jit(solution)/shard_map/ppermute | solution.py:229
  47.8 8.3 %collective-permute-start.10 = (bf16[256,768]{1,0:T(8,128)(2,1)S(1)}, bf16[256,768]{1,0:T(8,128)(2,1)S(1)}, u32[]{:S(2)}, u32[]{:S(2)}) collective-permute-start(bf16[256,768]{1,0:T(8,128)(2,1)S(1)} %slice_select_fusion.1.refs_4_), channel_id=1, source_target_pairs={{0,8},{4,12},{8,0},{12,4},{16,24},{20,28},{24,16},{28,20},{1,9},{5... | collective-permute-start | bytes 1179656 | tf_op jit(solution)/shard_map/ppermute | solution.py:239
  48.1 8.0 %collective-permute-start.11 = (bf16[256,768]{1,0:T(8,128)(2,1)S(1)}, bf16[256,768]{1,0:T(8,128)(2,1)S(1)}, u32[]{:S(2)}, u32[]{:S(2)}) collective-permute-start(bf16[256,768]{1,0:T(8,128)(2,1)S(1)} %slice_select_fusion.1.refs_4_), channel_id=1, source_target_pairs={{0,16},{4,20},{8,24},{12,28},{16,0},{20,4},{24,8},{28,12},{1,17},{... | collective-permute-start | bytes 1179656 | tf_op jit(solution)/shard_map/ppermute | solution.py:239
  49.3 16.0 %collective-permute-start.12 = (bf16[256,768]{1,0:T(8,128)(2,1)S(1)}, bf16[256,768]{1,0:T(8,128)(2,1)S(1)}, u32[]{:S(2)}, u32[]{:S(2)}) collective-permute-start(bf16[256,768]{1,0:T(8,128)(2,1)S(1)} %slice_select_fusion.1.refs_4_), channel_id=1, source_target_pairs={{0,24},{4,28},{8,16},{12,20},{16,8},{20,12},{24,0},{28,4},{1,25},{... | collective-permute-start | bytes 1179656 | tf_op jit(solution)/shard_map/ppermute | solution.py:239
  68.0 17.8 %collective-permute-start.13 = (bf16[512,768]{1,0:T(8,128)(2,1)}, bf16[512,768]{1,0:T(8,128)(2,1)}, u32[]{:S(2)}, u32[]{:S(2)}) collective-permute-start(bf16[512,768]{1,0:T(8,128)(2,1)} %collective-permute-done.9.refs_1_), channel_id=1, source_target_pairs={{1,0},{2,3},{5,4},{6,7},{9,8},{10,11},{13,12},{14,15},{17,16},{18,... | collective-permute-start | bytes 2359304 | tf_op jit(solution)/shard_map/ppermute | solution.py:232
  71.1 17.9 %collective-permute-start.14 = (bf16[256,768]{1,0:T(8,128)(2,1)}, bf16[256,768]{1,0:T(8,128)(2,1)}, u32[]{:S(2)}, u32[]{:S(2)}) collective-permute-start(bf16[256,768]{1,0:T(8,128)(2,1)} %slice_select_fusion.refs_8_), channel_id=1, source_target_pairs={{0,8},{4,12},{8,0},{12,4},{16,24},{20,28},{24,16},{28,20},{1,9},{5... | collective-permute-start | bytes 1179656 | tf_op jit(solution)/shard_map/ppermute | solution.py:239
  71.3 17.7 %collective-permute-start.15 = (bf16[256,768]{1,0:T(8,128)(2,1)}, bf16[256,768]{1,0:T(8,128)(2,1)}, u32[]{:S(2)}, u32[]{:S(2)}) collective-permute-start(bf16[256,768]{1,0:T(8,128)(2,1)} %slice_select_fusion.refs_8_), channel_id=1, source_target_pairs={{0,16},{4,20},{8,24},{12,28},{16,0},{20,4},{24,8},{28,12},{1,17},{... | collective-permute-start | bytes 1179656 | tf_op jit(solution)/shard_map/ppermute | solution.py:239
  72.6 16.5 %collective-permute-start.16 = (bf16[256,768]{1,0:T(8,128)(2,1)}, bf16[256,768]{1,0:T(8,128)(2,1)}, u32[]{:S(2)}, u32[]{:S(2)}) collective-permute-start(bf16[256,768]{1,0:T(8,128)(2,1)} %slice_select_fusion.refs_8_), channel_id=1, source_target_pairs={{0,24},{4,28},{8,16},{12,20},{16,8},{20,12},{24,0},{28,4},{1,25},{... | collective-permute-start | bytes 1179656 | tf_op jit(solution)/shard_map/ppermute | solution.py:239
  89.1 7.2 %collective-permute-start.18 = (bf16[256,512]{1,0:T(8,128)(2,1)S(1)}, bf16[256,512]{1,0:T(8,128)(2,1)S(1)}, u32[]{:S(2)}, u32[]{:S(2)}) collective-permute-start(bf16[256,512]{1,0:T(8,128)(2,1)S(1)} %pad_maximum_fusion.2.refs_0_), channel_id=1, source_target_pairs={{0,8},{4,12},{1,9},{5,13},{2,10},{6,14},{3,11},{7,15},{16,24},{20,... | collective-permute-start | bytes 786440 | tf_op jit(solution)/shard_map/ppermute | solution.py:17
  90.5 13.5 %collective-permute-start.17 = (bf16[256,512]{1,0:T(8,128)(2,1)S(1)}, bf16[256,512]{1,0:T(8,128)(2,1)S(1)}, u32[]{:S(2)}, u32[]{:S(2)}) collective-permute-start(bf16[256,512]{1,0:T(8,128)(2,1)S(1)} %pad_maximum_fusion.2.refs_0_), channel_id=1, source_target_pairs={{0,4},{8,12},{1,5},{9,13},{2,6},{10,14},{3,7},{11,15},{16,20},{24,... | collective-permute-start | bytes 786440 | tf_op jit(solution)/shard_map/ppermute | solution.py:266
  96.3 8.5 %collective-permute-start.19 = (bf16[256,512]{1,0:T(8,128)(2,1)S(1)}, bf16[256,512]{1,0:T(8,128)(2,1)S(1)}, u32[]{:S(2)}, u32[]{:S(2)}) collective-permute-start(bf16[256,512]{1,0:T(8,128)(2,1)S(1)} %collective-permute-done.18.refs_2_), channel_id=1, source_target_pairs={{8,12},{12,8},{9,13},{13,9},{10,14},{14,10},{11,15},{15,11},{24,28... | collective-permute-start | bytes 786440 | tf_op jit(solution)/shard_map/ppermute | solution.py:267
  106.5 4.3 %collective-permute-start.21 = (bf16[64,256]{1,0:T(8,128)(2,1)S(1)}, bf16[64,256]{1,0:T(8,128)(2,1)S(1)}, u32[]{:S(2)}, u32[]{:S(2)}) collective-permute-start(bf16[64,256]{1,0:T(8,128)(2,1)S(1)} %get-tuple-element.22), channel_id=1, source_target_pairs={{0,2},{1,3},{2,0},{3,1},{4,6},{5,7},{6,4},{7,5},{8,10},{9,11},{10,... | collective-permute-start | bytes 98312 | tf_op jit(solution)/shard_map/ppermute | solution.py:286
  109.5 4.6 %collective-permute-start.22 = (bf16[64,256]{1,0:T(8,128)(2,1)S(1)}, bf16[64,256]{1,0:T(8,128)(2,1)S(1)}, u32[]{:S(2)}, u32[]{:S(2)}) collective-permute-start(bf16[64,256]{1,0:T(8,128)(2,1)S(1)} %get-tuple-element.23), channel_id=1, source_target_pairs={{0,3},{1,2},{2,1},{3,0},{4,7},{5,6},{6,5},{7,4},{8,11},{9,10},{10,... | collective-permute-start | bytes 98312 | tf_op jit(solution)/shard_map/ppermute | solution.py:286
  110.6 3.5 %collective-permute-start.20 = (bf16[64,256]{1,0:T(8,128)(2,1)S(1)}, bf16[64,256]{1,0:T(8,128)(2,1)S(1)}, u32[]{:S(2)}, u32[]{:S(2)}) collective-permute-start(bf16[64,256]{1,0:T(8,128)(2,1)S(1)} %get-tuple-element.24), channel_id=1, source_target_pairs={{0,1},{1,0},{2,3},{3,2},{4,5},{5,4},{6,7},{7,6},{8,9},{9,8},{10,11... | collective-permute-start | bytes 98312 | tf_op jit(solution)/shard_map/ppermute | solution.py:286
  114.1 2.9 %collective-permute-start.23 = (bf16[64,1024]{1,0:T(8,128)(2,1)S(1)}, bf16[64,1024]{1,0:T(8,128)(2,1)S(1)}, u32[]{:S(2)}, u32[]{:S(2)}) collective-permute-start(bf16[64,1024]{1,0:T(8,128)(2,1)S(1)} %pad_maximum_fusion.5), channel_id=1, source_target_pairs={{0,4},{4,0},{8,12},{12,8},{16,20},{20,16},{24,28},{28,24},{1,5},{5... | collective-permute-start | bytes 393224 | tf_op jit(solution)/shard_map/ppermute | solution.py:235
  (28 other events, 387.3 us)

commit v4 on v3

--- a/solution.py
+++ b/solution.py
@@ -163,38 +163,60 @@
 
 
 def output_kernel(place_ref, att_ref, gate_ref, own_ref, *refs):
-    pieces, out_ref = refs[:-1], refs[-1]
+    pieces, outs, held_ref, sems = refs[:-4], refs[-4:-2], refs[-2], refs[-1]
     count = len(pieces) // 3
-    span = out_ref.shape[1] // count
+    span = outs[0].shape[1] // count
     width = own_ref.shape[0]
-    rows = out_ref.shape[0] // 2
+    rows = outs[0].shape[0]
     core, chip = place_ref[0] % 2, place_ref[0] // 2
+
+    def chunk_of(delta):
+        return pl.multiple_of((core * count + (chip ^ delta)) * span, 128)
+
+    copies = []
     for delta in range(count):
-        chunk = chip ^ delta
-        start = pl.multiple_of((core * count + chunk) * span, 128)
-        there = pl.ds(start, span)
-        total = jnp.dot(att_ref[:, :width], own_ref[:, there], preferred_element_type=jnp.float32)
-        for s in range(3):
+        sources = [own_ref.at[:, pl.ds(chunk_of(delta), span)]]
+        sources += [pieces[count * s + delta] for s in range(3)]
+        copies.append(
+            [
+                pltpu.make_async_copy(source, held_ref.at[4 * delta + s], sems.at[4 * delta + s])
+                for s, source in enumerate(sources)
+            ]
+        )
+    for group in copies:
+        for copy in group:
+            copy.start()
+    for delta in range(count):
+        there = pl.ds(chunk_of(delta), span)
+        total = jnp.zeros((2 * rows, span), jnp.float32)
+        for s, copy in enumerate(copies[delta]):
+            copy.wait()
             total += jnp.dot(
-                att_ref[:, (s + 1) * width : (s + 2) * width],
-                pieces[count * s + delta][...],
+                att_ref[:, s * width : (s + 1) * width],
+                held_ref[4 * delta + s],
                 preferred_element_type=jnp.float32,
             )
-        target = pl.ds(pl.multiple_of(chunk * span, 128), span)
+        target = pl.ds(pl.multiple_of((chip ^ delta) * span, 128), span)
         for half in range(2):
             part = total[half * rows : (half + 1) * rows] * gate_ref[half : half + 1, there]
-            out_ref[half * rows : (half + 1) * rows, target] = part.astype(jnp.bfloat16)
+            outs[half][:, target] = part.astype(jnp.bfloat16)
 
 
 def project_out(place, att, gate, own, pieces):
     rows, width = att.shape[0], own.shape[1] // 2
+    count = len(pieces) // 3
     vmem = pl.BlockSpec(memory_space=pltpu.VMEM)
+    anywhere = pl.BlockSpec(memory_space=pl.ANY)
     return pl.pallas_call(
         output_kernel,
-        out_shape=jax.ShapeDtypeStruct((rows, width), jnp.bfloat16),
-        in_specs=[pl.BlockSpec(memory_space=pltpu.SMEM)] + [vmem] * (3 + len(pieces)),
-        out_specs=vmem,
-        compiler_params=pltpu.CompilerParams(vmem_limit_bytes=40 << 20),
+        out_shape=[jax.ShapeDtypeStruct((rows // 2, width), jnp.bfloat16)] * 2,
+        in_specs=[pl.BlockSpec(memory_space=pltpu.SMEM), vmem, vmem] + [anywhere] * (1 + len(pieces)),
+        out_specs=[vmem, vmem],
+        scratch_shapes=[
+            pltpu.VMEM((4 * count,) + pieces[0].shape, jnp.bfloat16),
+            pltpu.SemaphoreType.DMA((4 * count,)),
+        ],
+        compiler_params=pltpu.CompilerParams(vmem_limit_bytes=56 << 20),
         cost_estimate=pl.CostEstimate(
             flops=16 * rows * att.shape[1] * width,
             bytes_accessed=2 * rows * width,
@@ -290,8 +312,8 @@
         [blocks[0], came[0], jnp.where(outer, came[1], came[2]), jnp.where(outer, came[2], came[1])],
         axis=1,
     )
-    both = project_out(place[None], jnp.concatenate([att, swap(att)], axis=0), gates, w_out, pieces)
-    mine, theirs = both[:rows], swap(both[rows:])
+    mine, theirs = project_out(place[None], jnp.concatenate([att, swap(att)], axis=0), gates, w_out, pieces)
+    theirs = swap(theirs)
     mixed = jnp.where(
         core == 0,
         jnp.concatenate([mine, theirs], axis=1),

time: 126 us -> 128 us (1.016)
  local copies, waits for them, and re-layouts: 16.4 us -> 11.2 us
  Pallas kernels: 11 us -> 14.3 us
  other arithmetic: 3.43 us -> 5.87 us
  waiting for transfers between devices: 54.7 us -> 56.9 us
    unnamed x55 -> x37, local copies, waits for them, and re-layouts: 14.3 us -> 9.21 us
    pallas_call x1, Pallas kernels: 2.38 us -> 5.69 us  [project_out(): pl.pallas_call(output_kernel, out_shape=[jax.ShapeDtypeStruct((rows // 2,...]
    ppermute x2, waiting for transfers between devices: 4.42 us -> 6.38 us  [outward(): return lax.ppermute(value, 'head', [(1, 0), (2, 3)])]
  transfers between devices with their start and end apart: 25 -> 25, of which waited for: 12 -> 11; matrix products, arithmetic and copies ran while one was open for 4% -> 4% of each run, Pallas kernels for 6% -> 5%
where the time goes in v4:
time: 128 us; the launch traced here: 127 us
  waiting for transfers between devices  56.9 us (44%)
  starting transfers between devices  37.7 us (29%)
  Pallas kernels  14.3 us (11%)
  local copies, waits for them, and re-layouts  11.2 us (9%)
  other arithmetic  5.87 us (5%)
    ppermute x2, waiting for transfers between devices, pair(): return lax.ppermute(value, 'head', [(0, 1), (1, 0), (2, 3), (3, 2)])  24.9 us
    ppermute x9, waiting for transfers between devices, across_plane(): lax.ppermute(piece, PLANE, [(i, i ^ delta) for i in range(plane)])  14.6 us
    unnamed x37, local copies, waits for them, and re-layouts  9.21 us
    ppermute x9, starting transfers between devices, across_plane(): lax.ppermute(piece, PLANE, [(i, i ^ delta) for i in range(plane)])  8.01 us
    ppermute x1, starting transfers between devices, gather_body(): kv_both = lax.ppermute(kv_chip, 'tract', [(2, 3), (3, 2)])  7.4 us
    pallas_call x2, Pallas kernels, project_qkv(): pl.pallas_call(functools.partial(qkv_kernel, [len(group) for group in gro...  6.53 us
    ppermute x2, starting transfers between devices, pair(): return lax.ppermute(value, 'head', [(0, 1), (1, 0), (2, 3), (3, 2)])  6.43 us
    ppermute x2, waiting for transfers between devices, outward(): return lax.ppermute(value, 'head', [(1, 0), (2, 3)])  6.38 us
  transfers between devices with their start and end apart: 25, of which 11 were waited for; matrix products, arithmetic and copies ran while one was open for 4% of the time, Pallas kernels for 5%

profile of v4, /device:TPU:3, one launch (start us, length us, event | category | flops | bytes accessed | tf_op | source)
XLA Modules:
  0.0 127.0 jit_solution(1396785788538129133)
XLA Ops:
  1.8 3.9 %collective-permute-start.3 = (bf16[256,768]{1,0:T(8,128)(2,1)S(1)}, bf16[256,768]{1,0:T(8,128)(2,1)S(1)}, u32[]{:S(2)}, u32[]{:S(2)}) collective-permute-start(bf16[256,768]{1,0:T(8,128)(2,1)S(1)} %constant_dynamic-slice_fusion), channel_id=1, source_target_pairs={{0,1},{1,0},{2,3},{3,2},{4,5},{5,4},{6,7},{7,6},{8,9},{9,8},{10,11... | collective-permute-start | bytes 1179656 | tf_op jit(solution)/shard_map/ppermute | solution.py:248
  5.7 1.5 %copy.8.style_ref = f32[8,3,6144]{2,1,0:T(4,128)S(1)} copy(f32[8,3,6144]{2,0,1:T(8,128)} %param.11) | data formatting | bytes 1179648 | tf_op args[5]
  9.6 4.6 %collective-permute-done.3.refs_0_ = bf16[256,768]{1,0:T(8,128)(2,1)S(1)} collective-permute-done((bf16[256,768]{1,0:T(8,128)(2,1)S(1)}, bf16[256,768]{1,0:T(8,128)(2,1)S(1)}, u32[]{:S(2)}, u32[]{:S(2)}) %collective-permute-start.3) | collective-permute-done | bytes 393248 | tf_op jit(solution)/shard_map/ppermute | solution.py:248
  15.8 2.5 %collective-permute-start.2 = (bf16[768,768]{1,0:T(8,128)(2,1)S(1)}, bf16[768,768]{1,0:T(8,128)(2,1)S(1)}, u32[]{:S(2)}, u32[]{:S(2)}) collective-permute-start(bf16[768,768]{1,0:T(8,128)(2,1)S(1)} %get-tuple-element.15), channel_id=1, source_target_pairs={{0,1},{1,0},{2,3},{3,2},{4,5},{5,4},{6,7},{7,6},{8,9},{9,8},{10,11... | collective-permute-start | bytes 3538952 | tf_op jit(solution)/shard_map/ppermute | solution.py:248
  22.3 20.3 %collective-permute-done.2.refs_1_ = bf16[768,768]{1,0:T(8,128)(2,1)S(1)} collective-permute-done((bf16[768,768]{1,0:T(8,128)(2,1)S(1)}, bf16[768,768]{1,0:T(8,128)(2,1)S(1)}, u32[]{:S(2)}, u32[]{:S(2)}) %collective-permute-start.2) | collective-permute-done | bytes 1179680 | tf_op jit(solution)/shard_map/ppermute | solution.py:248
  45.1 1.5 %collective-permute-start.9 = (bf16[512,768]{1,0:T(8,128)(2,1)}, bf16[512,768]{1,0:T(8,128)(2,1)}, u32[]{:S(2)}, u32[]{:S(2)}) collective-permute-start(bf16[512,768]{1,0:T(8,128)(2,1)} %slice.40), channel_id=1, source_target_pairs={{1,2},{2,1},{5,6},{6,5},{9,10},{10,9},{13,14},{14,13},{17,18},{18,... | collective-permute-start | bytes 2359304 | tf_op jit(solution)/shard_map/ppermute | solution.py:251
  49.4 5.3 %collective-permute-done.10.refs_5_ = bf16[256,768]{1,0:T(8,128)(2,1)S(1)} collective-permute-done((bf16[256,768]{1,0:T(8,128)(2,1)S(1)}, bf16[256,768]{1,0:T(8,128)(2,1)S(1)}, u32[]{:S(2)}, u32[]{:S(2)}) %collective-permute-start.10) | collective-permute-done | bytes 393248 | tf_op jit(solution)/shard_map/ppermute | solution.py:261
  54.8 9.3 %collective-permute-done.12.refs_7_ = bf16[256,768]{1,0:T(8,128)(2,1)S(1)} collective-permute-done((bf16[256,768]{1,0:T(8,128)(2,1)S(1)}, bf16[256,768]{1,0:T(8,128)(2,1)S(1)}, u32[]{:S(2)}, u32[]{:S(2)}) %collective-permute-start.12) | collective-permute-done | bytes 393248 | tf_op jit(solution)/shard_map/ppermute | solution.py:261
  64.0 3.8 %collective-permute-done.5.refs_2_ = bf16[768,768]{1,0:T(8,128)(2,1)} collective-permute-done((bf16[768,768]{1,0:T(8,128)(2,1)S(1)}, bf16[768,768]{1,0:T(8,128)(2,1)}, u32[]{:S(2)}, u32[]{:S(2)}) %collective-permute-start.5) | collective-permute-done | bytes 1179680 | tf_op jit(solution)/shard_map/ppermute | solution.py:254
  69.2 1.8 %slice_select_fusion.refs_8_ = bf16[256,768]{1,0:T(8,128)(2,1)} fusion(bf16[768,768]{1,0:T(8,128)(2,1)S(1)} %collective-permute-done.4.refs_3_, bf16[768,768]{1,0:T(8,128)(2,1)} %collective-permute-done.5.refs_2_, pred[]{:T(512)S(6)} %or.3), kind=kLoop, calls=%fused_computation.3 | loop fusion | flops 196608 | bytes 1179649 | tf_op jit(solution)/shard_map/jit(_where)/select_n | solution.py:280
  73.6 3.7 %copy-done = bf16[6144,3,256]{2,0,1:T(8,128)(2,1)S(1)} copy-done((bf16[6144,3,256]{2,0,1:T(8,128)(2,1)S(1)}, bf16[6144,3,256]{2,0,1:T(8,128)(2,1)}, u32[]{:S(2)}) %copy-start) | copy-done | bytes 9437208
  79.7 3.4 %project_qkv.2 = bf16[192,768]{1,0:T(8,128)(2,1)S(1)} custom-call(s32[1]{0:T(128)} %bitcast.1.outer_ref, bf16[512,768]{1,0:T(8,128)(2,1)S(1)} %bitcast.15, bf16[768,768]{1,0:T(8,128)(2,1)S(1)} %collective-permute-done.2.refs_1_, bf16[768,768]{1,0:T(8,128)(2,1)} %collective-permute-done.5.refs_2_, bf16[768,768]{1,0:T(8,128)(2,1)S(1)} %copy-done.5, ...), custom_call_target="tpu_custom_call" | custom-call | flops 1811939328 | bytes 11796480 | tf_op jit(solution)/shard_map/project_qkv/pallas_call | solution.py:149
  83.1 2.6 %collective-permute-done.13.refs_0_ = bf16[512,768]{1,0:T(8,128)(2,1)} collective-permute-done((bf16[512,768]{1,0:T(8,128)(2,1)}, bf16[512,768]{1,0:T(8,128)(2,1)}, u32[]{:S(2)}, u32[]{:S(2)}) %collective-permute-start.13) | collective-permute-done | bytes 786464 | tf_op jit(solution)/shard_map/ppermute | solution.py:254
  85.7 3.1 %project_qkv.3 = bf16[64,768]{1,0:T(8,128)(2,1)S(1)} custom-call(s32[1]{0:T(128)} %bitcast.1.outer_ref, bf16[512,768]{1,0:T(8,128)(2,1)} %collective-permute-done.13.refs_0_, bf16[512,768]{1,0:T(8,128)(2,1)} %collective-permute-done.9.refs_1_, bf16[3,6144,256]{2,1,0:T(8,128)(2,1)S(1)} %bitcast.13), custom_call_target="tpu_custom_call" | custom-call | flops 603979776 | bytes 10223616 | tf_op jit(solution)/shard_map/project_qkv/pallas_call | solution.py:149
  91.5 4.5 %collective-permute-done.18.refs_2_ = bf16[256,512]{1,0:T(8,128)(2,1)S(1)} collective-permute-done((bf16[256,512]{1,0:T(8,128)(2,1)S(1)}, bf16[256,512]{1,0:T(8,128)(2,1)S(1)}, u32[]{:S(2)}, u32[]{:S(2)}) %collective-permute-start.18) | collective-permute-done | bytes 262176 | tf_op jit(solution)/shard_map/ppermute | solution.py:17
  96.0 7.4 %collective-permute-start.19 = (bf16[256,512]{1,0:T(8,128)(2,1)S(1)}, bf16[256,512]{1,0:T(8,128)(2,1)S(1)}, u32[]{:S(2)}, u32[]{:S(2)}) collective-permute-start(bf16[256,512]{1,0:T(8,128)(2,1)S(1)} %collective-permute-done.18.refs_2_), channel_id=1, source_target_pairs={{8,12},{12,8},{9,13},{13,9},{10,14},{14,10},{11,15},{15,11},{24,28... | collective-permute-start | bytes 786440 | tf_op jit(solution)/shard_map/ppermute | solution.py:289
  104.6 1.6 %attend.1 = bf16[256,256]{1,0:T(8,128)(2,1)S(1)} custom-call(bf16[256,256]{1,0:T(8,128)(2,1)S(1)} %pad_maximum_fusion.4.q_ref, bf16[256,512]{1,0:T(8,128)(2,1)S(1)} %pad_maximum_fusion.2.refs_0_, bf16[256,512]{1,0:T(8,128)(2,1)S(1)} %collective-permute-done.17.refs_1_, bf16[256,512]{1,0:T(8,128)(2,1)S(1)} %collective-permute-done.18.refs_2_, ...), custom_call_target="tpu_custom_call" | custom-call | flops 134217728 | bytes 786432 | tf_op jit(solution)/shard_map/attend/pallas_call | solution.py:60
  106.2 2.5 %collective-permute-start.21 = (bf16[64,256]{1,0:T(8,128)(2,1)S(1)}, bf16[64,256]{1,0:T(8,128)(2,1)S(1)}, u32[]{:S(2)}, u32[]{:S(2)}) collective-permute-start(bf16[64,256]{1,0:T(8,128)(2,1)S(1)} %get-tuple-element.24), channel_id=1, source_target_pairs={{0,2},{1,3},{2,0},{3,1},{4,6},{5,7},{6,4},{7,5},{8,10},{9,11},{10,... | collective-permute-start | bytes 98312 | tf_op jit(solution)/shard_map/ppermute | solution.py:308
  108.7 1.4 %collective-permute-start.22 = (bf16[64,256]{1,0:T(8,128)(2,1)S(1)}, bf16[64,256]{1,0:T(8,128)(2,1)S(1)}, u32[]{:S(2)}, u32[]{:S(2)}) collective-permute-start(bf16[64,256]{1,0:T(8,128)(2,1)S(1)} %get-tuple-element.25), channel_id=1, source_target_pairs={{0,3},{1,2},{2,1},{3,0},{4,7},{5,6},{6,5},{7,4},{8,11},{9,10},{10,... | collective-permute-start | bytes 98312 | tf_op jit(solution)/shard_map/ppermute | solution.py:308
  110.2 3.1 %collective-permute-done.22 = bf16[64,256]{1,0:T(8,128)(2,1)S(1)} collective-permute-done((bf16[64,256]{1,0:T(8,128)(2,1)S(1)}, bf16[64,256]{1,0:T(8,128)(2,1)S(1)}, u32[]{:S(2)}, u32[]{:S(2)}) %collective-permute-start.22) | collective-permute-done | bytes 32800 | tf_op jit(solution)/shard_map/ppermute | solution.py:308
  113.3 2.1 %collective-permute-start.23 = (bf16[64,1024]{1,0:T(8,128)(2,1)S(1)}, bf16[64,1024]{1,0:T(8,128)(2,1)S(1)}, u32[]{:S(2)}, u32[]{:S(2)}) collective-permute-start(bf16[64,1024]{1,0:T(8,128)(2,1)S(1)} %pad_maximum_fusion.5), channel_id=1, source_target_pairs={{0,4},{4,0},{8,12},{12,8},{16,20},{20,16},{24,28},{28,24},{1,5},{5... | collective-permute-start | bytes 393224 | tf_op jit(solution)/shard_map/ppermute | solution.py:257
  117.2 5.7 %project_out.1 = (bf16[64,3072]{1,0:T(8,128)(2,1)}, bf16[64,3072]{1,0:T(8,128)(2,1)}) custom-call(s32[1]{0:T(128)} %bitcast.place_ref, bf16[128,1024]{1,0:T(8,128)(2,1)} %pad_maximum_fusion.3.att_ref, f32[2,6144]{1,0:T(2,128)} %pad_maximum_fusion.6.gate_ref, bf16[256,6144]{1,0:T(8,128)(2,1)} %own_ref.1, bf16[256,768]{1,0:T(8,128)(2,1)} %copy-done.8, ...), custom_call_target="tpu_custom_call" | custom-call | flops 6442450944 | bytes 786432 | tf_op jit(solution)/shard_map/project_out/pallas_call | solution.py:210
  123.3 1.6 %collective-permute-done.24 = bf16[64,3072]{1,0:T(8,128)(2,1)S(1)} collective-permute-done((bf16[64,3072]{1,0:T(8,128)(2,1)}, bf16[64,3072]{1,0:T(8,128)(2,1)S(1)}, u32[]{:S(2)}, u32[]{:S(2)}) %collective-permute-start.24) | collective-permute-done | bytes 393248 | tf_op jit(solution)/shard_map/ppermute | solution.py:257
  124.9 2.2 %maximum_select_fusion = bf16[1,64,6144]{2,1,0:T(8,128)(2,1)} fusion(bf16[1,64,3072]{2,1,0:T(8,128)(2,1)S(1)} %bitcast.18, bf16[1,64,3072]{2,1,0:T(8,128)(2,1)} %bitcast.17, pred[]{:T(512)S(6)} %eq.27), kind=kLoop, calls=%fused_computation.2 | loop fusion | flops 3538944 | bytes 1572865 | tf_op jit(solution)/shard_map/jit(_where)/select_n | solution.py:317
  (83 shorter events, 26.6 us)
Async XLA Ops:
  1.1 8.5 %collective-permute-start = (bf16[256,768]{1,0:T(8,128)(2,1)S(1)}, bf16[256,768]{1,0:T(8,128)(2,1)S(1)}, u32[]{:S(2)}, u32[]{:S(2)}) collective-permute-start(bf16[256,768]{1,0:T(8,128)(2,1)S(1)} %constant_dynamic-slice_fusion), channel_id=1, source_target_pairs={{1,2},{2,1},{5,6},{6,5},{9,10},{10,9},{13,14},{14,13},{17,18},{18,... | collective-permute-start | bytes 1179656 | tf_op jit(solution)/shard_map/ppermute | solution.py:251
  1.8 12.4 %collective-permute-start.3 = (bf16[256,768]{1,0:T(8,128)(2,1)S(1)}, bf16[256,768]{1,0:T(8,128)(2,1)S(1)}, u32[]{:S(2)}, u32[]{:S(2)}) collective-permute-start(bf16[256,768]{1,0:T(8,128)(2,1)S(1)} %constant_dynamic-slice_fusion), channel_id=1, source_target_pairs={{0,1},{1,0},{2,3},{3,2},{4,5},{5,4},{6,7},{7,6},{8,9},{9,8},{10,11... | collective-permute-start | bytes 1179656 | tf_op jit(solution)/shard_map/ppermute | solution.py:248
  8.3 6.8 %collective-permute-start.1 = (f32[1,6144]{1,0:T(1,128)S(1)}, f32[1,6144]{1,0:T(1,128)S(1)}, u32[]{:S(2)}, u32[]{:S(2)}) collective-permute-start(f32[1,6144]{1,0:T(1,128)S(1)} %get-tuple-element.14), channel_id=1, source_target_pairs={{0,4},{4,0},{8,12},{12,8},{16,20},{20,16},{24,28},{28,24},{1,5},{5... | collective-permute-start | bytes 73736 | tf_op jit(solution)/shard_map/ppermute | solution.py:257
  14.4 6.6 %collective-permute-start.4 = (bf16[768,768]{1,0:T(8,128)(2,1)S(1)}, bf16[768,768]{1,0:T(8,128)(2,1)S(1)}, u32[]{:S(2)}, u32[]{:S(2)}) collective-permute-start(bf16[768,768]{1,0:T(8,128)(2,1)S(1)} %get-tuple-element.21), channel_id=1, source_target_pairs={{1,2},{2,1},{5,6},{6,5},{9,10},{10,9},{13,14},{14,13},{17,18},{18,... | collective-permute-start | bytes 3538952 | tf_op jit(solution)/shard_map/ppermute | solution.py:251
  15.8 26.7 %collective-permute-start.2 = (bf16[768,768]{1,0:T(8,128)(2,1)S(1)}, bf16[768,768]{1,0:T(8,128)(2,1)S(1)}, u32[]{:S(2)}, u32[]{:S(2)}) collective-permute-start(bf16[768,768]{1,0:T(8,128)(2,1)S(1)} %get-tuple-element.15), channel_id=1, source_target_pairs={{0,1},{1,0},{2,3},{3,2},{4,5},{5,4},{6,7},{7,6},{8,9},{9,8},{10,11... | collective-permute-start | bytes 3538952 | tf_op jit(solution)/shard_map/ppermute | solution.py:248
  18.3 25.1 %collective-permute-start.6 = (bf16[256,768]{1,0:T(8,128)(2,1)S(1)}, bf16[256,768]{1,0:T(8,128)(2,1)S(1)}, u32[]{:S(2)}, u32[]{:S(2)}) collective-permute-start(bf16[256,768]{1,0:T(8,128)(2,1)S(1)} %collective-permute-done.3.refs_0_), channel_id=1, source_target_pairs={{0,8},{4,12},{8,0},{12,4},{16,24},{20,28},{24,16},{28,20},{1,9},{5... | collective-permute-start | bytes 1179656 | tf_op jit(solution)/shard_map/ppermute | solution.py:261
  18.6 24.9 %collective-permute-start.7 = (bf16[256,768]{1,0:T(8,128)(2,1)S(1)}, bf16[256,768]{1,0:T(8,128)(2,1)S(1)}, u32[]{:S(2)}, u32[]{:S(2)}) collective-permute-start(bf16[256,768]{1,0:T(8,128)(2,1)S(1)} %collective-permute-done.3.refs_0_), channel_id=1, source_target_pairs={{0,16},{4,20},{8,24},{12,28},{16,0},{20,4},{24,8},{28,12},{1,17},{... | collective-permute-start | bytes 1179656 | tf_op jit(solution)/shard_map/ppermute | solution.py:261
  19.8 23.7 %collective-permute-start.8 = (bf16[256,768]{1,0:T(8,128)(2,1)S(1)}, bf16[256,768]{1,0:T(8,128)(2,1)S(1)}, u32[]{:S(2)}, u32[]{:S(2)}) collective-permute-start(bf16[256,768]{1,0:T(8,128)(2,1)S(1)} %collective-permute-done.3.refs_0_), channel_id=1, source_target_pairs={{0,24},{4,28},{8,16},{12,20},{16,8},{20,12},{24,0},{28,4},{1,25},{... | collective-permute-start | bytes 1179656 | tf_op jit(solution)/shard_map/ppermute | solution.py:261
  21.0 46.9 %collective-permute-start.5 = (bf16[768,768]{1,0:T(8,128)(2,1)S(1)}, bf16[768,768]{1,0:T(8,128)(2,1)}, u32[]{:S(2)}, u32[]{:S(2)}) collective-permute-start(bf16[768,768]{1,0:T(8,128)(2,1)S(1)} %collective-permute-done.4.refs_3_), channel_id=1, source_target_pairs={{1,0},{2,3},{5,4},{6,7},{9,8},{10,11},{13,12},{14,15},{17,16},{18,... | collective-permute-start | bytes 3538952 | tf_op jit(solution)/shard_map/ppermute | solution.py:254
  45.1 18.9 %collective-permute-start.9 = (bf16[512,768]{1,0:T(8,128)(2,1)}, bf16[512,768]{1,0:T(8,128)(2,1)}, u32[]{:S(2)}, u32[]{:S(2)}) collective-permute-start(bf16[512,768]{1,0:T(8,128)(2,1)} %slice.40), channel_id=1, source_target_pairs={{1,2},{2,1},{5,6},{6,5},{9,10},{10,9},{13,14},{14,13},{17,18},{18,... | collective-permute-start | bytes 2359304 | tf_op jit(solution)/shard_map/ppermute | solution.py:251
  46.7 8.1 %collective-permute-start.10 = (bf16[256,768]{1,0:T(8,128)(2,1)S(1)}, bf16[256,768]{1,0:T(8,128)(2,1)S(1)}, u32[]{:S(2)}, u32[]{:S(2)}) collective-permute-start(bf16[256,768]{1,0:T(8,128)(2,1)S(1)} %slice_select_fusion.1.refs_4_), channel_id=1, source_target_pairs={{0,8},{4,12},{8,0},{12,4},{16,24},{20,28},{24,16},{28,20},{1,9},{5... | collective-permute-start | bytes 1179656 | tf_op jit(solution)/shard_map/ppermute | solution.py:261
  47.0 7.7 %collective-permute-start.11 = (bf16[256,768]{1,0:T(8,128)(2,1)S(1)}, bf16[256,768]{1,0:T(8,128)(2,1)S(1)}, u32[]{:S(2)}, u32[]{:S(2)}) collective-permute-start(bf16[256,768]{1,0:T(8,128)(2,1)S(1)} %slice_select_fusion.1.refs_4_), channel_id=1, source_target_pairs={{0,16},{4,20},{8,24},{12,28},{16,0},{20,4},{24,8},{28,12},{1,17},{... | collective-permute-start | bytes 1179656 | tf_op jit(solution)/shard_map/ppermute | solution.py:261
  48.3 15.8 %collective-permute-start.12 = (bf16[256,768]{1,0:T(8,128)(2,1)S(1)}, bf16[256,768]{1,0:T(8,128)(2,1)S(1)}, u32[]{:S(2)}, u32[]{:S(2)}) collective-permute-start(bf16[256,768]{1,0:T(8,128)(2,1)S(1)} %slice_select_fusion.1.refs_4_), channel_id=1, source_target_pairs={{0,24},{4,28},{8,16},{12,20},{16,8},{20,12},{24,0},{28,4},{1,25},{... | collective-permute-start | bytes 1179656 | tf_op jit(solution)/shard_map/ppermute | solution.py:261
  67.9 17.8 %collective-permute-start.13 = (bf16[512,768]{1,0:T(8,128)(2,1)}, bf16[512,768]{1,0:T(8,128)(2,1)}, u32[]{:S(2)}, u32[]{:S(2)}) collective-permute-start(bf16[512,768]{1,0:T(8,128)(2,1)} %collective-permute-done.9.refs_1_), channel_id=1, source_target_pairs={{1,0},{2,3},{5,4},{6,7},{9,8},{10,11},{13,12},{14,15},{17,16},{18,... | collective-permute-start | bytes 2359304 | tf_op jit(solution)/shard_map/ppermute | solution.py:254
  71.0 17.9 %collective-permute-start.14 = (bf16[256,768]{1,0:T(8,128)(2,1)}, bf16[256,768]{1,0:T(8,128)(2,1)}, u32[]{:S(2)}, u32[]{:S(2)}) collective-permute-start(bf16[256,768]{1,0:T(8,128)(2,1)} %slice_select_fusion.refs_8_), channel_id=1, source_target_pairs={{0,8},{4,12},{8,0},{12,4},{16,24},{20,28},{24,16},{28,20},{1,9},{5... | collective-permute-start | bytes 1179656 | tf_op jit(solution)/shard_map/ppermute | solution.py:261
  71.2 17.6 %collective-permute-start.15 = (bf16[256,768]{1,0:T(8,128)(2,1)}, bf16[256,768]{1,0:T(8,128)(2,1)S(1)}, u32[]{:S(2)}, u32[]{:S(2)}) collective-permute-start(bf16[256,768]{1,0:T(8,128)(2,1)} %slice_select_fusion.refs_8_), channel_id=1, source_target_pairs={{0,16},{4,20},{8,24},{12,28},{16,0},{20,4},{24,8},{28,12},{1,17},{... | collective-permute-start | bytes 1179656 | tf_op jit(solution)/shard_map/ppermute | solution.py:261
  72.5 16.4 %collective-permute-start.16 = (bf16[256,768]{1,0:T(8,128)(2,1)}, bf16[256,768]{1,0:T(8,128)(2,1)S(1)}, u32[]{:S(2)}, u32[]{:S(2)}) collective-permute-start(bf16[256,768]{1,0:T(8,128)(2,1)} %slice_select_fusion.refs_8_), channel_id=1, source_target_pairs={{0,24},{4,28},{8,16},{12,20},{16,8},{20,12},{24,0},{28,4},{1,25},{... | collective-permute-start | bytes 1179656 | tf_op jit(solution)/shard_map/ppermute | solution.py:261
  88.9 7.1 %collective-permute-start.18 = (bf16[256,512]{1,0:T(8,128)(2,1)S(1)}, bf16[256,512]{1,0:T(8,128)(2,1)S(1)}, u32[]{:S(2)}, u32[]{:S(2)}) collective-permute-start(bf16[256,512]{1,0:T(8,128)(2,1)S(1)} %pad_maximum_fusion.2.refs_0_), channel_id=1, source_target_pairs={{0,8},{4,12},{1,9},{5,13},{2,10},{6,14},{3,11},{7,15},{16,24},{20,... | collective-permute-start | bytes 786440 | tf_op jit(solution)/shard_map/ppermute | solution.py:17
  90.2 13.5 %collective-permute-start.17 = (bf16[256,512]{1,0:T(8,128)(2,1)S(1)}, bf16[256,512]{1,0:T(8,128)(2,1)S(1)}, u32[]{:S(2)}, u32[]{:S(2)}) collective-permute-start(bf16[256,512]{1,0:T(8,128)(2,1)S(1)} %pad_maximum_fusion.2.refs_0_), channel_id=1, source_target_pairs={{0,4},{8,12},{1,5},{9,13},{2,6},{10,14},{3,7},{11,15},{16,20},{24,... | collective-permute-start | bytes 786440 | tf_op jit(solution)/shard_map/ppermute | solution.py:288
  96.0 8.5 %collective-permute-start.19 = (bf16[256,512]{1,0:T(8,128)(2,1)S(1)}, bf16[256,512]{1,0:T(8,128)(2,1)S(1)}, u32[]{:S(2)}, u32[]{:S(2)}) collective-permute-start(bf16[256,512]{1,0:T(8,128)(2,1)S(1)} %collective-permute-done.18.refs_2_), channel_id=1, source_target_pairs={{8,12},{12,8},{9,13},{13,9},{10,14},{14,10},{11,15},{15,11},{24,28... | collective-permute-start | bytes 786440 | tf_op jit(solution)/shard_map/ppermute | solution.py:289
  106.2 4.0 %collective-permute-start.21 = (bf16[64,256]{1,0:T(8,128)(2,1)S(1)}, bf16[64,256]{1,0:T(8,128)(2,1)S(1)}, u32[]{:S(2)}, u32[]{:S(2)}) collective-permute-start(bf16[64,256]{1,0:T(8,128)(2,1)S(1)} %get-tuple-element.24), channel_id=1, source_target_pairs={{0,2},{1,3},{2,0},{3,1},{4,6},{5,7},{6,4},{7,5},{8,10},{9,11},{10,... | collective-permute-start | bytes 98312 | tf_op jit(solution)/shard_map/ppermute | solution.py:308
  108.7 4.6 %collective-permute-start.22 = (bf16[64,256]{1,0:T(8,128)(2,1)S(1)}, bf16[64,256]{1,0:T(8,128)(2,1)S(1)}, u32[]{:S(2)}, u32[]{:S(2)}) collective-permute-start(bf16[64,256]{1,0:T(8,128)(2,1)S(1)} %get-tuple-element.25), channel_id=1, source_target_pairs={{0,3},{1,2},{2,1},{3,0},{4,7},{5,6},{6,5},{7,4},{8,11},{9,10},{10,... | collective-permute-start | bytes 98312 | tf_op jit(solution)/shard_map/ppermute | solution.py:308
  110.2 3.1 %collective-permute-start.20 = (bf16[64,256]{1,0:T(8,128)(2,1)S(1)}, bf16[64,256]{1,0:T(8,128)(2,1)S(1)}, u32[]{:S(2)}, u32[]{:S(2)}) collective-permute-start(bf16[64,256]{1,0:T(8,128)(2,1)S(1)} %get-tuple-element.26), channel_id=1, source_target_pairs={{0,1},{1,0},{2,3},{3,2},{4,5},{5,4},{6,7},{7,6},{8,9},{9,8},{10,11... | collective-permute-start | bytes 98312 | tf_op jit(solution)/shard_map/ppermute | solution.py:308
  113.3 3.1 %collective-permute-start.23 = (bf16[64,1024]{1,0:T(8,128)(2,1)S(1)}, bf16[64,1024]{1,0:T(8,128)(2,1)S(1)}, u32[]{:S(2)}, u32[]{:S(2)}) collective-permute-start(bf16[64,1024]{1,0:T(8,128)(2,1)S(1)} %pad_maximum_fusion.5), channel_id=1, source_target_pairs={{0,4},{4,0},{8,12},{12,8},{16,20},{20,16},{24,28},{28,24},{1,5},{5... | collective-permute-start | bytes 393224 | tf_op jit(solution)/shard_map/ppermute | solution.py:257
  (19 other events, 217.5 us)

commit v5 on v3

--- a/solution.py
+++ b/solution.py
@@ -282,10 +282,9 @@
 
     blocks = [attended[i * rows : (i + 1) * rows] for i in range(4)]
     leaving = [blocks[1], jnp.where(outer, blocks[2], blocks[3]), jnp.where(outer, blocks[3], blocks[2])]
-    came = [
-        lax.ppermute(value, "head", [(i, i ^ (s + 1)) for i in range(4)])
-        for s, value in enumerate(leaving)
-    ]
+    came = [None] * 3
+    for s in (2, 1, 0):
+        came[s] = lax.ppermute(leaving[s], "head", [(i, i ^ (s + 1)) for i in range(4)])
     att = jnp.concatenate(
         [blocks[0], came[0], jnp.where(outer, came[1], came[2]), jnp.where(outer, came[2], came[1])],
         axis=1,

time: 126 us -> 126 us (level)
  no operation moved by 1% of the time
where the time goes in v5:
time: 126 us; the launch traced here: 125 us
  waiting for transfers between devices  54.7 us (43%)
  starting transfers between devices  38.6 us (31%)
  local copies, waits for them, and re-layouts  16.4 us (13%)
  Pallas kernels  11 us (9%)
  other arithmetic  3.43 us (3%)
    ppermute x2, waiting for transfers between devices, pair(): return lax.ppermute(value, 'head', [(0, 1), (1, 0), (2, 3), (3, 2)])  25.1 us
    unnamed x55, local copies, waits for them, and re-layouts  14.3 us
    ppermute x9, waiting for transfers between devices, across_plane(): lax.ppermute(piece, PLANE, [(i, i ^ delta) for i in range(plane)])  14.1 us
    ppermute x9, starting transfers between devices, across_plane(): lax.ppermute(piece, PLANE, [(i, i ^ delta) for i in range(plane)])  8.01 us
    ppermute x1, starting transfers between devices, gather_body(): kv_both = lax.ppermute(kv_chip, 'tract', [(2, 3), (3, 2)])  7.4 us
    ppermute x2, starting transfers between devices, pair(): return lax.ppermute(value, 'head', [(0, 1), (1, 0), (2, 3), (3, 2)])  7.08 us
    pallas_call x2, Pallas kernels, project_qkv(): pl.pallas_call(functools.partial(qkv_kernel, [len(group) for group in gro...  6.53 us
    ppermute x2, waiting for transfers between devices, outward(): return lax.ppermute(value, 'head', [(1, 0), (2, 3)])  4.42 us
  transfers between devices with their start and end apart: 25, of which 12 were waited for; matrix products, arithmetic and copies ran while one was open for 4% of the time, Pallas kernels for 6%

profile of v5, /device:TPU:3, one launch (start us, length us, event | category | flops | bytes accessed | tf_op | source)
XLA Modules:
  0.0 125.3 jit_solution(9882174832841928070)
XLA Ops:
  1.8 3.9 %collective-permute-start.3 = (bf16[256,768]{1,0:T(8,128)(2,1)S(1)}, bf16[256,768]{1,0:T(8,128)(2,1)S(1)}, u32[]{:S(2)}, u32[]{:S(2)}) collective-permute-start(bf16[256,768]{1,0:T(8,128)(2,1)S(1)} %constant_dynamic-slice_fusion), channel_id=1, source_target_pairs={{0,1},{1,0},{2,3},{3,2},{4,5},{5,4},{6,7},{7,6},{8,9},{9,8},{10,11... | collective-permute-start | bytes 1179656 | tf_op jit(solution)/shard_map/ppermute | solution.py:226
  5.7 1.5 %copy.8.style_ref = f32[8,3,6144]{2,1,0:T(4,128)S(1)} copy(f32[8,3,6144]{2,0,1:T(8,128)} %param.11) | data formatting | bytes 1179648 | tf_op args[5]
  9.6 4.6 %collective-permute-done.3.refs_0_ = bf16[256,768]{1,0:T(8,128)(2,1)S(1)} collective-permute-done((bf16[256,768]{1,0:T(8,128)(2,1)S(1)}, bf16[256,768]{1,0:T(8,128)(2,1)S(1)}, u32[]{:S(2)}, u32[]{:S(2)}) %collective-permute-start.3) | collective-permute-done | bytes 393248 | tf_op jit(solution)/shard_map/ppermute | solution.py:226
  15.3 3.2 %collective-permute-start.2 = (bf16[768,768]{1,0:T(8,128)(2,1)S(1)}, bf16[768,768]{1,0:T(8,128)(2,1)S(1)}, u32[]{:S(2)}, u32[]{:S(2)}) collective-permute-start(bf16[768,768]{1,0:T(8,128)(2,1)S(1)} %get-tuple-element.13), channel_id=1, source_target_pairs={{0,1},{1,0},{2,3},{3,2},{4,5},{5,4},{6,7},{7,6},{8,9},{9,8},{10,11... | collective-permute-start | bytes 3538952 | tf_op jit(solution)/shard_map/ppermute | solution.py:226
  22.5 20.5 %collective-permute-done.2.refs_1_ = bf16[768,768]{1,0:T(8,128)(2,1)S(1)} collective-permute-done((bf16[768,768]{1,0:T(8,128)(2,1)S(1)}, bf16[768,768]{1,0:T(8,128)(2,1)S(1)}, u32[]{:S(2)}, u32[]{:S(2)}) %collective-permute-start.2) | collective-permute-done | bytes 1179680 | tf_op jit(solution)/shard_map/ppermute | solution.py:226
  46.2 1.5 %collective-permute-start.9 = (bf16[512,768]{1,0:T(8,128)(2,1)}, bf16[512,768]{1,0:T(8,128)(2,1)}, u32[]{:S(2)}, u32[]{:S(2)}) collective-permute-start(bf16[512,768]{1,0:T(8,128)(2,1)} %slice.48), channel_id=1, source_target_pairs={{1,2},{2,1},{5,6},{6,5},{9,10},{10,9},{13,14},{14,13},{17,18},{18,... | collective-permute-start | bytes 2359304 | tf_op jit(solution)/shard_map/ppermute | solution.py:229
  50.5 5.6 %collective-permute-done.10.refs_5_ = bf16[256,768]{1,0:T(8,128)(2,1)S(1)} collective-permute-done((bf16[256,768]{1,0:T(8,128)(2,1)S(1)}, bf16[256,768]{1,0:T(8,128)(2,1)S(1)}, u32[]{:S(2)}, u32[]{:S(2)}) %collective-permute-start.10) | collective-permute-done | bytes 393248 | tf_op jit(solution)/shard_map/ppermute | solution.py:239
  56.9 8.5 %collective-permute-done.12.refs_7_ = bf16[256,768]{1,0:T(8,128)(2,1)S(1)} collective-permute-done((bf16[256,768]{1,0:T(8,128)(2,1)S(1)}, bf16[256,768]{1,0:T(8,128)(2,1)S(1)}, u32[]{:S(2)}, u32[]{:S(2)}) %collective-permute-start.12) | collective-permute-done | bytes 393248 | tf_op jit(solution)/shard_map/ppermute | solution.py:239
  66.1 1.9 %collective-permute-done.5.refs_2_ = bf16[768,768]{1,0:T(8,128)(2,1)} collective-permute-done((bf16[768,768]{1,0:T(8,128)(2,1)S(1)}, bf16[768,768]{1,0:T(8,128)(2,1)}, u32[]{:S(2)}, u32[]{:S(2)}) %collective-permute-start.5) | collective-permute-done | bytes 1179680 | tf_op jit(solution)/shard_map/ppermute | solution.py:232
  69.3 1.8 %slice_select_fusion.refs_8_ = bf16[256,768]{1,0:T(8,128)(2,1)} fusion(bf16[768,768]{1,0:T(8,128)(2,1)S(1)} %collective-permute-done.4.refs_3_, bf16[768,768]{1,0:T(8,128)(2,1)} %collective-permute-done.5.refs_2_, pred[]{:T(512)S(6)} %or.3), kind=kLoop, calls=%fused_computation.4 | loop fusion | flops 196608 | bytes 1179649 | tf_op jit(solution)/shard_map/jit(_where)/select_n | solution.py:258
  73.8 3.7 %copy-done = bf16[6144,3,256]{2,0,1:T(8,128)(2,1)S(1)} copy-done((bf16[6144,3,256]{2,0,1:T(8,128)(2,1)S(1)}, bf16[6144,3,256]{2,0,1:T(8,128)(2,1)}, u32[]{:S(2)}) %copy-start) | copy-done | bytes 9437208
  79.8 3.4 %project_qkv.2 = bf16[192,768]{1,0:T(8,128)(2,1)S(1)} custom-call(s32[1]{0:T(128)} %bitcast.1.outer_ref, bf16[512,768]{1,0:T(8,128)(2,1)S(1)} %bitcast.16, bf16[768,768]{1,0:T(8,128)(2,1)S(1)} %collective-permute-done.2.refs_1_, bf16[768,768]{1,0:T(8,128)(2,1)} %collective-permute-done.5.refs_2_, bf16[768,768]{1,0:T(8,128)(2,1)S(1)} %copy-done.5, ...), custom_call_target="tpu_custom_call" | custom-call | flops 1811939328 | bytes 11796480 | tf_op jit(solution)/shard_map/project_qkv/pallas_call | solution.py:149
  83.3 2.5 %collective-permute-done.13.refs_0_ = bf16[512,768]{1,0:T(8,128)(2,1)} collective-permute-done((bf16[512,768]{1,0:T(8,128)(2,1)}, bf16[512,768]{1,0:T(8,128)(2,1)}, u32[]{:S(2)}, u32[]{:S(2)}) %collective-permute-start.13) | collective-permute-done | bytes 786464 | tf_op jit(solution)/shard_map/ppermute | solution.py:232
  85.8 3.1 %project_qkv.3 = bf16[64,768]{1,0:T(8,128)(2,1)S(1)} custom-call(s32[1]{0:T(128)} %bitcast.1.outer_ref, bf16[512,768]{1,0:T(8,128)(2,1)} %collective-permute-done.13.refs_0_, bf16[512,768]{1,0:T(8,128)(2,1)} %collective-permute-done.9.refs_1_, bf16[3,6144,256]{2,1,0:T(8,128)(2,1)S(1)} %bitcast.14), custom_call_target="tpu_custom_call" | custom-call | flops 603979776 | bytes 10223616 | tf_op jit(solution)/shard_map/project_qkv/pallas_call | solution.py:149
  89.1 1.4 %collective-permute-start.18 = (bf16[256,512]{1,0:T(8,128)(2,1)S(1)}, bf16[256,512]{1,0:T(8,128)(2,1)S(1)}, u32[]{:S(2)}, u32[]{:S(2)}) collective-permute-start(bf16[256,512]{1,0:T(8,128)(2,1)S(1)} %pad_maximum_fusion.2.refs_0_), channel_id=1, source_target_pairs={{0,8},{4,12},{1,9},{5,13},{2,10},{6,14},{3,11},{7,15},{16,24},{20,... | collective-permute-start | bytes 786440 | tf_op jit(solution)/shard_map/ppermute | solution.py:17
  90.5 1.4 %collective-permute-start.17 = (bf16[256,512]{1,0:T(8,128)(2,1)S(1)}, bf16[256,512]{1,0:T(8,128)(2,1)S(1)}, u32[]{:S(2)}, u32[]{:S(2)}) collective-permute-start(bf16[256,512]{1,0:T(8,128)(2,1)S(1)} %pad_maximum_fusion.2.refs_0_), channel_id=1, source_target_pairs={{0,4},{8,12},{1,5},{9,13},{2,6},{10,14},{3,7},{11,15},{16,20},{24,... | collective-permute-start | bytes 786440 | tf_op jit(solution)/shard_map/ppermute | solution.py:266
  92.0 4.4 %collective-permute-done.18.refs_2_ = bf16[256,512]{1,0:T(8,128)(2,1)S(1)} collective-permute-done((bf16[256,512]{1,0:T(8,128)(2,1)S(1)}, bf16[256,512]{1,0:T(8,128)(2,1)S(1)}, u32[]{:S(2)}, u32[]{:S(2)}) %collective-permute-start.18) | collective-permute-done | bytes 262176 | tf_op jit(solution)/shard_map/ppermute | solution.py:17
  96.3 7.4 %collective-permute-start.19 = (bf16[256,512]{1,0:T(8,128)(2,1)S(1)}, bf16[256,512]{1,0:T(8,128)(2,1)S(1)}, u32[]{:S(2)}, u32[]{:S(2)}) collective-permute-start(bf16[256,512]{1,0:T(8,128)(2,1)S(1)} %collective-permute-done.18.refs_2_), channel_id=1, source_target_pairs={{8,12},{12,8},{9,13},{13,9},{10,14},{14,10},{11,15},{15,11},{24,28... | collective-permute-start | bytes 786440 | tf_op jit(solution)/shard_map/ppermute | solution.py:267
  104.9 1.6 %attend.1 = bf16[256,256]{1,0:T(8,128)(2,1)S(1)} custom-call(bf16[256,256]{1,0:T(8,128)(2,1)S(1)} %pad_maximum_fusion.4.q_ref, bf16[256,512]{1,0:T(8,128)(2,1)S(1)} %pad_maximum_fusion.2.refs_0_, bf16[256,512]{1,0:T(8,128)(2,1)S(1)} %collective-permute-done.17.refs_1_, bf16[256,512]{1,0:T(8,128)(2,1)S(1)} %collective-permute-done.18.refs_2_, ...), custom_call_target="tpu_custom_call" | custom-call | flops 134217728 | bytes 786432 | tf_op jit(solution)/shard_map/attend/pallas_call | solution.py:60
  106.5 3.0 %collective-permute-start.21 = (bf16[64,256]{1,0:T(8,128)(2,1)S(1)}, bf16[64,256]{1,0:T(8,128)(2,1)S(1)}, u32[]{:S(2)}, u32[]{:S(2)}) collective-permute-start(bf16[64,256]{1,0:T(8,128)(2,1)S(1)} %get-tuple-element.22), channel_id=1, source_target_pairs={{0,2},{1,3},{2,0},{3,1},{4,6},{5,7},{6,4},{7,5},{8,10},{9,11},{10,... | collective-permute-start | bytes 98312 | tf_op jit(solution)/shard_map/ppermute | solution.py:287
  110.8 3.3 %collective-permute-done.22 = bf16[64,256]{1,0:T(8,128)(2,1)S(1)} collective-permute-done((bf16[64,256]{1,0:T(8,128)(2,1)S(1)}, bf16[64,256]{1,0:T(8,128)(2,1)S(1)}, u32[]{:S(2)}, u32[]{:S(2)}) %collective-permute-start.22) | collective-permute-done | bytes 32800 | tf_op jit(solution)/shard_map/ppermute | solution.py:287
  114.1 1.9 %collective-permute-start.23 = (bf16[64,1024]{1,0:T(8,128)(2,1)S(1)}, bf16[64,1024]{1,0:T(8,128)(2,1)S(1)}, u32[]{:S(2)}, u32[]{:S(2)}) collective-permute-start(bf16[64,1024]{1,0:T(8,128)(2,1)S(1)} %pad_maximum_fusion.5), channel_id=1, source_target_pairs={{0,4},{4,0},{8,12},{12,8},{16,20},{20,16},{24,28},{28,24},{1,5},{5... | collective-permute-start | bytes 393224 | tf_op jit(solution)/shard_map/ppermute | solution.py:235
  117.1 1.9 %copy-done.11 = bf16[256,6144]{1,0:T(8,128)(2,1)S(1)} copy-done((bf16[256,6144]{1,0:T(8,128)(2,1)S(1)}, bf16[256,6144]{1,0:T(8,128)(2,1)}, u32[]{:S(2)}) %copy-start.11) | copy-done | bytes 3145752
  120.0 2.4 %project_out.1 = bf16[128,3072]{1,0:T(8,128)(2,1)S(1)} custom-call(s32[1]{0:T(128)} %bitcast.place_ref, bf16[128,1024]{1,0:T(8,128)(2,1)S(1)} %pad_maximum_fusion.3.att_ref, f32[2,6144]{1,0:T(2,128)S(1)} %pad_maximum_fusion.6.gate_ref, bf16[256,6144]{1,0:T(8,128)(2,1)S(1)} %copy-done.11, bf16[256,768]{1,0:T(8,128)(2,1)S(1)} %copy-done.10, ...), custom_call_target="tpu_custom_call" | custom-call | flops 6442450944 | bytes 786432 | tf_op jit(solution)/shard_map/project_out/pallas_call | solution.py:192
  (102 shorter events, 29.8 us)
Async XLA Ops:
  1.1 8.5 %collective-permute-start = (bf16[256,768]{1,0:T(8,128)(2,1)S(1)}, bf16[256,768]{1,0:T(8,128)(2,1)S(1)}, u32[]{:S(2)}, u32[]{:S(2)}) collective-permute-start(bf16[256,768]{1,0:T(8,128)(2,1)S(1)} %constant_dynamic-slice_fusion), channel_id=1, source_target_pairs={{1,2},{2,1},{5,6},{6,5},{9,10},{10,9},{13,14},{14,13},{17,18},{18,... | collective-permute-start | bytes 1179656 | tf_op jit(solution)/shard_map/ppermute | solution.py:229
  1.8 12.4 %collective-permute-start.3 = (bf16[256,768]{1,0:T(8,128)(2,1)S(1)}, bf16[256,768]{1,0:T(8,128)(2,1)S(1)}, u32[]{:S(2)}, u32[]{:S(2)}) collective-permute-start(bf16[256,768]{1,0:T(8,128)(2,1)S(1)} %constant_dynamic-slice_fusion), channel_id=1, source_target_pairs={{0,1},{1,0},{2,3},{3,2},{4,5},{5,4},{6,7},{7,6},{8,9},{9,8},{10,11... | collective-permute-start | bytes 1179656 | tf_op jit(solution)/shard_map/ppermute | solution.py:226
  8.3 7.0 %collective-permute-start.1 = (f32[1,6144]{1,0:T(1,128)S(1)}, f32[1,6144]{1,0:T(1,128)S(1)}, u32[]{:S(2)}, u32[]{:S(2)}) collective-permute-start(f32[1,6144]{1,0:T(1,128)S(1)} %get-tuple-element.12), channel_id=1, source_target_pairs={{0,4},{4,0},{8,12},{12,8},{16,20},{20,16},{24,28},{28,24},{1,5},{5... | collective-permute-start | bytes 73736 | tf_op jit(solution)/shard_map/ppermute | solution.py:235
  14.4 6.8 %collective-permute-start.4 = (bf16[768,768]{1,0:T(8,128)(2,1)S(1)}, bf16[768,768]{1,0:T(8,128)(2,1)S(1)}, u32[]{:S(2)}, u32[]{:S(2)}) collective-permute-start(bf16[768,768]{1,0:T(8,128)(2,1)S(1)} %get-tuple-element.19), channel_id=1, source_target_pairs={{1,2},{2,1},{5,6},{6,5},{9,10},{10,9},{13,14},{14,13},{17,18},{18,... | collective-permute-start | bytes 3538952 | tf_op jit(solution)/shard_map/ppermute | solution.py:229
  15.3 27.6 %collective-permute-start.2 = (bf16[768,768]{1,0:T(8,128)(2,1)S(1)}, bf16[768,768]{1,0:T(8,128)(2,1)S(1)}, u32[]{:S(2)}, u32[]{:S(2)}) collective-permute-start(bf16[768,768]{1,0:T(8,128)(2,1)S(1)} %get-tuple-element.13), channel_id=1, source_target_pairs={{0,1},{1,0},{2,3},{3,2},{4,5},{5,4},{6,7},{7,6},{8,9},{9,8},{10,11... | collective-permute-start | bytes 3538952 | tf_op jit(solution)/shard_map/ppermute | solution.py:226
  18.5 25.4 %collective-permute-start.6 = (bf16[256,768]{1,0:T(8,128)(2,1)S(1)}, bf16[256,768]{1,0:T(8,128)(2,1)S(1)}, u32[]{:S(2)}, u32[]{:S(2)}) collective-permute-start(bf16[256,768]{1,0:T(8,128)(2,1)S(1)} %collective-permute-done.3.refs_0_), channel_id=1, source_target_pairs={{0,8},{4,12},{8,0},{12,4},{16,24},{20,28},{24,16},{28,20},{1,9},{5... | collective-permute-start | bytes 1179656 | tf_op jit(solution)/shard_map/ppermute | solution.py:239
  18.8 25.9 %collective-permute-start.7 = (bf16[256,768]{1,0:T(8,128)(2,1)S(1)}, bf16[256,768]{1,0:T(8,128)(2,1)S(1)}, u32[]{:S(2)}, u32[]{:S(2)}) collective-permute-start(bf16[256,768]{1,0:T(8,128)(2,1)S(1)} %collective-permute-done.3.refs_0_), channel_id=1, source_target_pairs={{0,16},{4,20},{8,24},{12,28},{16,0},{20,4},{24,8},{28,12},{1,17},{... | collective-permute-start | bytes 1179656 | tf_op jit(solution)/shard_map/ppermute | solution.py:239
  20.0 25.4 %collective-permute-start.8 = (bf16[256,768]{1,0:T(8,128)(2,1)S(1)}, bf16[256,768]{1,0:T(8,128)(2,1)S(1)}, u32[]{:S(2)}, u32[]{:S(2)}) collective-permute-start(bf16[256,768]{1,0:T(8,128)(2,1)S(1)} %collective-permute-done.3.refs_0_), channel_id=1, source_target_pairs={{0,24},{4,28},{8,16},{12,20},{16,8},{20,12},{24,0},{28,4},{1,25},{... | collective-permute-start | bytes 1179656 | tf_op jit(solution)/shard_map/ppermute | solution.py:239
  21.2 46.8 %collective-permute-start.5 = (bf16[768,768]{1,0:T(8,128)(2,1)S(1)}, bf16[768,768]{1,0:T(8,128)(2,1)}, u32[]{:S(2)}, u32[]{:S(2)}) collective-permute-start(bf16[768,768]{1,0:T(8,128)(2,1)S(1)} %collective-permute-done.4.refs_3_), channel_id=1, source_target_pairs={{1,0},{2,3},{5,4},{6,7},{9,8},{10,11},{13,12},{14,15},{17,16},{18,... | collective-permute-start | bytes 3538952 | tf_op jit(solution)/shard_map/ppermute | solution.py:232
  46.2 20.0 %collective-permute-start.9 = (bf16[512,768]{1,0:T(8,128)(2,1)}, bf16[512,768]{1,0:T(8,128)(2,1)}, u32[]{:S(2)}, u32[]{:S(2)}) collective-permute-start(bf16[512,768]{1,0:T(8,128)(2,1)} %slice.48), channel_id=1, source_target_pairs={{1,2},{2,1},{5,6},{6,5},{9,10},{10,9},{13,14},{14,13},{17,18},{18,... | collective-permute-start | bytes 2359304 | tf_op jit(solution)/shard_map/ppermute | solution.py:229
  47.8 8.3 %collective-permute-start.10 = (bf16[256,768]{1,0:T(8,128)(2,1)S(1)}, bf16[256,768]{1,0:T(8,128)(2,1)S(1)}, u32[]{:S(2)}, u32[]{:S(2)}) collective-permute-start(bf16[256,768]{1,0:T(8,128)(2,1)S(1)} %slice_select_fusion.1.refs_4_), channel_id=1, source_target_pairs={{0,8},{4,12},{8,0},{12,4},{16,24},{20,28},{24,16},{28,20},{1,9},{5... | collective-permute-start | bytes 1179656 | tf_op jit(solution)/shard_map/ppermute | solution.py:239
  48.1 8.0 %collective-permute-start.11 = (bf16[256,768]{1,0:T(8,128)(2,1)S(1)}, bf16[256,768]{1,0:T(8,128)(2,1)S(1)}, u32[]{:S(2)}, u32[]{:S(2)}) collective-permute-start(bf16[256,768]{1,0:T(8,128)(2,1)S(1)} %slice_select_fusion.1.refs_4_), channel_id=1, source_target_pairs={{0,16},{4,20},{8,24},{12,28},{16,0},{20,4},{24,8},{28,12},{1,17},{... | collective-permute-start | bytes 1179656 | tf_op jit(solution)/shard_map/ppermute | solution.py:239
  49.3 16.0 %collective-permute-start.12 = (bf16[256,768]{1,0:T(8,128)(2,1)S(1)}, bf16[256,768]{1,0:T(8,128)(2,1)S(1)}, u32[]{:S(2)}, u32[]{:S(2)}) collective-permute-start(bf16[256,768]{1,0:T(8,128)(2,1)S(1)} %slice_select_fusion.1.refs_4_), channel_id=1, source_target_pairs={{0,24},{4,28},{8,16},{12,20},{16,8},{20,12},{24,0},{28,4},{1,25},{... | collective-permute-start | bytes 1179656 | tf_op jit(solution)/shard_map/ppermute | solution.py:239
  68.0 17.8 %collective-permute-start.13 = (bf16[512,768]{1,0:T(8,128)(2,1)}, bf16[512,768]{1,0:T(8,128)(2,1)}, u32[]{:S(2)}, u32[]{:S(2)}) collective-permute-start(bf16[512,768]{1,0:T(8,128)(2,1)} %collective-permute-done.9.refs_1_), channel_id=1, source_target_pairs={{1,0},{2,3},{5,4},{6,7},{9,8},{10,11},{13,12},{14,15},{17,16},{18,... | collective-permute-start | bytes 2359304 | tf_op jit(solution)/shard_map/ppermute | solution.py:232
  71.1 17.9 %collective-permute-start.14 = (bf16[256,768]{1,0:T(8,128)(2,1)}, bf16[256,768]{1,0:T(8,128)(2,1)}, u32[]{:S(2)}, u32[]{:S(2)}) collective-permute-start(bf16[256,768]{1,0:T(8,128)(2,1)} %slice_select_fusion.refs_8_), channel_id=1, source_target_pairs={{0,8},{4,12},{8,0},{12,4},{16,24},{20,28},{24,16},{28,20},{1,9},{5... | collective-permute-start | bytes 1179656 | tf_op jit(solution)/shard_map/ppermute | solution.py:239
  71.3 17.7 %collective-permute-start.15 = (bf16[256,768]{1,0:T(8,128)(2,1)}, bf16[256,768]{1,0:T(8,128)(2,1)}, u32[]{:S(2)}, u32[]{:S(2)}) collective-permute-start(bf16[256,768]{1,0:T(8,128)(2,1)} %slice_select_fusion.refs_8_), channel_id=1, source_target_pairs={{0,16},{4,20},{8,24},{12,28},{16,0},{20,4},{24,8},{28,12},{1,17},{... | collective-permute-start | bytes 1179656 | tf_op jit(solution)/shard_map/ppermute | solution.py:239
  72.6 16.5 %collective-permute-start.16 = (bf16[256,768]{1,0:T(8,128)(2,1)}, bf16[256,768]{1,0:T(8,128)(2,1)}, u32[]{:S(2)}, u32[]{:S(2)}) collective-permute-start(bf16[256,768]{1,0:T(8,128)(2,1)} %slice_select_fusion.refs_8_), channel_id=1, source_target_pairs={{0,24},{4,28},{8,16},{12,20},{16,8},{20,12},{24,0},{28,4},{1,25},{... | collective-permute-start | bytes 1179656 | tf_op jit(solution)/shard_map/ppermute | solution.py:239
  89.1 7.2 %collective-permute-start.18 = (bf16[256,512]{1,0:T(8,128)(2,1)S(1)}, bf16[256,512]{1,0:T(8,128)(2,1)S(1)}, u32[]{:S(2)}, u32[]{:S(2)}) collective-permute-start(bf16[256,512]{1,0:T(8,128)(2,1)S(1)} %pad_maximum_fusion.2.refs_0_), channel_id=1, source_target_pairs={{0,8},{4,12},{1,9},{5,13},{2,10},{6,14},{3,11},{7,15},{16,24},{20,... | collective-permute-start | bytes 786440 | tf_op jit(solution)/shard_map/ppermute | solution.py:17
  90.5 13.5 %collective-permute-start.17 = (bf16[256,512]{1,0:T(8,128)(2,1)S(1)}, bf16[256,512]{1,0:T(8,128)(2,1)S(1)}, u32[]{:S(2)}, u32[]{:S(2)}) collective-permute-start(bf16[256,512]{1,0:T(8,128)(2,1)S(1)} %pad_maximum_fusion.2.refs_0_), channel_id=1, source_target_pairs={{0,4},{8,12},{1,5},{9,13},{2,6},{10,14},{3,7},{11,15},{16,20},{24,... | collective-permute-start | bytes 786440 | tf_op jit(solution)/shard_map/ppermute | solution.py:266
  96.3 8.5 %collective-permute-start.19 = (bf16[256,512]{1,0:T(8,128)(2,1)S(1)}, bf16[256,512]{1,0:T(8,128)(2,1)S(1)}, u32[]{:S(2)}, u32[]{:S(2)}) collective-permute-start(bf16[256,512]{1,0:T(8,128)(2,1)S(1)} %collective-permute-done.18.refs_2_), channel_id=1, source_target_pairs={{8,12},{12,8},{9,13},{13,9},{10,14},{14,10},{11,15},{15,11},{24,28... | collective-permute-start | bytes 786440 | tf_op jit(solution)/shard_map/ppermute | solution.py:267
  106.5 4.3 %collective-permute-start.21 = (bf16[64,256]{1,0:T(8,128)(2,1)S(1)}, bf16[64,256]{1,0:T(8,128)(2,1)S(1)}, u32[]{:S(2)}, u32[]{:S(2)}) collective-permute-start(bf16[64,256]{1,0:T(8,128)(2,1)S(1)} %get-tuple-element.22), channel_id=1, source_target_pairs={{0,2},{1,3},{2,0},{3,1},{4,6},{5,7},{6,4},{7,5},{8,10},{9,11},{10,... | collective-permute-start | bytes 98312 | tf_op jit(solution)/shard_map/ppermute | solution.py:287
  109.5 4.6 %collective-permute-start.22 = (bf16[64,256]{1,0:T(8,128)(2,1)S(1)}, bf16[64,256]{1,0:T(8,128)(2,1)S(1)}, u32[]{:S(2)}, u32[]{:S(2)}) collective-permute-start(bf16[64,256]{1,0:T(8,128)(2,1)S(1)} %get-tuple-element.23), channel_id=1, source_target_pairs={{0,3},{1,2},{2,1},{3,0},{4,7},{5,6},{6,5},{7,4},{8,11},{9,10},{10,... | collective-permute-start | bytes 98312 | tf_op jit(solution)/shard_map/ppermute | solution.py:287
  110.6 3.5 %collective-permute-start.20 = (bf16[64,256]{1,0:T(8,128)(2,1)S(1)}, bf16[64,256]{1,0:T(8,128)(2,1)S(1)}, u32[]{:S(2)}, u32[]{:S(2)}) collective-permute-start(bf16[64,256]{1,0:T(8,128)(2,1)S(1)} %get-tuple-element.24), channel_id=1, source_target_pairs={{0,1},{1,0},{2,3},{3,2},{4,5},{5,4},{6,7},{7,6},{8,9},{9,8},{10,11... | collective-permute-start | bytes 98312 | tf_op jit(solution)/shard_map/ppermute | solution.py:287
  114.1 2.9 %collective-permute-start.23 = (bf16[64,1024]{1,0:T(8,128)(2,1)S(1)}, bf16[64,1024]{1,0:T(8,128)(2,1)S(1)}, u32[]{:S(2)}, u32[]{:S(2)}) collective-permute-start(bf16[64,1024]{1,0:T(8,128)(2,1)S(1)} %pad_maximum_fusion.5), channel_id=1, source_target_pairs={{0,4},{4,0},{8,12},{12,8},{16,20},{20,16},{24,28},{28,24},{1,5},{5... | collective-permute-start | bytes 393224 | tf_op jit(solution)/shard_map/ppermute | solution.py:235
  (28 other events, 387.3 us)
